TPU v7x, 256 devices: a whole 4x4x8 slice. The times are simulated.
256 devices in a mesh: ctx: 16 (over y_hi, x, core), ch: 16 (over y_lo, z).
Axes of the slice: x: 4, y: 4 (y_hi: 2, y_lo: 2; y = y_hi * 2 + y_lo), z: 8, core: 2. Of those that a mesh axis runs over, the one named last changes fastest.
Arguments:
- streams: bfloat16 [3, 24576, 4096], P(None, 'ctx', 'ch'), may hold values from -6 to 6
- taps: float32 [3, 3, 4096], P(None, None, 'ch'), may hold values from -4 to 4
- residues: float32 [4096, 16], P('ch'), may hold values from -4 to 4
- decay: float32 [4096, 16], P('ch'), may hold values from 8.138021e-06 to 0.03
- skip: float32 [4096], P('ch'), may hold values from 0.5 to 1.5
- w_out: bfloat16 [4096, 4096], P('ch', 'ctx'), may hold values from -0.125 to 0.125
Outputs:
- layer_out: bfloat16 [24576, 4096], P('ctx', 'ch')
All inputs are finite; a program needn't handle non-finite values.
Results may differ from a plain program's by a relative error of at most 0.0049.
Values may be sent and summed in bfloat16 or wider, within the bound.
No kernel may reach another device: no remote copies, remote signals or barrier semaphores. Data moves between devices by JAX's collectives and lax.ppermute only.
A program may use at most 128 MiB of HBM per device.

v0:
```python
import jax
import jax.numpy as jnp
from jax import lax
from jax.sharding import PartitionSpec as P

BLK = 64


def from_behind(block, axis, distance):
    devices = range(lax.axis_size(axis))
    route = [(i - distance, i) for i in devices if i - distance in devices]
    return lax.ppermute(block, axis, route)


def entering(x, axis, combine, identity):
    length, position = (lax.axis_size(axis), lax.axis_index(axis))
    everything = jax.tree.map(lambda part: lax.all_gather(part, axis), x)
    start = jax.tree.map(
        lambda part, zero: jnp.broadcast_to(jnp.asarray(zero, part.dtype), part.shape), x, identity
    )

    def turn(k, before):
        reached = k < position
        new = combine(before, jax.tree.map(lambda part: part[k], everything))
        return jax.tree.map(lambda a, b: jnp.where(reached, a, b), new, before)

    return lax.fori_loop(0, length, turn, start)


def join_states(earlier, later):
    return (earlier[0] * later[0], earlier[1] * later[0] + later[1])


def local(streams, taps, residues, decay, skip, w_out):
    tok = streams.shape[1]
    chans = streams.shape[2]
    blocks_count = tok // BLK
    tail = streams[:, tok - 2 :, :]
    before = from_behind(tail, "ctx", 1)
    extended = jnp.concatenate([before, streams], axis=1).astype(jnp.float32)
    filtered = (
        taps[:, 0, :][:, None, :] * extended[:, 2:, :]
        + taps[:, 1, :][:, None, :] * extended[:, 1:-1, :]
        + taps[:, 2, :][:, None, :] * extended[:, :-2, :]
    )
    query = filtered[0]
    drive = filtered[1] * filtered[2]
    wrow = lax.all_gather(w_out, "ctx", axis=1, tiled=True)
    scaled = residues * jnp.sqrt(decay)
    lags = jnp.arange(BLK).astype(jnp.float32)
    short_filt = jnp.sum(scaled[None] * jnp.exp(-decay[None] * lags[:, None, None]), axis=2)
    offsets = jnp.arange(BLK)[:, None] - jnp.arange(BLK)[None, :]
    toeplitz = jnp.where(
        (offsets >= 0)[:, :, None], jnp.take(short_filt, jnp.maximum(offsets, 0), axis=0), 0.0
    )
    blocks = drive.reshape(blocks_count, BLK, chans)
    inner = jnp.einsum("ijc,bjc->bic", toeplitz, blocks, precision=lax.Precision.HIGHEST)
    end_weight = jnp.exp(-decay[None] * (BLK - 1 - lags)[:, None, None])
    block_ends = jnp.einsum("bjc,jcm->bcm", blocks, end_weight, precision=lax.Precision.HIGHEST)
    step_decay = jnp.exp(-decay * BLK)

    def chain(state, block_end):
        return (step_decay * state + block_end, state)

    device_end, prior = lax.scan(chain, jnp.zeros(decay.shape, jnp.float32), block_ends)
    span = jnp.exp(-decay * tok)
    ident = (jnp.ones(decay.shape, jnp.float32), jnp.zeros(decay.shape, jnp.float32))
    unused, incoming = entering((span, device_end), "ctx", join_states, ident)
    block_pos = jnp.arange(blocks_count).astype(jnp.float32)
    states_before = (
        prior + jnp.exp(-decay[None] * (BLK * block_pos)[:, None, None]) * incoming[None]
    )
    entry_weight = scaled[None] * jnp.exp(-decay[None] * (lags + 1.0)[:, None, None])
    carried = jnp.einsum(
        "bcm,icm->bic", states_before, entry_weight, precision=lax.Precision.HIGHEST
    )
    conv = (inner + carried).reshape(tok, chans)
    gated = (query * (conv + skip[None, :] * drive)).astype(jnp.bfloat16)
    summed = lax.psum_scatter(
        lax.dot_general(wrow, gated, (((0,), (1,)), ((), ())), preferred_element_type=jnp.float32),
        "ch",
        scatter_dimension=0,
        tiled=True,
    )
    return summed.T.astype(jnp.bfloat16)


def solution(mesh):
    return jax.shard_map(
        local,
        mesh=mesh,
        in_specs=(
            P(None, "ctx", "ch"),
            P(None, None, "ch"),
            P("ch", None),
            P("ch", None),
            P("ch"),
            P("ch", "ctx"),
        ),
        out_specs=P("ctx", "ch"),
        check_vma=False,
    )
```

profile of v0, /device:TPU:2, one launch (start us, length us, event | category | flops | bytes accessed | tf_op | source)
XLA Modules:
  0.0 477.2 jit_solution(2721281230618491485)
XLA Ops:
  8.0 1.9 collective-permute-start
  11.1 0.8 fusion.35
  12.0 0.7 sqrt_multiply_fusion
  13.0 21.3 %all-gather = f32[4096,16]{0,1:T(8,128)S(1)} all-gather(f32[256,16]{0,1:T(8,128)S(1)} %get-tuple-element.215), channel_id=2, replica_groups=mesh['ctx'=16,'ch'=16] {'ctx'}, dimensions={0}, use_global_device_ids=true | all-gather | bytes 278528 | tf_op jit(solution)/shard_map/all_gather | solution.py:17
  34.3 1.6 multiply_reduce_fusion
  36.5 0.8 copy.41
  37.3 16.1 %gather_fusion = f32[4096,256]{1,0:T(8,128)} fusion(f32[64,256]{1,0:T(8,128)S(1)} %copy.27, s32[4096]{0:T(1024)S(1)} %broadcast_clamp_fusion), kind=kCustom, calls=%fused_computation | custom fusion | bytes 8404992 | tf_op jit(solution)/shard_map/jit(_take)/gather | solution.py:54
  53.4 9.3 %copy.28 = f32[64,64,256]{1,0,2:T(8,128)} copy(f32[64,64,256]{2,1,0:T(8,128)} %bitcast.72) | data formatting | bytes 8388608 | tf_op jit(solution)/shard_map/jit(_take)/gather | solution.py:54
  63.2 1.4 fusion.6
  64.6 2.2 copy-done
  66.8 1.4 slice_multiply_fusion.3
  68.2 2.2 copy.29
  70.5 6.4 %fusion.21 = f32[24,256,16]{0,2,1:T(8,128)} fusion(f32[24,64,256]{1,0,2:T(8,128)S(1)} %copy.29, f32[64]{0:T(128)S(1)} %broadcast_subtract_fusion, f32[256,16]{1,0:T(8,128)S(1)} %copy.26), kind=kOutput, calls=%fused_computation.33 | convolution fusion | flops 75759616 | bytes 1982720 | tf_op jit(solution)/shard_map/bjc,jcm->bcm/dot_general | solution.py:59
  76.9 3.4 copy.31
  80.2 32.0 %while.27 = (s32[]{:T(128)}, f32[256,16]{0,1:T(8,128)S(1)}, f32[24,256,16]{1,2,0:T(8,128)}, f32[256,16]{0,1:T(8,128)S(1)}, f32[24,256,16]{1,2,0:T(8,128)}, /*index=5*/s32[]{:T(128)}, s32[]{:T(128)}) while((s32[]{:T(128)}, f32[256,16]{0,1:T(8,128)S(1)}, f32[24,256,16]{1,2,0:T(8,128)}, f32[256,16]{0,1:T(8,128)S(1)}, ...), condition=%wide.region_2.3_spmd.clone, body=%wide.region_1.2_spmd.clone.sunk | while | flops 16387 | bytes 98408 | solution.py:65
  80.9 0.7 bitcast_add_fusion.3
  82.2 0.7 bitcast_add_fusion.3
  83.5 0.7 bitcast_add_fusion.3
  84.9 0.7 bitcast_add_fusion.3
  86.2 0.7 bitcast_add_fusion.3
  87.5 0.7 bitcast_add_fusion.3
  88.9 0.7 bitcast_add_fusion.3
  90.2 0.7 bitcast_add_fusion.3
  91.5 0.7 bitcast_add_fusion.3
  92.9 0.7 bitcast_add_fusion.3
  94.2 0.7 bitcast_add_fusion.3
  95.5 0.7 bitcast_add_fusion.3
  98.2 0.7 bitcast_add_fusion.3
  99.5 0.7 bitcast_add_fusion.3
  100.9 0.7 bitcast_add_fusion.3
  102.2 0.7 bitcast_add_fusion.3
  103.5 0.7 bitcast_add_fusion.3
  104.9 0.7 bitcast_add_fusion.3
  106.2 0.7 bitcast_add_fusion.3
  107.5 0.7 bitcast_add_fusion.3
  110.2 0.7 bitcast_add_fusion.3
  111.5 0.7 bitcast_add_fusion.3
  112.2 24.0 %all-gather.1 = f32[4096,16]{0,1:T(8,128)S(1)} all-gather(f32[256,16]{0,1:T(8,128)S(1)} %get-tuple-element.128), channel_id=3, replica_groups=mesh['ctx'=16,'ch'=16] {'ctx'}, dimensions={0}, use_global_device_ids=true | all-gather | bytes 278528 | tf_op jit(solution)/shard_map/all_gather | solution.py:17
  136.4 15.7 %while.28 = (s32[]{:T(128)}, f32[256,16]{0,1:T(8,128)S(1)}, s32[]{:T(128)}, f32[16,256,16]{1,0,2:T(8,128)}, f32[16,256,16]{1,0,2:T(8,128)S(1)}, /*index=5*/s32[]{:T(128)}, s32[]{:T(128)}) while((s32[]{:T(128)}, f32[256,16]{0,1:T(8,128)S(1)}, s32[]{:T(128)}, f32[16,256,16]{1,0,2:T(8,128)}, f32[16,256,16]{1,0,2:T(8,128)S(1)}, ...), condition=%wide.region_4.5_spmd.clone, body=%wide.region_3.4_spmd.clone.sunk | while | flops 16388 | bytes 131181 | solution.py:27
  136.4 0.9 constant_dynamic-slice_fusion.3
  137.4 0.9 constant_dynamic-slice_fusion.3
  138.3 0.9 constant_dynamic-slice_fusion.3
  139.3 0.9 constant_dynamic-slice_fusion.3
  140.3 0.9 constant_dynamic-slice_fusion.3
  141.3 0.9 constant_dynamic-slice_fusion.3
  142.2 0.9 constant_dynamic-slice_fusion.3
  143.2 0.9 constant_dynamic-slice_fusion.3
  144.2 0.9 constant_dynamic-slice_fusion.3
  145.2 0.9 constant_dynamic-slice_fusion.3
  146.2 0.9 constant_dynamic-slice_fusion.3
  147.1 0.9 constant_dynamic-slice_fusion.3
  148.1 0.9 constant_dynamic-slice_fusion.3
  149.1 0.9 constant_dynamic-slice_fusion.3
  150.1 0.9 constant_dynamic-slice_fusion.3
  151.0 0.9 constant_dynamic-slice_fusion.3
  152.0 1.1 multiply_add_fusion
  153.2 2.5 copy.34
  155.7 8.5 %fusion.15 = f32[256,64,24]{1,2,0:T(8,128)S(1)} fusion(f32[24,256,16]{0,2,1:T(8,128)} %copy.34, f32[64]{0:T(128)} %broadcast_add_fusion, f32[256,16]{1,0:T(8,128)} %copy-done.2, f32[256,16]{1,0:T(8,128)} %copy-done.3), kind=kOutput, calls=%fused_computation.28 | convolution fusion | flops 76021760 | bytes 1999104 | tf_op jit(solution)/shard_map/bcm,icm->bic/dot_general | solution.py:74
  164.3 17.2 %bitcast_add_fusion.1 = f32[24,64,256]{1,0,2:T(8,128)} fusion(f32[256,64,24]{1,2,0:T(8,128)S(1)} %fusion.15, f32[24,64,256]{1,0,2:T(8,128)S(1)} %copy.29, f32[64,64,256]{1,0,2:T(8,128)} %copy.28, pred[64,64]{1,0:T(8,128)(4,1)S(1)} %copy-done.5, pred[64,64]{1,0:T(8,128)(4,1)S(1)} %copy-done.6), kind=kOutput, calls=%fused_computation.23 | convolution fusion | flops 304480256 | bytes 8921088 | tf_op jit(solution)/shard_map/ijc,bjc->bic/dot_general | solution.py:57
  181.4 2.4 copy.35
  183.8 2.7 fusion.25
  186.6 11.7 %convolution_bitcast_fusion = f32[4096,1536]{0,1:T(8,128)} fusion(bf16[1536,256]{1,0:T(8,128)(2,1)S(1)} %fusion.25, bf16[256,4096]{1,0:T(8,128)(2,1)} %all-gather.4.cloned.1.call-done), kind=kOutput, calls=%fused_computation.10 | convolution fusion | flops 3221225472 | bytes 28049408 | tf_op jit(solution)/shard_map/dot_general | solution.py:80
  198.3 269.7 %reduce-scatter.2.cloned.1.call-done = f32[256,1536]{0,1:T(8,128)} async-done(((f32[4096,1536]{0,1:T(8,128)}), f32[256,1536]{0,1:T(8,128)}) %reduce-scatter.2.cloned.1.call-update) | async-done | bytes 1572880 | tf_op jit(solution)/shard_map/reduce_scatter | solution.py:79
  468.0 2.4 convert_bitcast_fusion
  (82 shorter events, 20.3 us)
Async XLA Ops:
  6.5 180.1 %all-gather.4.cloned.1.call-start = ((), (), s32[]{:S(2)}) async-start(), calls=%async_computation.1 | async-start | bytes 2228224 | tf_op jit(solution)/shard_map/all_gather | solution.py:48
  7.3 460.7 %reduce-scatter.2.cloned.1.call-start = ((), (), s32[]{:S(2)}) async-start(), calls=%async_computation.2 | async-start | bytes 26738688 | tf_op jit(solution)/shard_map/reduce_scatter | solution.py:79
  8.0 54.7 %collective-permute-start = (bf16[3,2,256]{2,1,0:T(2,128)(2,1)S(1)}, bf16[3,2,256]{2,1,0:T(2,128)(2,1)S(1)}, u32[]{:S(2)}, u32[]{:S(2)}) collective-permute-start(bf16[3,2,256]{2,1,0:T(2,128)(2,1)S(1)} %slice.31), channel_id=1, source_target_pairs={{0,16},{16,32},{32,48},{48,64},{64,80},{80,96},{96,112},{112,128},... | collective-permute-start | bytes 9224 | tf_op jit(solution)/shard_map/ppermute | solution.py:12
  12.8 23.7 %copy-start.4 = (f32[256,16]{0,1:T(8,128)}, f32[256,16]{0,1:T(8,128)S(1)}, u32[]{:S(2)}) copy-start(f32[256,16]{0,1:T(8,128)S(1)} %get-tuple-element.216) | copy-start | bytes 49156
  12.9 40.6 %copy-start.3 = (f32[256,16]{1,0:T(8,128)}, f32[256,16]{1,0:T(8,128)S(1)}, u32[]{:S(2)}) copy-start(f32[256,16]{1,0:T(8,128)S(1)} %copy.25) | copy-start | bytes 49156
  13.0 57.5 %copy-start.2 = (f32[256,16]{1,0:T(8,128)}, f32[256,16]{1,0:T(8,128)S(1)}, u32[]{:S(2)}) copy-start(f32[256,16]{1,0:T(8,128)S(1)} %copy.26) | copy-start | bytes 49156
  53.4 9.3 %copy-start.1 = (bf16[3,1536,256]{2,1,0:T(8,128)(2,1)S(1)}, bf16[3,1536,256]{2,1,0:T(8,128)(2,1)}, u32[]{:S(2)}) copy-start(bf16[3,1536,256]{2,1,0:T(8,128)(2,1)} %param.10) | copy-start | bytes 7077892
  64.6 2.2 copy-start
  155.7 8.6 %copy-start.5 = (pred[64,64]{1,0:T(8,128)(4,1)S(1)}, pred[64,64]{1,0:T(8,128)(4,1)}, u32[]{:S(2)}) copy-start(pred[64,64]{1,0:T(8,128)(4,1)} %get-tuple-element.222) | copy-start | bytes 12292
  155.7 8.6 %copy-start.6 = (pred[64,64]{1,0:T(8,128)(4,1)S(1)}, pred[64,64]{1,0:T(8,128)(4,1)}, u32[]{:S(2)}) copy-start(pred[64,64]{1,0:T(8,128)(4,1)} %get-tuple-element.223) | copy-start | bytes 12292
  181.4 2.4 copy-start.7
Sparse Core Ops, SparseCore 0:
  9.9 57.4 all-gather.3
  198.4 269.5 reduce-scatter.1
where the time goes:
time: 481 us; the launch traced here: 477 us
  waiting for transfers between devices  270 us (56%)
  local copies, waits for them, and re-layouts  56 us (12%)
  other arithmetic  45.6 us (9%)
  blocking collectives  45.3 us (9%)
  matrix products  43.8 us (9%)
  between operations  13.6 us (3%)
    reduce_scatter x1, waiting for transfers between devices, local(): lax.psum_scatter(lax.dot_general(wrow, gated, (((0,), (1,)), ((), ())), p...  270 us
    all_gather x2, blocking collectives, entering(): everything = jax.tree.map(lambda part: lax.all_gather(part, axis), x)  45.3 us
    gather x2, local copies, waits for them, and re-layouts, local(): jnp.take(short_filt, jnp.maximum(offsets, 0), axis=0)  25.5 us
    add x24, other arithmetic, chain(): return (step_decay * state + block_end, state)  17.4 us
    dot_general x1, matrix products, local(): jnp.einsum('ijc,bjc->bic', toeplitz, blocks, precision=lax.Precision.HIGH...  17.2 us
    dynamic_slice x16, local copies, waits for them, and re-layouts, turn(): new = combine(before, jax.tree.map(lambda part: part[k], everything))  15 us
    dynamic_update_slice x24, other arithmetic, local(): lax.scan(chain, jnp.zeros(decay.shape, jnp.float32), block_ends)  14.6 us
    dot_general x1, matrix products, local(): lax.dot_general(wrow, gated, (((0,), (1,)), ((), ())), preferred_element_...  11.7 us
  transfers between devices with their start and end apart: 3, of which 1 were waited for; matrix products, arithmetic and copies ran while one was open for 27% of the time, Pallas kernels for 0%

commit v1 on v0

v1 whole, which is shorter than its diff:
```python
import functools

import jax
import jax.numpy as jnp
from jax import lax
from jax.experimental import pallas as pl
from jax.experimental.pallas import tpu as pltpu
from jax.sharding import PartitionSpec as P

MODES = 16
LANES = 128
SEGS = 8
CHUNKS = 3
CTX = 16
CH = 16
RING = 8
F32 = jnp.float32
BF16 = jnp.bfloat16
VMEM_LIMIT = 24 * 1024 * 1024


def row_ids():
    return lax.broadcasted_iota(jnp.int32, (SEGS, LANES), 0)


def wide(row):
    return jnp.broadcast_to(row, (SEGS, LANES))


def states_kernel(
    me_ref, k_ref, v_ref, halo_ref, taps_ref, decay_ref,
    drive_ref, segend_ref, start_ref, send_ref, kx, vx, ends,
):
    tokens = k_ref.shape[1]
    chunk = tokens // CHUNKS
    steps = chunk // SEGS
    kx[pl.ds(8, tokens), :] = k_ref[0].astype(F32)
    vx[pl.ds(8, tokens), :] = v_ref[0].astype(F32)
    kx[pl.ds(6, 2), :] = halo_ref[1].astype(F32)
    vx[pl.ds(6, 2), :] = halo_ref[2].astype(F32)
    decay = decay_ref[...]
    keep = jnp.exp(-decay)
    keeps = [wide(keep[m : m + 1]) for m in range(MODES)]
    tk = [wide(taps_ref[1, j : j + 1, :]) for j in range(3)]
    tv = [wide(taps_ref[2, j : j + 1, :]) for j in range(3)]
    later = (SEGS - 1 - row_ids()).astype(F32) * steps

    for c in range(CHUNKS):
        base = 8 + c * chunk

        def at(ref, i):
            return ref[pl.ds(base + i, SEGS, stride=steps), :]

        def step(i, carry):
            k1, k2, v1, v2, acc = carry
            k0, v0 = at(kx, i), at(vx, i)
            keyed = tk[0] * k0 + tk[1] * k1 + tk[2] * k2
            valued = tv[0] * v0 + tv[1] * v1 + tv[2] * v2
            drive = keyed * valued
            drive_ref[pl.ds(pl.multiple_of(c * chunk + i * SEGS, SEGS), SEGS), :] = drive
            return k0, k1, v0, v1, tuple(a * s + drive for a, s in zip(keeps, acc))

        zero = tuple(jnp.zeros((SEGS, LANES), F32) for _ in range(MODES))
        acc = lax.fori_loop(
            0, steps, step,
            (at(kx, -1), at(kx, -2), at(vx, -1), at(vx, -2), zero),
            unroll=4,
        )[4]
        for m in range(MODES):
            segend_ref[c, m] = acc[m]
            weight = jnp.exp(-wide(decay[m : m + 1]) * later)
            ends[c, pl.ds(m, 1), :] = jnp.sum(acc[m] * weight, axis=0, keepdims=True)

    state = jnp.zeros((MODES, LANES), F32)
    span = jnp.exp(-decay * chunk)
    for c in range(CHUNKS):
        start_ref[c] = state
        state = state * span + ends[c]
    me = me_ref[0]
    for j in range(CTX):
        gap = j - 1 - me
        lag = (jnp.maximum(gap, 0) * tokens).astype(F32)
        send_ref[j] = jnp.where(gap >= 0, jnp.exp(-decay * lag) * state, 0.0)


def gate_kernel(
    c, q_ref, qb_ref, taps_ref, decay_ref, res_ref, skip_ref, drive_ref, segend_ref,
    start_ref, recv_ref, out_ref, qx, gx,
):
    chunk = q_ref.shape[1]
    steps = chunk // SEGS
    qx[pl.ds(8, chunk), :] = q_ref[0].astype(F32)
    before = qb_ref[0].astype(F32)
    qx[pl.ds(6, 2), :] = before[before.shape[0] - 2 :]
    decay = decay_ref[...]
    keep = jnp.exp(-decay)
    keep1 = jnp.exp(-decay * steps)
    keep2 = jnp.exp(-decay * (2 * steps))
    keep4 = jnp.exp(-decay * (4 * steps))
    scaled = res_ref[...] * jnp.sqrt(decay)
    incoming = recv_ref[0]
    for j in range(1, CTX):
        incoming = incoming + recv_ref[j]
    entry = jnp.exp(-decay * (c * chunk)) * incoming + start_ref[0]
    rows = row_ids()
    acc = []
    for m in range(MODES):
        x = jnp.where(rows == 0, wide(entry[m : m + 1]), pltpu.roll(segend_ref[0, m], 1, 0))
        for far, factor in ((1, keep1), (2, keep2), (4, keep4)):
            moved = pltpu.roll(x, far, 0) * wide(factor[m : m + 1])
            x = x + jnp.where(rows >= far, moved, 0.0)
        acc.append(x)
    keeps = [wide(keep[m : m + 1]) for m in range(MODES)]
    gains = [wide(scaled[m : m + 1]) for m in range(MODES)]
    tq = [wide(taps_ref[0, j : j + 1, :]) for j in range(3)]
    skip = wide(skip_ref[...])

    def at(i):
        return qx[pl.ds(8 + i, SEGS, stride=steps), :]

    def step(i, carry):
        q1, q2, acc = carry
        q0 = at(i)
        drive = drive_ref[pl.ds(pl.multiple_of(i * SEGS, SEGS), SEGS), :]
        acc = tuple(a * s + drive for a, s in zip(keeps, acc))
        terms = [g * s for g, s in zip(gains, acc)] + [skip * drive]
        while len(terms) > 1:
            terms = [sum(terms[i : i + 2]) for i in range(0, len(terms), 2)]
        query = tq[0] * q0 + tq[1] * q1 + tq[2] * q2
        gx[pl.ds(i, SEGS, stride=steps), :] = query * terms[0]
        return q0, q1, acc

    lax.fori_loop(0, steps, step, (at(-1), at(-2), tuple(acc)), unroll=4)
    out_ref[...] = gx[...].astype(BF16)


def project_kernel(place_ref, *refs):
    blocks, w_ref, own_ref, other_ref = refs[:9], refs[9], refs[10], refs[11]
    z, side = place_ref[0], place_ref[1]
    shifts = (0, -1, -2, -3, 1, 2, 3, 4)
    values = [b[...] for b in blocks[:7]]
    values.append(jnp.concatenate([blocks[7][...], blocks[8][...]], axis=0))
    for out_ref, half in ((own_ref, side), (other_ref, 1 - side)):
        total = None
        for shift, value in zip(shifts, values):
            row = lax.rem(z + shift + RING, RING)
            term = jnp.dot(value, w_ref[half * RING + row], preferred_element_type=F32)
            total = term if total is None else total + term
        out_ref[...] = total.astype(out_ref.dtype)


def local(streams, taps, residues, decay, skip, w_out):
    tokens, chans = streams.shape[1], streams.shape[2]
    chunk = tokens // CHUNKS
    tiles = chans // LANES
    ctx = lax.axis_index("ctx")
    ch = lax.axis_index("ch")

    halo = lax.ppermute(streams[:, tokens - 2 :, :], "ctx", [(i, i + 1) for i in range(CTX - 1)])
    swap = []
    for h in range(2):
        for a in range(RING):
            for y in range(2):
                for z in range(RING):
                    swap.append((((h * RING + a) * 2 + y) * RING + z, ((h * RING + z) * 2 + y) * RING + a))
    w_block = lax.ppermute(w_out, ("ctx", "ch"), swap)
    w_all = lax.all_gather(w_block, "ctx")

    decay_t, res_t = decay.T, residues.T
    skip_row = skip[None, :]
    me = jnp.reshape(ctx, (1,)).astype(jnp.int32)
    smem = pl.BlockSpec(memory_space=pltpu.SMEM)
    params = pltpu.CompilerParams(vmem_limit_bytes=VMEM_LIMIT)
    lane = lambda *lead: pl.BlockSpec((*lead, LANES), lambda g: (*([0] * len(lead)), g))

    drive, segend, start, send = pl.pallas_call(
        states_kernel,
        grid=(tiles,),
        in_specs=[
            smem,
            pl.BlockSpec((1, tokens, LANES), lambda g: (1, 0, g)),
            pl.BlockSpec((1, tokens, LANES), lambda g: (2, 0, g)),
            lane(3, 2),
            lane(3, 3),
            lane(MODES),
        ],
        out_specs=[lane(tokens), lane(CHUNKS, MODES, SEGS), lane(CHUNKS, MODES), lane(CTX, MODES)],
        out_shape=[
            jax.ShapeDtypeStruct((tokens, chans), F32),
            jax.ShapeDtypeStruct((CHUNKS, MODES, SEGS, chans), F32),
            jax.ShapeDtypeStruct((CHUNKS, MODES, chans), F32),
            jax.ShapeDtypeStruct((CTX, MODES, chans), F32),
        ],
        scratch_shapes=[
            pltpu.VMEM((tokens + 8, LANES), F32),
            pltpu.VMEM((tokens + 8, LANES), F32),
            pltpu.VMEM((CHUNKS, MODES, LANES), F32),
        ],
        compiler_params=params,
        name="states",
    )(me, streams, streams, halo, taps, decay_t)
    recv = lax.all_to_all(send, "ctx", 0, 0)

    def gate(c):
        if c == 0:
            before, before_spec = halo, lane(1, 2)
        else:
            before = streams
            before_spec = pl.BlockSpec((1, 16, LANES), lambda g: (0, c * chunk // 16 - 1, g))
        return pl.pallas_call(
            functools.partial(gate_kernel, c),
            grid=(tiles,),
            in_specs=[
                pl.BlockSpec((1, chunk, LANES), lambda g: (0, c, g)),
                before_spec,
                lane(3, 3),
                lane(MODES),
                lane(MODES),
                lane(1),
                pl.BlockSpec((chunk, LANES), lambda g: (c, g)),
                pl.BlockSpec((1, MODES, SEGS, LANES), lambda g: (c, 0, 0, g)),
                pl.BlockSpec((1, MODES, LANES), lambda g: (c, 0, g)),
                lane(CTX, MODES),
            ],
            out_specs=lane(chunk),
            out_shape=jax.ShapeDtypeStruct((chunk, chans), BF16),
            scratch_shapes=[pltpu.VMEM((chunk + 8, LANES), F32), pltpu.VMEM((chunk, LANES), F32)],
            compiler_params=params,
            name="gate",
        )(streams, before, taps, decay_t, res_t, skip_row, drive, segend, start, recv)

    up = [(y * RING + z, y * RING + (z + 1) % RING) for y in range(2) for z in range(RING)]
    down = [(d, s) for s, d in up]
    across = [(i, (i + RING) % CH) for i in range(CH)]
    half = chunk // 2
    place = jnp.stack([lax.rem(ch, RING), ch // RING]).astype(jnp.int32)

    gated = [gate(c) for c in range(CHUNKS)]
    held = [[g] for g in gated]
    from_low = list(gated)
    from_high = list(gated)
    lows = [[] for _ in range(CHUNKS)]
    highs = [[] for _ in range(CHUNKS)]
    for s in range(1, 5):
        for c in range(CHUNKS):
            a, b = from_low[c], from_high[c]
            if s == 4:
                a, b = a[:half], b[half:]
            from_low[c] = lax.ppermute(a, "ch", up)
            from_high[c] = lax.ppermute(b, "ch", down)
            lows[c].append(from_low[c])
            highs[c].append(from_high[c])

    outs = []
    for c in range(CHUNKS):
        parts = [gated[c], *lows[c][:3], *highs[c][:3], lows[c][3], highs[c][3]]
        own, other = pl.pallas_call(
            project_kernel,
            in_specs=[smem] + [pl.BlockSpec(memory_space=pltpu.VMEM)] * 10,
            out_specs=[pl.BlockSpec(memory_space=pltpu.VMEM)] * 2,
            out_shape=[
                jax.ShapeDtypeStruct((chunk, chans), F32),
                jax.ShapeDtypeStruct((chunk, chans), BF16),
            ],
            compiler_params=params,
            name="project",
        )(place, *parts, w_all)
        theirs = lax.ppermute(other, "ch", across)
        outs.append((own + theirs.astype(F32)).astype(BF16))
    return jnp.concatenate(outs, axis=0)


def solution(mesh):
    return jax.shard_map(
        local,
        mesh=mesh,
        in_specs=(
            P(None, "ctx", "ch"),
            P(None, None, "ch"),
            P("ch", None),
            P("ch", None),
            P("ch"),
            P("ch", "ctx"),
        ),
        out_specs=P("ctx", "ch"),
        check_vma=False,
    )
```

time: 481 us -> 161 us (0.33)
  waiting for transfers between devices: 270 us -> 56.4 us
  other arithmetic: 45.6 us -> 1.2 us
  local copies, waits for them, and re-layouts: 56 us -> 12 us
  matrix products: 43.8 us -> 0 us
  starting transfers between devices: 1.95 us -> 42.4 us
  blocking collectives: 45.3 us -> 15.8 us
  Pallas kernels: 0 us -> 18.8 us
    reduce_scatter x1 -> x0, waiting for transfers between devices: 270 us -> none  [local(): lax.psum_scatter(lax.dot_general(wrow, gated, (((0,), (1,)), ((), ())), p...]
    ppermute x1 -> x29, waiting for transfers between devices: 0.01 us -> 56.4 us  [the longest x12 28.9 us: local(): from_low[c] = lax.ppermute(a, 'ch', up)]
    all_gather x2 -> x0, blocking collectives: 45.3 us -> none  [entering(): everything = jax.tree.map(lambda part: lax.all_gather(part, axis), x)]
    dot_general x4 -> x0, matrix products: 43.8 us -> none  [the longest x1 17.2 us: local(): jnp.einsum('ijc,bjc->bic', toeplitz, blocks, precision=lax.Precision.HIGH...]
    ppermute x1 -> x29, starting transfers between devices: 1.91 us -> 42.4 us  [the longest x12 28.3 us: local(): from_high[c] = lax.ppermute(b, 'ch', down)]
    gather x2 -> x0, local copies, waits for them, and re-layouts: 25.5 us -> none  [local(): jnp.take(short_filt, jnp.maximum(offsets, 0), axis=0)]
    add x27 -> x0, other arithmetic: 20.4 us -> none  [the longest x24 17.4 us: chain(): return (step_decay * state + block_end, state)]
    pallas_call x0 -> x7, Pallas kernels: none -> 18.8 us  [the longest x3 6.91 us: local(): pl.pallas_call(project_kernel, in_specs=[smem] + [pl.BlockSpec(memory_spa...]
  transfers between devices with their start and end apart: 3 -> 30, of which waited for: 1 -> 16; matrix products, arithmetic and copies ran while one was open for 27% -> 1% of each run, Pallas kernels for 0% -> 12%
where the time goes in v1:
time: 161 us; the launch traced here: 160 us
  waiting for transfers between devices  56.4 us (35%)
  starting transfers between devices  42.4 us (26%)
  Pallas kernels  18.8 us (12%)
  blocking collectives  15.8 us (10%)
  between operations  13.6 us (8%)
  local copies, waits for them, and re-layouts  12 us (7%)
    ppermute x12, waiting for transfers between devices, local(): from_low[c] = lax.ppermute(a, 'ch', up)  28.9 us
    ppermute x12, starting transfers between devices, local(): from_high[c] = lax.ppermute(b, 'ch', down)  28.3 us
    all_to_all x1, blocking collectives, local(): recv = lax.all_to_all(send, 'ctx', 0, 0)  15.8 us
    ppermute x1, waiting for transfers between devices, local(): w_block = lax.ppermute(w_out, ('ctx', 'ch'), swap)  10.6 us
    unnamed x34, local copies, waits for them, and re-layouts  10.6 us
    ppermute x12, waiting for transfers between devices, local(): from_high[c] = lax.ppermute(b, 'ch', down)  7.28 us
    pallas_call x3, Pallas kernels, local(): pl.pallas_call(project_kernel, in_specs=[smem] + [pl.BlockSpec(memory_spa...  6.91 us
    pallas_call x3, Pallas kernels, gate(): pl.pallas_call(functools.partial(gate_kernel, c), grid=(tiles,), in_specs...  6.89 us
  transfers between devices with their start and end apart: 30, of which 16 were waited for; matrix products, arithmetic and copies ran while one was open for 1% of the time, Pallas kernels for 12%

profile of v1, /device:TPU:2, one launch (start us, length us, event | category | flops | bytes accessed | tf_op | source)
XLA Modules:
  0.0 160.1 jit_solution(2122251931612658822)
XLA Ops:
  6.5 5.1 %collective-permute-start.9 = (bf16[256,256]{1,0:T(8,128)(2,1)}, bf16[256,256]{1,0:T(8,128)(2,1)S(1)}, u32[]{:S(2)}, u32[]{:S(2)}) collective-permute-start(bf16[256,256]{1,0:T(8,128)(2,1)} %param.11), channel_id=1, source_target_pairs={{0,0},{1,16},{2,32},{3,48},{4,64},{5,80},{6,96},{7,112},{8,8},{9,2... | collective-permute-start | bytes 393224 | tf_op jit(solution)/shard_map/ppermute | solution.py:166
  11.7 10.6 %collective-permute-done.9 = bf16[256,256]{1,0:T(8,128)(2,1)S(1)} collective-permute-done((bf16[256,256]{1,0:T(8,128)(2,1)}, bf16[256,256]{1,0:T(8,128)(2,1)S(1)}, u32[]{:S(2)}, u32[]{:S(2)}) %collective-permute-start.9) | collective-permute-done | bytes 131104 | tf_op jit(solution)/shard_map/ppermute | solution.py:166
  22.3 0.6 copy-done.16
  23.0 0.7 slice.21
  23.7 1.9 %collective-permute-start = (bf16[3,2,256]{2,1,0:T(2,128)(2,1)S(1)}, bf16[3,2,256]{2,1,0:T(2,128)(2,1)S(1)}, u32[]{:S(2)}, u32[]{:S(2)}) collective-permute-start(bf16[3,2,256]{2,1,0:T(2,128)(2,1)S(1)} %slice.21), channel_id=1, source_target_pairs={{0,16},{16,32},{32,48},{48,64},{64,80},{80,96},{96,112},{112,128},... | collective-permute-start | bytes 9224 | tf_op jit(solution)/shard_map/ppermute | solution.py:159
  25.6 3.0 %collective-permute-done.halo_ref.qb_ref = bf16[3,2,256]{2,1,0:T(2,128)(2,1)S(1)} collective-permute-done((bf16[3,2,256]{2,1,0:T(2,128)(2,1)S(1)}, bf16[3,2,256]{2,1,0:T(2,128)(2,1)S(1)}, u32[]{:S(2)}, u32[]{:S(2)}) %collective-permute-start) | collective-permute-done | bytes 3104 | tf_op jit(solution)/shard_map/ppermute | solution.py:159
  28.6 1.7 %copy-done = bf16[3,1536,256]{2,1,0:T(8,128)(2,1)S(1)} copy-done((bf16[3,1536,256]{2,1,0:T(8,128)(2,1)S(1)}, bf16[3,1536,256]{2,1,0:T(8,128)(2,1)}, u32[]{:S(2)}) %copy-start) | copy-done | bytes 2359320
  30.2 0.7 copy-done.4
  31.0 0.7 copy-done.13
  31.7 5.0 %states.1 = (f32[1536,256]{1,0:T(8,128)S(1)}, f32[3,16,8,256]{3,2,1,0:T(8,128)S(1)}, f32[3,16,256]{2,1,0:T(8,128)S(1)}, f32[16,16,256]{2,1,0:T(8,128)S(1)}) custom-call(s32[1]{0:T(128)} %bitcast.5.me_ref, bf16[3,1536,256]{2,1,0:T(8,128)(2,1)S(1)} %copy-done, bf16[3,1536,256]{2,1,0:T(8,128)(2,1)S(1)} %copy-done, ...), custom_call_target="tpu_custom_call" | custom-call | tf_op jit(solution)/shard_map/states/pallas_call | solution.py:176
  36.7 15.8 %all_to_all.5.recv_ref = f32[16,16,256]{2,1,0:T(8,128)S(1)} all-to-all(f32[16,16,256]{2,1,0:T(8,128)S(1)} %get-tuple-element.18), channel_id=1, replica_groups=mesh['ctx'=16,'ch'=16] {'ctx'}, dimensions={0} | all-to-all | bytes 524288 | tf_op jit(solution)/shard_map/all_to_all | solution.py:202
  52.5 2.3 %gate.4.refs_0_ = bf16[512,256]{1,0:T(8,128)(2,1)S(1)} custom-call(bf16[3,1536,256]{2,1,0:T(8,128)(2,1)S(1)} %copy-done.1, bf16[3,1536,256]{2,1,0:T(8,128)(2,1)S(1)} %copy-done.1, f32[3,3,256]{2,1,0:T(4,128)S(1)} %copy-done.13, f32[16,256]{1,0:T(8,128)S(1)} %bitcast.11, f32[16,256]{1,0:T(8,128)S(1)} %bitcast.14, f32[1,256]{1,0:T(1,128)S(1)} %bitcast.17, ...), custom_call_target="tpu_custom_call" | custom-call | tf_op jit(solution)/shard_map/gate/pallas_call | solution.py:210
  54.8 6.2 %collective-permute-start.14 = (bf16[512,256]{1,0:T(8,128)(2,1)S(1)}, bf16[512,256]{1,0:T(8,128)(2,1)S(1)}, u32[]{:S(2)}, u32[]{:S(2)}) collective-permute-start(bf16[512,256]{1,0:T(8,128)(2,1)S(1)} %gate.4.refs_0_), channel_id=1, source_target_pairs={{1,0},{2,1},{3,2},{4,3},{5,4},{6,5},{7,6},{0,7},{9,8},{10,9},{11,1... | collective-permute-start | bytes 786440 | tf_op jit(solution)/shard_map/ppermute | solution.py:250
  61.0 2.3 %gate.5.refs_0_ = bf16[512,256]{1,0:T(8,128)(2,1)S(1)} custom-call(bf16[3,1536,256]{2,1,0:T(8,128)(2,1)S(1)} %copy-done.1, bf16[3,1536,256]{2,1,0:T(8,128)(2,1)S(1)} %copy-done.1, f32[3,3,256]{2,1,0:T(4,128)S(1)} %copy-done.13, f32[16,256]{1,0:T(8,128)S(1)} %bitcast.12, f32[16,256]{1,0:T(8,128)S(1)} %bitcast.15, f32[1,256]{1,0:T(1,128)S(1)} %bitcast.18, ...), custom_call_target="tpu_custom_call" | custom-call | tf_op jit(solution)/shard_map/gate/pallas_call | solution.py:210
  63.3 3.3 %collective-permute-start.23 = (bf16[512,256]{1,0:T(8,128)(2,1)S(1)}, bf16[512,256]{1,0:T(8,128)(2,1)S(1)}, u32[]{:S(2)}, u32[]{:S(2)}) collective-permute-start(bf16[512,256]{1,0:T(8,128)(2,1)S(1)} %gate.5.refs_0_), channel_id=1, source_target_pairs={{1,0},{2,1},{3,2},{4,3},{5,4},{6,5},{7,6},{0,7},{9,8},{10,9},{11,1... | collective-permute-start | bytes 786440 | tf_op jit(solution)/shard_map/ppermute | solution.py:250
  66.6 1.1 collective-permute-done.14.refs_4_
  67.7 3.7 %collective-permute-start.15 = (bf16[512,256]{1,0:T(8,128)(2,1)S(1)}, bf16[512,256]{1,0:T(8,128)(2,1)S(1)}, u32[]{:S(2)}, u32[]{:S(2)}) collective-permute-start(bf16[512,256]{1,0:T(8,128)(2,1)S(1)} %collective-permute-done.14.refs_4_), channel_id=1, source_target_pairs={{1,0},{2,1},{3,2},{4,3},{5,4},{6,5},{7,6},{0,7},{9,8},{10,9},{11,1... | collective-permute-start | bytes 786440 | tf_op jit(solution)/shard_map/ppermute | solution.py:250
  71.4 2.3 %gate.3.refs_0_ = bf16[512,256]{1,0:T(8,128)(2,1)S(1)} custom-call(bf16[3,1536,256]{2,1,0:T(8,128)(2,1)S(1)} %copy-done.1, bf16[3,2,256]{2,1,0:T(2,128)(2,1)S(1)} %collective-permute-done.halo_ref.qb_ref, f32[3,3,256]{2,1,0:T(4,128)S(1)} %copy-done.13, f32[16,256]{1,0:T(8,128)S(1)} %bitcast.13, f32[16,256]{1,0:T(8,128)S(1)} %bitcast.16, ...), custom_call_target="tpu_custom_call" | custom-call | tf_op jit(solution)/shard_map/gate/pallas_call | solution.py:210
  73.7 3.3 %collective-permute-start.4 = (bf16[512,256]{1,0:T(8,128)(2,1)S(1)}, bf16[512,256]{1,0:T(8,128)(2,1)S(1)}, u32[]{:S(2)}, u32[]{:S(2)}) collective-permute-start(bf16[512,256]{1,0:T(8,128)(2,1)S(1)} %gate.3.refs_0_), channel_id=1, source_target_pairs={{1,0},{2,1},{3,2},{4,3},{5,4},{6,5},{7,6},{0,7},{9,8},{10,9},{11,1... | collective-permute-start | bytes 786440 | tf_op jit(solution)/shard_map/ppermute | solution.py:250
  77.0 0.1 collective-permute-start.12
  77.1 1.8 %collective-permute-done.15.refs_5_ = bf16[512,256]{1,0:T(8,128)(2,1)S(1)} collective-permute-done((bf16[512,256]{1,0:T(8,128)(2,1)S(1)}, bf16[512,256]{1,0:T(8,128)(2,1)S(1)}, u32[]{:S(2)}, u32[]{:S(2)}) %collective-permute-start.15) | collective-permute-done | bytes 262176 | tf_op jit(solution)/shard_map/ppermute | solution.py:250
  78.9 3.7 %collective-permute-start.16 = (bf16[512,256]{1,0:T(8,128)(2,1)S(1)}, bf16[512,256]{1,0:T(8,128)(2,1)S(1)}, u32[]{:S(2)}, u32[]{:S(2)}) collective-permute-start(bf16[512,256]{1,0:T(8,128)(2,1)S(1)} %collective-permute-done.15.refs_5_), channel_id=1, source_target_pairs={{1,0},{2,1},{3,2},{4,3},{5,4},{6,5},{7,6},{0,7},{9,8},{10,9},{11,1... | collective-permute-start | bytes 786440 | tf_op jit(solution)/shard_map/ppermute | solution.py:250
  82.6 0.7 copy-done.9
  83.3 0.7 collective-permute-start.24
  84.0 0.5 collective-permute-done.4.refs_4_
  84.5 0.8 collective-permute-start.21
  85.3 2.1 %collective-permute-done.1.refs_1_ = bf16[512,256]{1,0:T(8,128)(2,1)S(1)} collective-permute-done((bf16[512,256]{1,0:T(8,128)(2,1)S(1)}, bf16[512,256]{1,0:T(8,128)(2,1)S(1)}, u32[]{:S(2)}, u32[]{:S(2)}) %collective-permute-start.1) | collective-permute-done | bytes 262176 | tf_op jit(solution)/shard_map/ppermute | solution.py:249
  87.5 0.8 collective-permute-start.5
  88.2 4.9 %collective-permute-done.12.refs_2_ = bf16[512,256]{1,0:T(8,128)(2,1)S(1)} collective-permute-done((bf16[512,256]{1,0:T(8,128)(2,1)S(1)}, bf16[512,256]{1,0:T(8,128)(2,1)S(1)}, u32[]{:S(2)}, u32[]{:S(2)}) %collective-permute-start.12) | collective-permute-done | bytes 262176 | tf_op jit(solution)/shard_map/ppermute | solution.py:249
  93.1 0.7 copy-done.11
  93.8 1.9 %collective-permute-done.24.refs_5_ = bf16[512,256]{1,0:T(8,128)(2,1)} collective-permute-done((bf16[512,256]{1,0:T(8,128)(2,1)S(1)}, bf16[512,256]{1,0:T(8,128)(2,1)}, u32[]{:S(2)}, u32[]{:S(2)}) %collective-permute-start.24) | collective-permute-done | bytes 262176 | tf_op jit(solution)/shard_map/ppermute | solution.py:250
  95.8 3.8 %collective-permute-start.18 = (bf16[256,256]{1,0:T(8,128)(2,1)S(1)}, bf16[256,256]{1,0:T(8,128)(2,1)S(1)}, u32[]{:S(2)}, u32[]{:S(2)}) collective-permute-start(bf16[256,256]{1,0:T(8,128)(2,1)S(1)} %slice.31), channel_id=1, source_target_pairs={{1,0},{2,1},{3,2},{4,3},{5,4},{6,5},{7,6},{0,7},{9,8},{10,9},{11,1... | collective-permute-start | bytes 393224 | tf_op jit(solution)/shard_map/ppermute | solution.py:250
  99.6 0.7 collective-permute-start.25
  100.3 1.1 collective-permute-done.5.refs_5_
  101.4 0.2 collective-permute-start.22
  101.6 2.8 %collective-permute-done.2.refs_2_ = bf16[512,256]{1,0:T(8,128)(2,1)} collective-permute-done((bf16[512,256]{1,0:T(8,128)(2,1)S(1)}, bf16[512,256]{1,0:T(8,128)(2,1)}, u32[]{:S(2)}, u32[]{:S(2)}) %collective-permute-start.2) | collective-permute-done | bytes 262176 | tf_op jit(solution)/shard_map/ppermute | solution.py:249
  104.4 0.8 collective-permute-start.6
  105.2 4.8 %collective-permute-done.13.refs_3_ = bf16[512,256]{1,0:T(8,128)(2,1)S(1)} collective-permute-done((bf16[512,256]{1,0:T(8,128)(2,1)S(1)}, bf16[512,256]{1,0:T(8,128)(2,1)S(1)}, u32[]{:S(2)}, u32[]{:S(2)}) %collective-permute-start.13) | collective-permute-done | bytes 262176 | tf_op jit(solution)/shard_map/ppermute | solution.py:249
  109.9 0.7 slice.30
  110.6 0.1 pad_add_fusion.place_ref
  110.7 11.9 %collective-permute-done.17.refs_7_ = bf16[256,256]{1,0:T(8,128)(2,1)} collective-permute-done((bf16[256,256]{1,0:T(8,128)(2,1)}, bf16[256,256]{1,0:T(8,128)(2,1)}, u32[]{:S(2)}, u32[]{:S(2)}) %collective-permute-start.17) | collective-permute-done | bytes 131104 | tf_op jit(solution)/shard_map/ppermute | solution.py:249
  122.6 1.6 copy-done.2
  124.2 0.9 copy-done.6
  125.1 0.9 copy-done.8
  126.1 0.9 copy-done.10
  127.0 0.9 copy-done.12
  128.0 2.3 %project.4 = (f32[512,256]{1,0:T(8,128)S(1)}, bf16[512,256]{1,0:T(8,128)(2,1)S(1)}) custom-call(s32[2]{0:T(128)S(1)} %pad_add_fusion.place_ref, bf16[512,256]{1,0:T(8,128)(2,1)S(1)} %gate.4.refs_0_, bf16[512,256]{1,0:T(8,128)(2,1)S(1)} %copy-done.8, bf16[512,256]{1,0:T(8,128)(2,1)S(1)} %copy-done.12, bf16[512,256]{1,0:T(8,128)(2,1)S(1)} %collective-permute-done.13.refs_3_, ...), custom_call_target="tpu_custom_call" | custom-call | tf_op jit(solution)/shard_map/project/pallas_call | solution.py:257
  130.3 0.7 collective-permute-start.19
  131.0 0.1 collective-permute-start.27
  131.1 2.1 %collective-permute-start.26 = (bf16[256,256]{1,0:T(8,128)(2,1)S(1)}, bf16[256,256]{1,0:T(8,128)(2,1)S(1)}, u32[]{:S(2)}, u32[]{:S(2)}) collective-permute-start(bf16[256,256]{1,0:T(8,128)(2,1)S(1)} %slice.32), channel_id=1, source_target_pairs={{0,1},{1,2},{2,3},{3,4},{4,5},{5,6},{6,7},{7,0},{8,9},{9,10},{10,1... | collective-permute-start | bytes 393224 | tf_op jit(solution)/shard_map/ppermute | solution.py:249
  133.2 1.3 collective-permute-start.8
  134.6 0.9 collective-permute-start.7
  135.4 0.9 collective-permute-done.27.refs_8_
  136.3 2.5 %collective-permute-done.26.refs_7_ = bf16[256,256]{1,0:T(8,128)(2,1)S(1)} collective-permute-done((bf16[256,256]{1,0:T(8,128)(2,1)S(1)}, bf16[256,256]{1,0:T(8,128)(2,1)S(1)}, u32[]{:S(2)}, u32[]{:S(2)}) %collective-permute-start.26) | collective-permute-done | bytes 131104 | tf_op jit(solution)/shard_map/ppermute | solution.py:249
  138.8 2.3 %project.5 = (f32[512,256]{1,0:T(8,128)S(1)}, bf16[512,256]{1,0:T(8,128)(2,1)S(1)}) custom-call(s32[2]{0:T(128)S(1)} %pad_add_fusion.place_ref, bf16[512,256]{1,0:T(8,128)(2,1)S(1)} %gate.5.refs_0_, bf16[512,256]{1,0:T(8,128)(2,1)S(1)} %collective-permute-done.20.refs_1_, bf16[512,256]{1,0:T(8,128)(2,1)} %collective-permute-done.21.refs_2_, ...), custom_call_target="tpu_custom_call" | custom-call | tf_op jit(solution)/shard_map/project/pallas_call | solution.py:257
  141.1 1.4 collective-permute-start.28
  142.5 2.3 %project.3 = (f32[512,256]{1,0:T(8,128)S(1)}, bf16[512,256]{1,0:T(8,128)(2,1)S(1)}) custom-call(s32[2]{0:T(128)S(1)} %pad_add_fusion.place_ref, bf16[512,256]{1,0:T(8,128)(2,1)S(1)} %gate.3.refs_0_, bf16[512,256]{1,0:T(8,128)(2,1)S(1)} %collective-permute-done.1.refs_1_, bf16[512,256]{1,0:T(8,128)(2,1)} %collective-permute-done.2.refs_2_, ...), custom_call_target="tpu_custom_call" | custom-call | tf_op jit(solution)/shard_map/project/pallas_call | solution.py:257
  144.8 0.8 collective-permute-start.10
  145.6 0.1 add_convert_fusion.1
  145.6 3.8 %collective-permute-done.28 = bf16[512,256]{1,0:T(8,128)(2,1)S(1)} collective-permute-done((bf16[512,256]{1,0:T(8,128)(2,1)S(1)}, bf16[512,256]{1,0:T(8,128)(2,1)S(1)}, u32[]{:S(2)}, u32[]{:S(2)}) %collective-permute-start.28) | collective-permute-done | bytes 262176 | tf_op jit(solution)/shard_map/ppermute | solution.py:268
  149.5 0.1 add_convert_fusion
  149.5 2.7 %collective-permute-done.10 = bf16[512,256]{1,0:T(8,128)(2,1)S(1)} collective-permute-done((bf16[512,256]{1,0:T(8,128)(2,1)S(1)}, bf16[512,256]{1,0:T(8,128)(2,1)S(1)}, u32[]{:S(2)}, u32[]{:S(2)}) %collective-permute-start.10) | collective-permute-done | bytes 262176 | tf_op jit(solution)/shard_map/ppermute | solution.py:268
  152.3 0.1 add_convert_fusion.2
  152.3 0.9 pad_maximum_fusion
  (51 shorter events, 0.2 us)
Async XLA Ops:
  6.5 116.0 %all-gather.3.cloned.1.call-start = ((), (), s32[]{:S(2)}) async-start(), calls=%async_computation.1 | async-start | bytes 2228224 | tf_op jit(solution)/shard_map/all_gather | solution.py:167
  6.5 15.8 %collective-permute-start.9 = (bf16[256,256]{1,0:T(8,128)(2,1)}, bf16[256,256]{1,0:T(8,128)(2,1)S(1)}, u32[]{:S(2)}, u32[]{:S(2)}) collective-permute-start(bf16[256,256]{1,0:T(8,128)(2,1)} %param.11), channel_id=1, source_target_pairs={{0,0},{1,16},{2,32},{3,48},{4,64},{5,80},{6,96},{7,112},{8,8},{9,2... | collective-permute-start | bytes 393224 | tf_op jit(solution)/shard_map/ppermute | solution.py:166
  22.3 0.6 copy-start.16
  23.7 4.9 %collective-permute-start = (bf16[3,2,256]{2,1,0:T(2,128)(2,1)S(1)}, bf16[3,2,256]{2,1,0:T(2,128)(2,1)S(1)}, u32[]{:S(2)}, u32[]{:S(2)}) collective-permute-start(bf16[3,2,256]{2,1,0:T(2,128)(2,1)S(1)} %slice.21), channel_id=1, source_target_pairs={{0,16},{16,32},{32,48},{48,64},{64,80},{80,96},{96,112},{112,128},... | collective-permute-start | bytes 9224 | tf_op jit(solution)/shard_map/ppermute | solution.py:159
  28.6 1.7 %copy-start = (bf16[3,1536,256]{2,1,0:T(8,128)(2,1)S(1)}, bf16[3,1536,256]{2,1,0:T(8,128)(2,1)}, u32[]{:S(2)}) copy-start(bf16[3,1536,256]{2,1,0:T(8,128)(2,1)} %qb_ref.3) | copy-start | bytes 7077892
  30.2 0.7 copy-start.4
  31.0 0.7 copy-start.13
  31.7 20.8 %copy-start.1 = (bf16[3,1536,256]{2,1,0:T(8,128)(2,1)S(1)}, bf16[3,1536,256]{2,1,0:T(8,128)(2,1)}, u32[]{:S(2)}) copy-start(bf16[3,1536,256]{2,1,0:T(8,128)(2,1)} %qb_ref.3) | copy-start | bytes 7077892
  31.7 20.8 %copy-start.14 = (f32[256,16]{0,1:T(8,128)S(1)}, f32[256,16]{0,1:T(8,128)}, u32[]{:S(2)}) copy-start(f32[256,16]{0,1:T(8,128)} %param.8) | copy-start | bytes 49156
  31.7 20.8 %copy-start.15 = (f32[256]{0:T(256)S(1)}, f32[256]{0:T(256)}, u32[]{:S(2)}) copy-start(f32[256]{0:T(256)} %param.10) | copy-start | bytes 3076
  54.8 12.9 %collective-permute-start.14 = (bf16[512,256]{1,0:T(8,128)(2,1)S(1)}, bf16[512,256]{1,0:T(8,128)(2,1)S(1)}, u32[]{:S(2)}, u32[]{:S(2)}) collective-permute-start(bf16[512,256]{1,0:T(8,128)(2,1)S(1)} %gate.4.refs_0_), channel_id=1, source_target_pairs={{1,0},{2,1},{3,2},{4,3},{5,4},{6,5},{7,6},{0,7},{9,8},{10,9},{11,1... | collective-permute-start | bytes 786440 | tf_op jit(solution)/shard_map/ppermute | solution.py:250
  61.0 16.0 %collective-permute-start.11 = (bf16[512,256]{1,0:T(8,128)(2,1)S(1)}, bf16[512,256]{1,0:T(8,128)(2,1)S(1)}, u32[]{:S(2)}, u32[]{:S(2)}) collective-permute-start(bf16[512,256]{1,0:T(8,128)(2,1)S(1)} %gate.4.refs_0_), channel_id=1, source_target_pairs={{0,1},{1,2},{2,3},{3,4},{4,5},{5,6},{6,7},{7,0},{8,9},{9,10},{10,1... | collective-permute-start | bytes 786440 | tf_op jit(solution)/shard_map/ppermute | solution.py:249
  63.3 13.7 %collective-permute-start.23 = (bf16[512,256]{1,0:T(8,128)(2,1)S(1)}, bf16[512,256]{1,0:T(8,128)(2,1)S(1)}, u32[]{:S(2)}, u32[]{:S(2)}) collective-permute-start(bf16[512,256]{1,0:T(8,128)(2,1)S(1)} %gate.5.refs_0_), channel_id=1, source_target_pairs={{1,0},{2,1},{3,2},{4,3},{5,4},{6,5},{7,6},{0,7},{9,8},{10,9},{11,1... | collective-permute-start | bytes 786440 | tf_op jit(solution)/shard_map/ppermute | solution.py:250
  67.7 6.0 %copy-start.5 = (bf16[512,256]{1,0:T(8,128)(2,1)}, bf16[512,256]{1,0:T(8,128)(2,1)S(1)}, u32[]{:S(2)}) copy-start(bf16[512,256]{1,0:T(8,128)(2,1)S(1)} %collective-permute-done.14.refs_4_) | copy-start | bytes 786436
  67.7 11.2 %collective-permute-start.15 = (bf16[512,256]{1,0:T(8,128)(2,1)S(1)}, bf16[512,256]{1,0:T(8,128)(2,1)S(1)}, u32[]{:S(2)}, u32[]{:S(2)}) collective-permute-start(bf16[512,256]{1,0:T(8,128)(2,1)S(1)} %collective-permute-done.14.refs_4_), channel_id=1, source_target_pairs={{1,0},{2,1},{3,2},{4,3},{5,4},{6,5},{7,6},{0,7},{9,8},{10,9},{11,1... | collective-permute-start | bytes 786440 | tf_op jit(solution)/shard_map/ppermute | solution.py:250
  71.4 11.9 %collective-permute-start.20 = (bf16[512,256]{1,0:T(8,128)(2,1)S(1)}, bf16[512,256]{1,0:T(8,128)(2,1)S(1)}, u32[]{:S(2)}, u32[]{:S(2)}) collective-permute-start(bf16[512,256]{1,0:T(8,128)(2,1)S(1)} %gate.5.refs_0_), channel_id=1, source_target_pairs={{0,1},{1,2},{2,3},{3,4},{4,5},{5,6},{6,7},{7,0},{8,9},{9,10},{10,1... | collective-permute-start | bytes 786440 | tf_op jit(solution)/shard_map/ppermute | solution.py:249
  73.7 10.8 %collective-permute-start.4 = (bf16[512,256]{1,0:T(8,128)(2,1)S(1)}, bf16[512,256]{1,0:T(8,128)(2,1)S(1)}, u32[]{:S(2)}, u32[]{:S(2)}) collective-permute-start(bf16[512,256]{1,0:T(8,128)(2,1)S(1)} %gate.3.refs_0_), channel_id=1, source_target_pairs={{1,0},{2,1},{3,2},{4,3},{5,4},{6,5},{7,6},{0,7},{9,8},{10,9},{11,1... | collective-permute-start | bytes 786440 | tf_op jit(solution)/shard_map/ppermute | solution.py:250
  77.0 23.3 %copy-start.7 = (bf16[512,256]{1,0:T(8,128)(2,1)}, bf16[512,256]{1,0:T(8,128)(2,1)S(1)}, u32[]{:S(2)}) copy-start(bf16[512,256]{1,0:T(8,128)(2,1)S(1)} %collective-permute-done.11.refs_1_) | copy-start | bytes 786436
  77.0 10.5 %collective-permute-start.1 = (bf16[512,256]{1,0:T(8,128)(2,1)S(1)}, bf16[512,256]{1,0:T(8,128)(2,1)S(1)}, u32[]{:S(2)}, u32[]{:S(2)}) collective-permute-start(bf16[512,256]{1,0:T(8,128)(2,1)S(1)} %gate.3.refs_0_), channel_id=1, source_target_pairs={{0,1},{1,2},{2,3},{3,4},{4,5},{5,6},{6,7},{7,0},{8,9},{9,10},{10,1... | collective-permute-start | bytes 786440 | tf_op jit(solution)/shard_map/ppermute | solution.py:249
  77.0 16.1 %collective-permute-start.12 = (bf16[512,256]{1,0:T(8,128)(2,1)S(1)}, bf16[512,256]{1,0:T(8,128)(2,1)S(1)}, u32[]{:S(2)}, u32[]{:S(2)}) collective-permute-start(bf16[512,256]{1,0:T(8,128)(2,1)S(1)} %collective-permute-done.11.refs_1_), channel_id=1, source_target_pairs={{0,1},{1,2},{2,3},{3,4},{4,5},{5,6},{6,7},{7,0},{8,9},{9,10},{10,1... | collective-permute-start | bytes 786440 | tf_op jit(solution)/shard_map/ppermute | solution.py:249
  78.9 14.2 %collective-permute-start.16 = (bf16[512,256]{1,0:T(8,128)(2,1)S(1)}, bf16[512,256]{1,0:T(8,128)(2,1)S(1)}, u32[]{:S(2)}, u32[]{:S(2)}) collective-permute-start(bf16[512,256]{1,0:T(8,128)(2,1)S(1)} %collective-permute-done.15.refs_5_), channel_id=1, source_target_pairs={{1,0},{2,1},{3,2},{4,3},{5,4},{6,5},{7,6},{0,7},{9,8},{10,9},{11,1... | collective-permute-start | bytes 786440 | tf_op jit(solution)/shard_map/ppermute | solution.py:250
  82.6 0.7 copy-start.9
  83.3 12.5 %collective-permute-start.24 = (bf16[512,256]{1,0:T(8,128)(2,1)S(1)}, bf16[512,256]{1,0:T(8,128)(2,1)}, u32[]{:S(2)}, u32[]{:S(2)}) collective-permute-start(bf16[512,256]{1,0:T(8,128)(2,1)S(1)} %collective-permute-done.23.refs_4_), channel_id=1, source_target_pairs={{1,0},{2,1},{3,2},{4,3},{5,4},{6,5},{7,6},{0,7},{9,8},{10,9},{11,1... | collective-permute-start | bytes 786440 | tf_op jit(solution)/shard_map/ppermute | solution.py:250
  84.5 15.0 %collective-permute-start.21 = (bf16[512,256]{1,0:T(8,128)(2,1)S(1)}, bf16[512,256]{1,0:T(8,128)(2,1)}, u32[]{:S(2)}, u32[]{:S(2)}) collective-permute-start(bf16[512,256]{1,0:T(8,128)(2,1)S(1)} %collective-permute-done.20.refs_1_), channel_id=1, source_target_pairs={{0,1},{1,2},{2,3},{3,4},{4,5},{5,6},{6,7},{7,0},{8,9},{9,10},{10,1... | collective-permute-start | bytes 786440 | tf_op jit(solution)/shard_map/ppermute | solution.py:249
  87.5 13.9 %collective-permute-start.5 = (bf16[512,256]{1,0:T(8,128)(2,1)S(1)}, bf16[512,256]{1,0:T(8,128)(2,1)}, u32[]{:S(2)}, u32[]{:S(2)}) collective-permute-start(bf16[512,256]{1,0:T(8,128)(2,1)S(1)} %collective-permute-done.4.refs_4_), channel_id=1, source_target_pairs={{1,0},{2,1},{3,2},{4,3},{5,4},{6,5},{7,6},{0,7},{9,8},{10,9},{11,1... | collective-permute-start | bytes 786440 | tf_op jit(solution)/shard_map/ppermute | solution.py:250
  93.1 11.3 %collective-permute-start.2 = (bf16[512,256]{1,0:T(8,128)(2,1)S(1)}, bf16[512,256]{1,0:T(8,128)(2,1)}, u32[]{:S(2)}, u32[]{:S(2)}) collective-permute-start(bf16[512,256]{1,0:T(8,128)(2,1)S(1)} %collective-permute-done.1.refs_1_), channel_id=1, source_target_pairs={{0,1},{1,2},{2,3},{3,4},{4,5},{5,6},{6,7},{7,0},{8,9},{9,10},{10,1... | collective-permute-start | bytes 786440 | tf_op jit(solution)/shard_map/ppermute | solution.py:249
  93.1 16.8 %collective-permute-start.13 = (bf16[512,256]{1,0:T(8,128)(2,1)S(1)}, bf16[512,256]{1,0:T(8,128)(2,1)S(1)}, u32[]{:S(2)}, u32[]{:S(2)}) collective-permute-start(bf16[512,256]{1,0:T(8,128)(2,1)S(1)} %collective-permute-done.12.refs_2_), channel_id=1, source_target_pairs={{0,1},{1,2},{2,3},{3,4},{4,5},{5,6},{6,7},{7,0},{8,9},{9,10},{10,1... | collective-permute-start | bytes 786440 | tf_op jit(solution)/shard_map/ppermute | solution.py:249
  93.1 0.7 copy-start.11
  95.8 14.9 %collective-permute-start.18 = (bf16[256,256]{1,0:T(8,128)(2,1)S(1)}, bf16[256,256]{1,0:T(8,128)(2,1)S(1)}, u32[]{:S(2)}, u32[]{:S(2)}) collective-permute-start(bf16[256,256]{1,0:T(8,128)(2,1)S(1)} %slice.31), channel_id=1, source_target_pairs={{1,0},{2,1},{3,2},{4,3},{5,4},{6,5},{7,6},{0,7},{9,8},{10,9},{11,1... | collective-permute-start | bytes 393224 | tf_op jit(solution)/shard_map/ppermute | solution.py:250
  99.6 31.4 %collective-permute-start.25 = (bf16[512,256]{1,0:T(8,128)(2,1)}, bf16[512,256]{1,0:T(8,128)(2,1)S(1)}, u32[]{:S(2)}, u32[]{:S(2)}) collective-permute-start(bf16[512,256]{1,0:T(8,128)(2,1)} %collective-permute-done.24.refs_5_), channel_id=1, source_target_pairs={{1,0},{2,1},{3,2},{4,3},{5,4},{6,5},{7,6},{0,7},{9,8},{10,9},{11,1... | collective-permute-start | bytes 786440 | tf_op jit(solution)/shard_map/ppermute | solution.py:250
  101.4 29.7 %collective-permute-start.22 = (bf16[512,256]{1,0:T(8,128)(2,1)}, bf16[512,256]{1,0:T(8,128)(2,1)S(1)}, u32[]{:S(2)}, u32[]{:S(2)}) collective-permute-start(bf16[512,256]{1,0:T(8,128)(2,1)} %collective-permute-done.21.refs_2_), channel_id=1, source_target_pairs={{0,1},{1,2},{2,3},{3,4},{4,5},{5,6},{6,7},{7,0},{8,9},{9,10},{10,1... | collective-permute-start | bytes 786440 | tf_op jit(solution)/shard_map/ppermute | solution.py:249
  104.4 28.8 %collective-permute-start.6 = (bf16[512,256]{1,0:T(8,128)(2,1)}, bf16[512,256]{1,0:T(8,128)(2,1)S(1)}, u32[]{:S(2)}, u32[]{:S(2)}) collective-permute-start(bf16[512,256]{1,0:T(8,128)(2,1)} %collective-permute-done.5.refs_5_), channel_id=1, source_target_pairs={{1,0},{2,1},{3,2},{4,3},{5,4},{6,5},{7,6},{0,7},{9,8},{10,9},{11,1... | collective-permute-start | bytes 786440 | tf_op jit(solution)/shard_map/ppermute | solution.py:250
  109.9 24.6 %collective-permute-start.3 = (bf16[512,256]{1,0:T(8,128)(2,1)}, bf16[512,256]{1,0:T(8,128)(2,1)S(1)}, u32[]{:S(2)}, u32[]{:S(2)}) collective-permute-start(bf16[512,256]{1,0:T(8,128)(2,1)} %collective-permute-done.2.refs_2_), channel_id=1, source_target_pairs={{0,1},{1,2},{2,3},{3,4},{4,5},{5,6},{6,7},{7,0},{8,9},{9,10},{10,1... | collective-permute-start | bytes 786440 | tf_op jit(solution)/shard_map/ppermute | solution.py:249
  110.6 11.9 %collective-permute-start.17 = (bf16[256,256]{1,0:T(8,128)(2,1)}, bf16[256,256]{1,0:T(8,128)(2,1)}, u32[]{:S(2)}, u32[]{:S(2)}) collective-permute-start(bf16[256,256]{1,0:T(8,128)(2,1)} %slice.30), channel_id=1, source_target_pairs={{0,1},{1,2},{2,3},{3,4},{4,5},{5,6},{6,7},{7,0},{8,9},{9,10},{10,1... | collective-permute-start | bytes 393224 | tf_op jit(solution)/shard_map/ppermute | solution.py:249
  122.6 1.6 copy-start.2
  124.2 0.9 copy-start.6
  125.1 0.9 copy-start.8
  126.1 0.9 copy-start.10
  127.0 0.9 copy-start.12
  128.0 10.8 %copy-start.3 = (bf16[4096,256]{1,0:T(8,128)(2,1)S(1)}, bf16[4096,256]{1,0:T(8,128)(2,1)}, u32[]{:S(2)}) copy-start(bf16[4096,256]{1,0:T(8,128)(2,1)} %all-gather.3.cloned.1.call-done) | copy-start | bytes 6291460
  130.3 15.3 %collective-permute-start.19 = (bf16[512,256]{1,0:T(8,128)(2,1)S(1)}, bf16[512,256]{1,0:T(8,128)(2,1)S(1)}, u32[]{:S(2)}, u32[]{:S(2)}) collective-permute-start(bf16[512,256]{1,0:T(8,128)(2,1)S(1)} %get-tuple-element.22), channel_id=1, source_target_pairs={{0,8},{1,9},{2,10},{3,11},{4,12},{5,13},{6,14},{7,15},{8,0},{9,1},... | collective-permute-start | bytes 786440 | tf_op jit(solution)/shard_map/ppermute | solution.py:268
  131.0 5.3 %collective-permute-start.27 = (bf16[256,256]{1,0:T(8,128)(2,1)S(1)}, bf16[256,256]{1,0:T(8,128)(2,1)S(1)}, u32[]{:S(2)}, u32[]{:S(2)}) collective-permute-start(bf16[256,256]{1,0:T(8,128)(2,1)S(1)} %slice.33), channel_id=1, source_target_pairs={{1,0},{2,1},{3,2},{4,3},{5,4},{6,5},{7,6},{0,7},{9,8},{10,9},{11,1... | collective-permute-start | bytes 393224 | tf_op jit(solution)/shard_map/ppermute | solution.py:250
  131.1 7.6 %collective-permute-start.26 = (bf16[256,256]{1,0:T(8,128)(2,1)S(1)}, bf16[256,256]{1,0:T(8,128)(2,1)S(1)}, u32[]{:S(2)}, u32[]{:S(2)}) collective-permute-start(bf16[256,256]{1,0:T(8,128)(2,1)S(1)} %slice.32), channel_id=1, source_target_pairs={{0,1},{1,2},{2,3},{3,4},{4,5},{5,6},{6,7},{7,0},{8,9},{9,10},{10,1... | collective-permute-start | bytes 393224 | tf_op jit(solution)/shard_map/ppermute | solution.py:249
  133.2 9.3 %collective-permute-start.8 = (bf16[256,256]{1,0:T(8,128)(2,1)S(1)}, bf16[256,256]{1,0:T(8,128)(2,1)S(1)}, u32[]{:S(2)}, u32[]{:S(2)}) collective-permute-start(bf16[256,256]{1,0:T(8,128)(2,1)S(1)} %slice.29), channel_id=1, source_target_pairs={{1,0},{2,1},{3,2},{4,3},{5,4},{6,5},{7,6},{0,7},{9,8},{10,9},{11,1... | collective-permute-start | bytes 393224 | tf_op jit(solution)/shard_map/ppermute | solution.py:250
  134.6 7.9 %collective-permute-start.7 = (bf16[256,256]{1,0:T(8,128)(2,1)S(1)}, bf16[256,256]{1,0:T(8,128)(2,1)S(1)}, u32[]{:S(2)}, u32[]{:S(2)}) collective-permute-start(bf16[256,256]{1,0:T(8,128)(2,1)S(1)} %slice.28), channel_id=1, source_target_pairs={{0,1},{1,2},{2,3},{3,4},{4,5},{5,6},{6,7},{7,0},{8,9},{9,10},{10,1... | collective-permute-start | bytes 393224 | tf_op jit(solution)/shard_map/ppermute | solution.py:249
  141.1 8.4 %collective-permute-start.28 = (bf16[512,256]{1,0:T(8,128)(2,1)S(1)}, bf16[512,256]{1,0:T(8,128)(2,1)S(1)}, u32[]{:S(2)}, u32[]{:S(2)}) collective-permute-start(bf16[512,256]{1,0:T(8,128)(2,1)S(1)} %get-tuple-element.24), channel_id=1, source_target_pairs={{0,8},{1,9},{2,10},{3,11},{4,12},{5,13},{6,14},{7,15},{8,0},{9,1},... | collective-permute-start | bytes 786440 | tf_op jit(solution)/shard_map/ppermute | solution.py:268
  144.8 7.5 %collective-permute-start.10 = (bf16[512,256]{1,0:T(8,128)(2,1)S(1)}, bf16[512,256]{1,0:T(8,128)(2,1)S(1)}, u32[]{:S(2)}, u32[]{:S(2)}) collective-permute-start(bf16[512,256]{1,0:T(8,128)(2,1)S(1)} %get-tuple-element.20), channel_id=1, source_target_pairs={{0,8},{1,9},{2,10},{3,11},{4,12},{5,13},{6,14},{7,15},{8,0},{9,1},... | collective-permute-start | bytes 786440 | tf_op jit(solution)/shard_map/ppermute | solution.py:268
Sparse Core Ops, SparseCore 0:
  23.1 55.5 all-gather.2

commit v2 on v1

v2 whole, which is shorter than its diff:
```python
import functools

import jax
import jax.numpy as jnp
from jax import lax
from jax.experimental import pallas as pl
from jax.experimental.pallas import tpu as pltpu
from jax.sharding import PartitionSpec as P

MODES = 16
LANES = 128
SEGS = 8
CHUNKS = ((0, 512), (512, 512), (1024, 512))
ROWS = 48
TILE = 256
CTX = 16
CH = 16
RING = 8
F32 = jnp.float32
BF16 = jnp.bfloat16
MIB = 1024 * 1024


PLAN = [
    ("hop", 0, 1),
    ("hop", 1, 1),
    ("later", 2, 0, 1),
    ("hop", 0, 2),
    ("hop", 2, 1),
    ("hop", 1, 2),
    ("hop", 0, 3),
    ("hop", 2, 2),
    ("hop", 1, 3),
    ("hop", 0, 4, "up"),
    ("hop", 2, 3),
    ("hop", 1, 4, "down"),
    ("hop", 2, 4),
    ("project", 0),
    ("project", 1),
    ("project", 2),
]


def row_ids():
    return lax.broadcasted_iota(jnp.int32, (SEGS, LANES), 0)


def wide(row):
    return jnp.broadcast_to(row, (SEGS, LANES))


def states_kernel(
    k_ref, v_ref, q_tail_ref, taps_ref, decay_ref, res_ref,
    drive_ref, segend_ref, start_ref, send_ref, modes_ref, kx, vx,
):
    tokens = k_ref.shape[1]
    kx[pl.ds(0, 8), :] = jnp.zeros((8, LANES), F32)
    vx[pl.ds(0, 8), :] = jnp.zeros((8, LANES), F32)
    kx[pl.ds(8, tokens), :] = k_ref[0].astype(F32)
    vx[pl.ds(8, tokens), :] = v_ref[0].astype(F32)
    decay = decay_ref[...]
    modes_ref[0] = decay
    modes_ref[1] = res_ref[...] * jnp.sqrt(decay)
    keep = jnp.exp(-decay)
    keeps = [wide(keep[m : m + 1]) for m in range(MODES)]
    tk = [wide(taps_ref[1, j : j + 1, :]) for j in range(3)]
    tv = [wide(taps_ref[2, j : j + 1, :]) for j in range(3)]
    later = (SEGS - 1 - row_ids()).astype(F32)
    state = jnp.zeros((MODES, LANES), F32)

    for c, (offset, chunk) in enumerate(CHUNKS):
        steps = chunk // SEGS

        def at(ref, i):
            return ref[pl.ds(8 + offset + i, SEGS, stride=steps), :]

        def step(i, carry):
            k1, k2, v1, v2, acc = carry
            k0, v0 = at(kx, i), at(vx, i)
            keyed = tk[0] * k0 + tk[1] * k1 + tk[2] * k2
            valued = tv[0] * v0 + tv[1] * v1 + tv[2] * v2
            drive = keyed * valued
            drive_ref[pl.ds(pl.multiple_of(offset + i * SEGS, SEGS), SEGS), :] = drive
            return k0, k1, v0, v1, tuple(a * s + drive for a, s in zip(keeps, acc))

        zero = tuple(jnp.zeros((SEGS, LANES), F32) for _ in range(MODES))
        acc = lax.fori_loop(
            0, steps, step,
            (at(kx, -1), at(kx, -2), at(vx, -1), at(vx, -2), zero),
            unroll=8,
        )[4]
        start_ref[c] = state
        ends = []
        for m in range(MODES):
            segend_ref[c, m] = acc[m]
            weight = jnp.exp(-wide(decay[m : m + 1]) * (later * steps))
            ends.append(jnp.sum(acc[m] * weight, axis=0, keepdims=True))
        state = state * jnp.exp(-decay * chunk) + jnp.concatenate(ends, axis=0)

    tail = q_tail_ref.shape[1] - 2
    upper = state.astype(BF16).astype(F32)
    payload = jnp.concatenate(
        [
            upper,
            state - upper,
            kx[pl.ds(8, 2), :],
            vx[pl.ds(8, 2), :],
            q_tail_ref[0].astype(F32)[tail:],
            kx[pl.ds(6 + tokens, 2), :],
            vx[pl.ds(6 + tokens, 2), :],
            jnp.zeros((ROWS - 2 * MODES - 10, LANES), F32),
        ],
        axis=0,
    ).astype(BF16)
    for j in range(CTX):
        send_ref[j] = payload


def first_drive(taps_ref, heads, tails):
    short, full = [], []
    for s in (1, 2):
        t0, t1, t2 = (taps_ref[s, j : j + 1, :] for j in range(3))
        (x0, x1), (p2, p1) = heads[s - 1], tails[s - 1]
        short.append((t0 * x0, t0 * x1 + t1 * x0))
        full.append((short[-1][0] + t1 * p1 + t2 * p2, short[-1][1] + t2 * p1))
    return [full[0][i] * full[1][i] - short[0][i] * short[1][i] for i in range(2)]


def incoming_states(me, tokens, taps_ref, decay, recv_ref):
    span = jnp.exp(-decay * tokens)
    near = jnp.exp(-decay * (tokens - 1))
    next_to_near = jnp.exp(-decay * (tokens - 2))
    state = jnp.zeros((MODES, LANES), F32)
    extra = [jnp.zeros((1, LANES), F32)] * 2
    q_halo = jnp.zeros((2, LANES), F32)
    raw = [recv_ref[i, pl.ds(2 * MODES, 16), :].astype(F32) for i in range(CTX)]
    for i in range(CTX):
        ended = recv_ref[i, :MODES, :].astype(F32) + recv_ref[i, MODES : 2 * MODES, :].astype(F32)
        if i > 0:
            heads = [[raw[i][r : r + 1], raw[i][r + 1 : r + 2]] for r in (0, 2)]
            tails = [[raw[i - 1][r : r + 1], raw[i - 1][r + 1 : r + 2]] for r in (6, 8)]
            d0, d1 = first_drive(taps_ref, heads, tails)
            extra = [jnp.where(me == i, d, e) for d, e in zip((d0, d1), extra)]
            q_halo = jnp.where(me == i, raw[i - 1][4:6], q_halo)
            ended = ended + near * d0 + next_to_near * d1
        state = jnp.where(i < me, state * span + ended, state)
    return state, extra, q_halo


def gate_kernel(group, tokens, *refs):
    first = group[0] == 0
    if first:
        (me_ref, q_ref, taps_ref, modes_ref, skip_ref, drive_ref, segend_ref, start_ref, recv_ref) = refs[:9]
        out_refs = refs[9 : 9 + len(group)]
        (entry_ref, qx, gx) = refs[9 + len(group) :]
    else:
        (q_ref, qb_ref, taps_ref, modes_ref, skip_ref, drive_ref, segend_ref, entry_ref) = refs[:8]
        out_refs = refs[8 : 8 + len(group)]
        (qx, gx) = refs[8 + len(group) :]
    decay = modes_ref[0]
    qx[pl.ds(8, q_ref.shape[1]), :] = q_ref[0].astype(F32)
    extra = None
    if first:
        state, extra, q_halo = incoming_states(me_ref[0], tokens, taps_ref, decay, recv_ref)
        qx[pl.ds(6, 2), :] = q_halo
        entries = [state]
        for c in range(1, len(CHUNKS)):
            offset = CHUNKS[c][0]
            entries.append(
                jnp.exp(-decay * offset) * state
                + start_ref[c]
                + jnp.exp(-decay * (offset - 1)) * extra[0]
                + jnp.exp(-decay * (offset - 2)) * extra[1]
            )
            if c not in group:
                entry_ref[c - len(group)] = entries[c]
    else:
        before = qb_ref[0].astype(F32)
        qx[pl.ds(6, 2), :] = before[before.shape[0] - 2 :]
        entries = [entry_ref[k] for k in range(len(group))]
    keep = jnp.exp(-decay)
    scaled = modes_ref[1]
    rows = row_ids()
    keeps = [wide(keep[m : m + 1]) for m in range(MODES)]
    gains = [wide(scaled[m : m + 1]) for m in range(MODES)]
    tq = [wide(taps_ref[0, j : j + 1, :]) for j in range(3)]
    skip = wide(skip_ref[...])

    for k, c in enumerate(group):
        offset, chunk = CHUNKS[c]
        base = offset - CHUNKS[group[0]][0]
        steps = chunk // SEGS
        keep1 = jnp.exp(-decay * steps)
        keep2 = jnp.exp(-decay * (2 * steps))
        keep4 = jnp.exp(-decay * (4 * steps))
        if c == 0:
            fix = jnp.exp(-decay * (steps - 1)) * extra[0] + jnp.exp(-decay * (steps - 2)) * extra[1]
        acc = []
        for m in range(MODES):
            ended = segend_ref[k, m]
            if c == 0:
                ended = ended + jnp.where(rows == 0, wide(fix[m : m + 1]), 0.0)
            x = jnp.where(rows == 0, wide(entries[k][m : m + 1]), pltpu.roll(ended, 1, 0))
            for far, factor in ((1, keep1), (2, keep2), (4, keep4)):
                moved = pltpu.roll(x, far, 0) * wide(factor[m : m + 1])
                x = x + jnp.where(rows >= far, moved, 0.0)
            acc.append(x)

        def at(i):
            return qx[pl.ds(8 + base + i, SEGS, stride=steps), :]

        def step(i, carry, more=None):
            q1, q2, acc = carry
            q0 = at(i)
            drive = drive_ref[pl.ds(pl.multiple_of(base + i * SEGS, SEGS), SEGS), :]
            if more is not None:
                drive = drive + jnp.where(rows == 0, wide(more), 0.0)
            acc = tuple(a * s + drive for a, s in zip(keeps, acc))
            terms = [g * s for g, s in zip(gains, acc)] + [skip * drive]
            while len(terms) > 1:
                terms = [sum(terms[i + 1 : i + 2], terms[i]) for i in range(0, len(terms), 2)]
            query = tq[0] * q0 + tq[1] * q1 + tq[2] * q2
            gx[pl.ds(base + i, SEGS, stride=steps), :] = query * terms[0]
            return q0, q1, acc

        carry = (at(-1), at(-2), tuple(acc))
        begin = 0
        if c == 0:
            for begin in range(4):
                carry = step(begin, carry, extra[begin] if begin < 2 else None)
            begin = 4
        lax.fori_loop(begin, steps, step, carry, unroll=4)
        out_refs[k][...] = gx[pl.ds(base, chunk), :].astype(BF16)


def project_kernel(side_ref, *refs):
    w_ref, own_ref, other_ref = refs[-3:]
    values = [r[...] for r in refs[:-3]]
    if len(values) == 9:
        far = jnp.where(pl.program_id(0) < pl.num_programs(0) // 2, values[4], values[5])
        values = values[:4] + [far] + values[6:]
    rows = jnp.concatenate(values, axis=1)
    side = side_ref[0]
    own_ref[...] = jnp.dot(rows, w_ref[side], preferred_element_type=F32)
    other_ref[...] = jnp.dot(rows, w_ref[1 - side], preferred_element_type=F32).astype(BF16)


def local(streams, taps, residues, decay, skip, w_out):
    tokens, chans = streams.shape[1], streams.shape[2]
    tiles = chans // LANES
    ctx = lax.axis_index("ctx")
    ch = lax.axis_index("ch")

    swap = []
    for h in range(2):
        for a in range(RING):
            for y in range(2):
                for z in range(RING):
                    there = h * RING + (z - a) % RING
                    swap.append((((h * RING + a) * 2 + y) * RING + z, (there * 2 + y) * RING + a))
    w_block = lax.ppermute(w_out, ("ctx", "ch"), swap)

    skip_row = skip[None, :]
    me = jnp.reshape(ctx, (1,)).astype(jnp.int32)
    smem = pl.BlockSpec(memory_space=pltpu.SMEM)
    cost = pl.CostEstimate(flops=4_000_000_000, bytes_accessed=4_000_000, transcendentals=0)
    params = lambda mib: pltpu.CompilerParams(vmem_limit_bytes=mib * MIB)
    lane = lambda *lead: pl.BlockSpec((*lead, LANES), lambda g: (*([0] * len(lead)), g))

    drive, segend, start, send, modes = pl.pallas_call(
        states_kernel,
        grid=(tiles,),
        in_specs=[
            pl.BlockSpec((1, tokens, LANES), lambda g: (1, 0, g)),
            pl.BlockSpec((1, tokens, LANES), lambda g: (2, 0, g)),
            pl.BlockSpec((1, 16, LANES), lambda g: (0, tokens // 16 - 1, g)),
            lane(3, 3),
            lane(MODES),
            lane(MODES),
        ],
        out_specs=[
            lane(tokens),
            lane(len(CHUNKS), MODES, SEGS),
            lane(len(CHUNKS), MODES),
            lane(CTX, ROWS),
            lane(2, MODES),
        ],
        out_shape=[
            jax.ShapeDtypeStruct((tokens, chans), F32),
            jax.ShapeDtypeStruct((len(CHUNKS), MODES, SEGS, chans), F32),
            jax.ShapeDtypeStruct((len(CHUNKS), MODES, chans), F32),
            jax.ShapeDtypeStruct((CTX, ROWS, chans), BF16),
            jax.ShapeDtypeStruct((2, MODES, chans), F32),
        ],
        scratch_shapes=[pltpu.VMEM((tokens + 8, LANES), F32)] * 2,
        compiler_params=params(60),
        cost_estimate=cost,
        name="states",
    )(streams, streams, streams, taps, decay.T, residues.T)
    w_block, send = lax.optimization_barrier((w_block, send))
    w_all = lax.all_gather(w_block, "ctx").reshape(2, RING * chans, w_out.shape[1])
    recv = lax.all_to_all(send, "ctx", 0, 0)

    def gate(group, entry):
        offset, size = CHUNKS[group[0]][0], sum(CHUNKS[c][1] for c in group)
        many, rest = len(group), len(CHUNKS) - len(group)
        q_spec = pl.BlockSpec((1, size, LANES), lambda g: (0, offset // size, g))
        shared_specs = [
            lane(3, 3),
            lane(2, MODES),
            lane(1),
            pl.BlockSpec((size, LANES), lambda g: (offset // size, g)),
            pl.BlockSpec((many, MODES, SEGS, LANES), lambda g: (group[0] // many, 0, 0, g)),
        ]
        shared = [taps, modes, skip_row, drive, segend]
        out_specs = [lane(CHUNKS[c][1]) for c in group]
        out_shape = [jax.ShapeDtypeStruct((CHUNKS[c][1], chans), BF16) for c in group]
        if group[0] == 0:
            in_specs = [smem, q_spec, *shared_specs, lane(len(CHUNKS), MODES), lane(CTX, ROWS)]
            args = [me, streams, *shared, start, recv]
            out_specs.append(lane(rest, MODES))
            out_shape.append(jax.ShapeDtypeStruct((rest, MODES, chans), F32))
        else:
            before = pl.BlockSpec((1, 16, LANES), lambda g: (0, offset // 16 - 1, g))
            in_specs = [q_spec, before, *shared_specs, lane(rest if many > rest else many, MODES)]
            args = [streams, streams, *shared, entry]
        return pl.pallas_call(
            functools.partial(gate_kernel, group, tokens),
            grid=(tiles,),
            in_specs=in_specs,
            out_specs=out_specs,
            out_shape=out_shape,
            scratch_shapes=[pltpu.VMEM((size + 8, LANES), F32), pltpu.VMEM((size, LANES), F32)],
            compiler_params=params(60),
            cost_estimate=cost,
            name="gate",
        )(*args)

    up = [(y * RING + z, y * RING + (z + 1) % RING) for y in range(2) for z in range(RING)]
    down = [(d, s) for s, d in up]
    across = [(i, (i + RING) % CH) for i in range(CH)]
    side = jnp.reshape(ch // RING, (1,)).astype(jnp.int32)

    *gated, entry = gate((0, 1), None)
    gated += gate((2,), entry)
    count = len(CHUNKS)
    low = [[g] for g in gated]
    high = [[g] for g in gated]

    def hop(c, s, *ways):
        a, b = low[c][-1], high[c][-1]
        if len(ways) == 0:
            ways = ("up", "down")
            if s == RING // 2:
                half = a.shape[0] // 2
                a, b = a[:half], b[half:]
        if "up" in ways:
            low[c].append(lax.ppermute(a, "ch", up))
        if "down" in ways:
            high[c].append(lax.ppermute(b, "ch", down))

    def later(d, c, s):
        low[c][s], high[c][s], g = lax.optimization_barrier((low[c][s], high[c][s], low[d][0]))
        low[d][0], high[d][0] = g, g

    def after(c, d):
        low[c][0], low[d][3], high[d][3] = lax.optimization_barrier((low[c][0], low[d][3], high[d][3]))

    tile = pl.BlockSpec((TILE, chans), lambda g: (g, 0))
    own = [None] * count
    theirs = [None] * count

    def project(c):
        chunk = CHUNKS[c][1]
        far = [*low[c][4:], *high[c][4:]]
        parts = [low[c][0], *high[c][1:4], *far, *low[c][3:0:-1]]
        count = chunk // TILE
        far_specs = [tile]
        if len(far) == 2:
            far_specs = [
                pl.BlockSpec((TILE, chans), lambda g: (jnp.minimum(g, count // 2 - 1), 0)),
                pl.BlockSpec((TILE, chans), lambda g: (jnp.maximum(g - count // 2, 0), 0)),
            ]
        mine, other = pl.pallas_call(
            project_kernel,
            grid=(count,),
            in_specs=[smem] + [tile] * 4 + far_specs + [tile] * 3 + [pl.BlockSpec(w_all.shape, lambda g: (0, 0, 0))],
            out_specs=[tile] * 2,
            out_shape=[
                jax.ShapeDtypeStruct((chunk, chans), F32),
                jax.ShapeDtypeStruct((chunk, chans), BF16),
            ],
            compiler_params=params(60),
            cost_estimate=cost,
            name="project",
        )(side, *parts, w_all)
        own[c] = mine
        theirs[c] = lax.ppermute(other, "ch", across)

    steps = {"hop": hop, "later": later, "after": after, "project": project}
    for kind, *rest in PLAN:
        steps[kind](*rest)

    outs = [(mine + other.astype(F32)).astype(BF16) for mine, other in zip(own, theirs)]
    return jnp.concatenate(outs, axis=0)


def solution(mesh):
    return jax.shard_map(
        local,
        mesh=mesh,
        in_specs=(
            P(None, "ctx", "ch"),
            P(None, None, "ch"),
            P("ch", None),
            P("ch", None),
            P("ch"),
            P("ch", "ctx"),
        ),
        out_specs=P("ctx", "ch"),
        check_vma=False,
    )
```

time: 161 us -> 140 us (0.87)
  blocking collectives: 15.8 us -> 0 us
  waiting for transfers between devices: 56.4 us -> 42.8 us
  Pallas kernels: 18.8 us -> 29.8 us
  local copies, waits for them, and re-layouts: 12 us -> 2.12 us
  starting transfers between devices: 42.4 us -> 50.2 us
    all_to_all x1 -> x0, blocking collectives: 15.8 us -> none  [local(): recv = lax.all_to_all(send, 'ctx', 0, 0)]
    ppermute x28 -> x25, waiting for transfers between devices: 45.8 us -> 33.4 us  [the longest x11 17.6 us: hop(): low[c].append(lax.ppermute(a, 'ch', up))]
    pallas_call x7 -> x6, Pallas kernels: 18.8 us -> 29.8 us  [the longest x3 13.3 us: project(): pl.pallas_call(project_kernel, grid=(count,), in_specs=[smem] + [tile] *...]
    all_to_all x0 -> x1, starting transfers between devices: none -> 10 us  [local(): recv = lax.all_to_all(send, 'ctx', 0, 0)]
    ppermute x1, waiting for transfers between devices: 10.6 us -> 1.49 us  [local(): w_block = lax.ppermute(w_out, ('ctx', 'ch'), swap)]
    unnamed x34 -> x36, local copies, waits for them, and re-layouts: 10.6 us -> 2.1 us
    all_to_all x0 -> x1, waiting for transfers between devices: none -> 7.85 us  [local(): recv = lax.all_to_all(send, 'ctx', 0, 0)]
    ppermute x28 -> x25, starting transfers between devices: 37.2 us -> 33.5 us  [the longest x11 27.3 us: hop(): high[c].append(lax.ppermute(b, 'ch', down))]
  transfers between devices with their start and end apart: 30 -> 28, of which waited for: 16 -> 15; matrix products, arithmetic and copies ran while one was open for 1% -> 0% of each run, Pallas kernels for 12% -> 21%
where the time goes in v2:
time: 140 us
  starting transfers between devices  50.2 us (36%)
  waiting for transfers between devices  42.8 us (31%)
  Pallas kernels  29.8 us (21%)
  between operations  13.6 us (10%)
  local copies, waits for them, and re-layouts  2.12 us (2%)
    ppermute x11, starting transfers between devices, hop(): high[c].append(lax.ppermute(b, 'ch', down))  27.3 us
    ppermute x11, waiting for transfers between devices, hop(): low[c].append(lax.ppermute(a, 'ch', up))  17.6 us
    pallas_call x3, Pallas kernels, project(): pl.pallas_call(project_kernel, grid=(count,), in_specs=[smem] + [tile] *...  13.3 us
    pallas_call x2, Pallas kernels, gate(): pl.pallas_call(functools.partial(gate_kernel, group, tokens), grid=(tiles...  10.1 us
    all_to_all x1, starting transfers between devices, local(): recv = lax.all_to_all(send, 'ctx', 0, 0)  10 us
    ppermute x11, waiting for transfers between devices, hop(): high[c].append(lax.ppermute(b, 'ch', down))  8.77 us
    all_to_all x1, waiting for transfers between devices, local(): recv = lax.all_to_all(send, 'ctx', 0, 0)  7.85 us
    ppermute x3, waiting for transfers between devices, project(): theirs[c] = lax.ppermute(other, 'ch', across)  7.1 us
  transfers between devices with their start and end apart: 28, of which 15 were waited for; matrix products, arithmetic and copies ran while one was open for 0% of the time, Pallas kernels for 21%

profile of v2, /device:TPU:2, one launch (start us, length us, event | category | flops | bytes accessed | tf_op | source)
XLA Modules:
  0.0 139.7 jit_solution(17095152366673094125)
XLA Ops:
  6.5 6.7 %collective-permute-start = (bf16[256,256]{1,0:T(8,128)(2,1)}, bf16[256,256]{1,0:T(8,128)(2,1)S(1)}, u32[]{:S(2)}, u32[]{:S(2)}) collective-permute-start(bf16[256,256]{1,0:T(8,128)(2,1)} %param.11), channel_id=1, source_target_pairs={{0,0},{1,16},{2,32},{3,48},{4,64},{5,80},{6,96},{7,112},{8,8},{9,2... | collective-permute-start | bytes 393224 | tf_op jit(solution)/shard_map/ppermute | solution.py:261
  13.3 6.4 %states.1 = (f32[1536,256]{1,0:T(8,128)}, f32[3,16,8,256]{3,2,1,0:T(8,128)}, f32[3,16,256]{2,1,0:T(8,128)}, bf16[16,48,256]{2,1,0:T(8,128)(2,1)}, f32[2,16,256]{2,1,0:T(8,128)}) custom-call(bf16[3,1536,256]{2,1,0:T(8,128)(2,1)} %refs_1_.3, bf16[3,1536,256]{2,1,0:T(8,128)(2,1)} %refs_1_.3, bf16[3,1536,256]{2,1,0:T(8,128)(2,1)} %refs_1_.3, ...), custom_call_target="tpu_custom_call" | custom-call | flops 4000000000 | bytes 4000000 | tf_op jit(solution)/shard_map/states/pallas_call | solution.py:270
  19.6 1.5 %collective-permute-done = bf16[256,256]{1,0:T(8,128)(2,1)S(1)} collective-permute-done((bf16[256,256]{1,0:T(8,128)(2,1)}, bf16[256,256]{1,0:T(8,128)(2,1)S(1)}, u32[]{:S(2)}, u32[]{:S(2)}) %collective-permute-start) | collective-permute-done | bytes 131104 | tf_op jit(solution)/shard_map/ppermute | solution.py:261
  21.1 0.7 copy-done.4
  21.8 0.0 all-gather.3.cloned.1.call-update
  21.8 10.0 %all-to-all-start = ((bf16[16,48,256]{2,1,0:T(8,128)(2,1)}), bf16[16,48,256]{2,1,0:T(8,128)(2,1)S(1)}, u32[]{:S(2)}, u32[]{:S(2)}) async-start(bf16[16,48,256]{2,1,0:T(8,128)(2,1)} %get-tuple-element.29), calls=%async_computation | async-start | bytes 786432 | tf_op jit(solution)/shard_map/all_to_all | solution.py:302
  31.8 7.8 %all-to-all-done.refs_8_ = bf16[16,48,256]{2,1,0:T(8,128)(2,1)S(1)} async-done(((bf16[16,48,256]{2,1,0:T(8,128)(2,1)}), bf16[16,48,256]{2,1,0:T(8,128)(2,1)S(1)}, u32[]{:S(2)}, u32[]{:S(2)}) %all-to-all-start) | async-done | bytes 393248 | tf_op jit(solution)/shard_map/all_to_all | solution.py:302
  39.7 0.7 copy-done.3
  40.4 6.4 %gate.2 = (bf16[512,256]{1,0:T(8,128)(2,1)}, bf16[512,256]{1,0:T(8,128)(2,1)}, f32[1,16,256]{2,1,0:T(8,128)}) custom-call(s32[1]{0:T(128)} %bitcast.1.refs_0_, bf16[3,1536,256]{2,1,0:T(8,128)(2,1)} %refs_1_.3, f32[3,3,256]{2,1,0:T(4,128)} %refs_2_.3, f32[2,16,256]{2,1,0:T(8,128)} %get-tuple-element.24.refs_3_, f32[1,256]{1,0:T(1,128)} %bitcast.11, ...), custom_call_target="tpu_custom_call" | custom-call | flops 4000000000 | bytes 4000000 | tf_op jit(solution)/shard_map/gate/pallas_call | solution.py:327
  46.8 2.5 %collective-permute-start.2 = (bf16[512,256]{1,0:T(8,128)(2,1)}, bf16[512,256]{1,0:T(8,128)(2,1)S(1)}, u32[]{:S(2)}, u32[]{:S(2)}) collective-permute-start(bf16[512,256]{1,0:T(8,128)(2,1)} %get-tuple-element.30.refs_0_), channel_id=1, source_target_pairs={{1,0},{2,1},{3,2},{4,3},{5,4},{6,5},{7,6},{0,7},{9,8},{10,9},{11,1... | collective-permute-start | bytes 786440 | tf_op jit(solution)/shard_map/ppermute | solution.py:360
  49.3 0.0 collective-permute-start.1
  49.3 1.5 %collective-permute-start.13 = (bf16[512,256]{1,0:T(8,128)(2,1)}, bf16[512,256]{1,0:T(8,128)(2,1)S(1)}, u32[]{:S(2)}, u32[]{:S(2)}) collective-permute-start(bf16[512,256]{1,0:T(8,128)(2,1)} %get-tuple-element.37.refs_0_), channel_id=1, source_target_pairs={{0,1},{1,2},{2,3},{3,4},{4,5},{5,6},{6,7},{7,0},{8,9},{9,10},{10,1... | collective-permute-start | bytes 786440 | tf_op jit(solution)/shard_map/ppermute | solution.py:358
  50.8 1.8 %collective-permute-start.9 = (bf16[512,256]{1,0:T(8,128)(2,1)}, bf16[512,256]{1,0:T(8,128)(2,1)S(1)}, u32[]{:S(2)}, u32[]{:S(2)}) collective-permute-start(bf16[512,256]{1,0:T(8,128)(2,1)} %get-tuple-element.37.refs_0_), channel_id=1, source_target_pairs={{1,0},{2,1},{3,2},{4,3},{5,4},{6,5},{7,6},{0,7},{9,8},{10,9},{11,1... | collective-permute-start | bytes 786440 | tf_op jit(solution)/shard_map/ppermute | solution.py:360
  52.6 3.8 %gate.3.refs_0_ = bf16[512,256]{1,0:T(8,128)(2,1)} custom-call(bf16[3,1536,256]{2,1,0:T(8,128)(2,1)} %refs_1_.3, bf16[3,1536,256]{2,1,0:T(8,128)(2,1)} %refs_1_.3, f32[3,3,256]{2,1,0:T(4,128)} %refs_2_.3, f32[2,16,256]{2,1,0:T(8,128)} %get-tuple-element.24.refs_3_, f32[1,256]{1,0:T(1,128)} %bitcast.12, f32[1536,256]{1,0:T(8,128)} %get-tuple-element.25.refs_5_, ...), custom_call_target="tpu_custom_call" | custom-call | flops 4000000000 | bytes 4000000 | tf_op jit(solution)/shard_map/gate/pallas_call | solution.py:327
  56.4 0.0 collective-permute-done.2.refs_1_
  56.4 0.0 copy-start.9
  56.4 3.5 %collective-permute-done.1.refs_7_ = bf16[512,256]{1,0:T(8,128)(2,1)S(1)} collective-permute-done((bf16[512,256]{1,0:T(8,128)(2,1)}, bf16[512,256]{1,0:T(8,128)(2,1)S(1)}, u32[]{:S(2)}, u32[]{:S(2)}) %collective-permute-start.1) | collective-permute-done | bytes 262176 | tf_op jit(solution)/shard_map/ppermute | solution.py:358
  59.9 0.0 collective-permute-start.20
  59.9 3.2 %collective-permute-start.17 = (bf16[512,256]{1,0:T(8,128)(2,1)}, bf16[512,256]{1,0:T(8,128)(2,1)S(1)}, u32[]{:S(2)}, u32[]{:S(2)}) collective-permute-start(bf16[512,256]{1,0:T(8,128)(2,1)} %gate.3.refs_0_), channel_id=1, source_target_pairs={{1,0},{2,1},{3,2},{4,3},{5,4},{6,5},{7,6},{0,7},{9,8},{10,9},{11,1... | collective-permute-start | bytes 786440 | tf_op jit(solution)/shard_map/ppermute | solution.py:360
  63.1 0.4 collective-permute-start.3
  63.5 2.0 %collective-permute-done.13.refs_7_ = bf16[512,256]{1,0:T(8,128)(2,1)S(1)} collective-permute-done((bf16[512,256]{1,0:T(8,128)(2,1)}, bf16[512,256]{1,0:T(8,128)(2,1)S(1)}, u32[]{:S(2)}, u32[]{:S(2)}) %collective-permute-start.13) | collective-permute-done | bytes 262176 | tf_op jit(solution)/shard_map/ppermute | solution.py:358
  65.5 0.0 collective-permute-start.5
  65.5 0.0 collective-permute-done.9.refs_1_
  65.5 3.2 %collective-permute-start.10 = (bf16[512,256]{1,0:T(8,128)(2,1)S(1)}, bf16[512,256]{1,0:T(8,128)(2,1)S(1)}, u32[]{:S(2)}, u32[]{:S(2)}) collective-permute-start(bf16[512,256]{1,0:T(8,128)(2,1)S(1)} %collective-permute-done.9.refs_1_), channel_id=1, source_target_pairs={{1,0},{2,1},{3,2},{4,3},{5,4},{6,5},{7,6},{0,7},{9,8},{10,9},{11,1... | collective-permute-start | bytes 786440 | tf_op jit(solution)/shard_map/ppermute | solution.py:360
  68.7 2.4 %collective-permute-done.20.refs_8_ = bf16[512,256]{1,0:T(8,128)(2,1)S(1)} collective-permute-done((bf16[512,256]{1,0:T(8,128)(2,1)}, bf16[512,256]{1,0:T(8,128)(2,1)S(1)}, u32[]{:S(2)}, u32[]{:S(2)}) %collective-permute-start.20) | collective-permute-done | bytes 262176 | tf_op jit(solution)/shard_map/ppermute | solution.py:358
  71.1 0.0 collective-permute-start.21
  71.1 0.0 collective-permute-done.17.refs_1_
  71.1 3.2 %collective-permute-start.18 = (bf16[512,256]{1,0:T(8,128)(2,1)S(1)}, bf16[512,256]{1,0:T(8,128)(2,1)}, u32[]{:S(2)}, u32[]{:S(2)}) collective-permute-start(bf16[512,256]{1,0:T(8,128)(2,1)S(1)} %collective-permute-done.17.refs_1_), channel_id=1, source_target_pairs={{1,0},{2,1},{3,2},{4,3},{5,4},{6,5},{7,6},{0,7},{9,8},{10,9},{11,1... | collective-permute-start | bytes 786440 | tf_op jit(solution)/shard_map/ppermute | solution.py:360
  74.3 1.3 collective-permute-done.3.refs_2_
  75.7 1.0 collective-permute-done.5.refs_6_
  76.7 1.0 collective-permute-start.6
  77.7 3.6 %collective-permute-done.10.refs_2_ = bf16[512,256]{1,0:T(8,128)(2,1)S(1)} collective-permute-done((bf16[512,256]{1,0:T(8,128)(2,1)S(1)}, bf16[512,256]{1,0:T(8,128)(2,1)S(1)}, u32[]{:S(2)}, u32[]{:S(2)}) %collective-permute-start.10) | collective-permute-done | bytes 262176 | tf_op jit(solution)/shard_map/ppermute | solution.py:360
  81.3 3.7 %collective-permute-start.11 = (bf16[512,256]{1,0:T(8,128)(2,1)S(1)}, bf16[512,256]{1,0:T(8,128)(2,1)}, u32[]{:S(2)}, u32[]{:S(2)}) collective-permute-start(bf16[512,256]{1,0:T(8,128)(2,1)S(1)} %collective-permute-done.10.refs_2_), channel_id=1, source_target_pairs={{1,0},{2,1},{3,2},{4,3},{5,4},{6,5},{7,6},{0,7},{9,8},{10,9},{11,1... | collective-permute-start | bytes 786440 | tf_op jit(solution)/shard_map/ppermute | solution.py:360
  85.0 0.0 collective-permute-done.21.refs_7_
  85.0 1.9 %collective-permute-done.18.refs_2_ = bf16[512,256]{1,0:T(8,128)(2,1)} collective-permute-done((bf16[512,256]{1,0:T(8,128)(2,1)S(1)}, bf16[512,256]{1,0:T(8,128)(2,1)}, u32[]{:S(2)}, u32[]{:S(2)}) %collective-permute-start.18) | collective-permute-done | bytes 262176 | tf_op jit(solution)/shard_map/ppermute | solution.py:360
  86.9 3.8 %collective-permute-start.19 = (bf16[512,256]{1,0:T(8,128)(2,1)}, bf16[512,256]{1,0:T(8,128)(2,1)S(1)}, u32[]{:S(2)}, u32[]{:S(2)}) collective-permute-start(bf16[512,256]{1,0:T(8,128)(2,1)} %collective-permute-done.18.refs_2_), channel_id=1, source_target_pairs={{1,0},{2,1},{3,2},{4,3},{5,4},{6,5},{7,6},{0,7},{9,8},{10,9},{11,1... | collective-permute-start | bytes 786440 | tf_op jit(solution)/shard_map/ppermute | solution.py:360
  90.7 0.1 collective-permute-start.4
  90.8 2.9 %collective-permute-done.6.refs_5_ = bf16[512,256]{1,0:T(8,128)(2,1)} collective-permute-done((bf16[512,256]{1,0:T(8,128)(2,1)S(1)}, bf16[512,256]{1,0:T(8,128)(2,1)}, u32[]{:S(2)}, u32[]{:S(2)}) %collective-permute-start.6) | collective-permute-done | bytes 262176 | tf_op jit(solution)/shard_map/ppermute | solution.py:358
  93.7 0.0 collective-permute-start.7
  93.7 0.0 collective-permute-done.11.refs_3_
  93.7 0.3 collective-permute-start.15
  93.9 5.2 %collective-permute-done.22.refs_6_ = bf16[512,256]{1,0:T(8,128)(2,1)S(1)} collective-permute-done((bf16[512,256]{1,0:T(8,128)(2,1)S(1)}, bf16[512,256]{1,0:T(8,128)(2,1)S(1)}, u32[]{:S(2)}, u32[]{:S(2)}) %collective-permute-start.22) | collective-permute-done | bytes 262176 | tf_op jit(solution)/shard_map/ppermute | solution.py:358
  99.2 1.6 %collective-permute-start.12 = (bf16[512,256]{1,0:T(8,128)(2,1)}, bf16[512,256]{1,0:T(8,128)(2,1)}, u32[]{:S(2)}, u32[]{:S(2)}) collective-permute-start(bf16[512,256]{1,0:T(8,128)(2,1)} %collective-permute-done.11.refs_3_), channel_id=1, source_target_pairs={{1,0},{2,1},{3,2},{4,3},{5,4},{6,5},{7,6},{0,7},{9,8},{10,9},{11,1... | collective-permute-start | bytes 786440 | tf_op jit(solution)/shard_map/ppermute | solution.py:360
  100.8 0.5 collective-permute-start.23
  101.3 1.9 %collective-permute-done.4.refs_3_ = bf16[512,256]{1,0:T(8,128)(2,1)} collective-permute-done((bf16[512,256]{1,0:T(8,128)(2,1)}, bf16[512,256]{1,0:T(8,128)(2,1)}, u32[]{:S(2)}, u32[]{:S(2)}) %collective-permute-start.4) | collective-permute-done | bytes 262176 | tf_op jit(solution)/shard_map/ppermute | solution.py:360
  103.2 3.7 %collective-permute-start.24 = (bf16[256,256]{1,0:T(8,128)(2,1)S(1)}, bf16[256,256]{1,0:T(8,128)(2,1)}, u32[]{:S(2)}, u32[]{:S(2)}) collective-permute-start(bf16[256,256]{1,0:T(8,128)(2,1)S(1)} %slice.9), channel_id=1, source_target_pairs={{1,0},{2,1},{3,2},{4,3},{5,4},{6,5},{7,6},{0,7},{9,8},{10,9},{11,1... | collective-permute-start | bytes 393224 | tf_op jit(solution)/shard_map/ppermute | solution.py:360
  106.9 4.5 %project.3 = (f32[512,256]{1,0:T(8,128)}, bf16[512,256]{1,0:T(8,128)(2,1)}) custom-call(s32[1]{0:T(128)} %bitcast.side_ref, bf16[512,256]{1,0:T(8,128)(2,1)} %get-tuple-element.30.refs_0_, bf16[512,256]{1,0:T(8,128)(2,1)} %copy-done.9, bf16[512,256]{1,0:T(8,128)(2,1)} %collective-permute-done.3.refs_2_, bf16[512,256]{1,0:T(8,128)(2,1)} %collective-permute-done.4.refs_3_, ...), custom_call_target="tpu_custom_call" | custom-call | flops 4000000000 | bytes 4000000 | tf_op jit(solution)/shard_map/project/pallas_call | solution.py:384
  111.5 0.8 collective-permute-start.8
  112.2 0.6 collective-permute-done.23.refs_4_
  112.9 0.0 collective-permute-done.24.refs_5_
  112.9 0.6 copy-done.17
  113.5 4.4 %project.5 = (f32[512,256]{1,0:T(8,128)}, bf16[512,256]{1,0:T(8,128)(2,1)}) custom-call(s32[1]{0:T(128)} %bitcast.side_ref, bf16[512,256]{1,0:T(8,128)(2,1)} %gate.3.refs_0_, bf16[512,256]{1,0:T(8,128)(2,1)} %copy-done.13, bf16[512,256]{1,0:T(8,128)(2,1)} %collective-permute-done.18.refs_2_, bf16[512,256]{1,0:T(8,128)(2,1)} %copy-done.6, ...), custom_call_target="tpu_custom_call" | custom-call | flops 4000000000 | bytes 4000000 | tf_op jit(solution)/shard_map/project/pallas_call | solution.py:384
  118.0 0.0 copy-start.1
  118.0 0.8 collective-permute-start.25
  118.8 0.0 collective-permute-done.15.refs_5_
  118.8 0.0 collective-permute-done.12.refs_4_
  118.8 4.4 %project.4 = (f32[512,256]{1,0:T(8,128)}, bf16[512,256]{1,0:T(8,128)(2,1)}) custom-call(s32[1]{0:T(128)} %bitcast.side_ref, bf16[512,256]{1,0:T(8,128)(2,1)} %get-tuple-element.37.refs_0_, bf16[512,256]{1,0:T(8,128)(2,1)} %copy-done.8, bf16[512,256]{1,0:T(8,128)(2,1)} %copy-done.10, bf16[512,256]{1,0:T(8,128)(2,1)} %collective-permute-done.11.refs_3_, ...), custom_call_target="tpu_custom_call" | custom-call | flops 4000000000 | bytes 4000000 | tf_op jit(solution)/shard_map/project/pallas_call | solution.py:384
  123.2 1.4 collective-permute-start.16
  124.6 0.1 add_convert_fusion.2
  124.7 2.2 %collective-permute-done.25 = bf16[512,256]{1,0:T(8,128)(2,1)S(1)} collective-permute-done((bf16[512,256]{1,0:T(8,128)(2,1)}, bf16[512,256]{1,0:T(8,128)(2,1)S(1)}, u32[]{:S(2)}, u32[]{:S(2)}) %collective-permute-start.25) | collective-permute-done | bytes 262176 | tf_op jit(solution)/shard_map/ppermute | solution.py:398
  126.8 0.1 add_convert_fusion
  126.9 4.9 %collective-permute-done.16 = bf16[512,256]{1,0:T(8,128)(2,1)S(1)} collective-permute-done((bf16[512,256]{1,0:T(8,128)(2,1)}, bf16[512,256]{1,0:T(8,128)(2,1)S(1)}, u32[]{:S(2)}, u32[]{:S(2)}) %collective-permute-start.16) | collective-permute-done | bytes 262176 | tf_op jit(solution)/shard_map/ppermute | solution.py:398
  131.8 0.1 add_convert_fusion.1
  131.9 0.9 pad_maximum_fusion
  (41 shorter events, 0.1 us)
Async XLA Ops:
  6.5 100.4 %all-gather.3.cloned.1.call-start = ((), (), s32[]{:S(2)}) async-start(), calls=%async_computation.1 | async-start | bytes 2228224 | tf_op jit(solution)/shard_map/all_gather | solution.py:301
  6.5 14.6 %collective-permute-start = (bf16[256,256]{1,0:T(8,128)(2,1)}, bf16[256,256]{1,0:T(8,128)(2,1)S(1)}, u32[]{:S(2)}, u32[]{:S(2)}) collective-permute-start(bf16[256,256]{1,0:T(8,128)(2,1)} %param.11), channel_id=1, source_target_pairs={{0,0},{1,16},{2,32},{3,48},{4,64},{5,80},{6,96},{7,112},{8,8},{9,2... | collective-permute-start | bytes 393224 | tf_op jit(solution)/shard_map/ppermute | solution.py:261
  21.1 0.7 copy-start.4
  21.8 17.8 %all-to-all-start = ((bf16[16,48,256]{2,1,0:T(8,128)(2,1)}), bf16[16,48,256]{2,1,0:T(8,128)(2,1)S(1)}, u32[]{:S(2)}, u32[]{:S(2)}) async-start(bf16[16,48,256]{2,1,0:T(8,128)(2,1)} %get-tuple-element.29), calls=%async_computation | async-start | bytes 786432 | tf_op jit(solution)/shard_map/all_to_all | solution.py:302
  39.7 0.7 copy-start.3
  46.8 9.6 %collective-permute-start.2 = (bf16[512,256]{1,0:T(8,128)(2,1)}, bf16[512,256]{1,0:T(8,128)(2,1)S(1)}, u32[]{:S(2)}, u32[]{:S(2)}) collective-permute-start(bf16[512,256]{1,0:T(8,128)(2,1)} %get-tuple-element.30.refs_0_), channel_id=1, source_target_pairs={{1,0},{2,1},{3,2},{4,3},{5,4},{6,5},{7,6},{0,7},{9,8},{10,9},{11,1... | collective-permute-start | bytes 786440 | tf_op jit(solution)/shard_map/ppermute | solution.py:360
  49.3 10.5 %collective-permute-start.1 = (bf16[512,256]{1,0:T(8,128)(2,1)}, bf16[512,256]{1,0:T(8,128)(2,1)S(1)}, u32[]{:S(2)}, u32[]{:S(2)}) collective-permute-start(bf16[512,256]{1,0:T(8,128)(2,1)} %get-tuple-element.30.refs_0_), channel_id=1, source_target_pairs={{0,1},{1,2},{2,3},{3,4},{4,5},{5,6},{6,7},{7,0},{8,9},{9,10},{10,1... | collective-permute-start | bytes 786440 | tf_op jit(solution)/shard_map/ppermute | solution.py:358
  49.3 16.1 %collective-permute-start.13 = (bf16[512,256]{1,0:T(8,128)(2,1)}, bf16[512,256]{1,0:T(8,128)(2,1)S(1)}, u32[]{:S(2)}, u32[]{:S(2)}) collective-permute-start(bf16[512,256]{1,0:T(8,128)(2,1)} %get-tuple-element.37.refs_0_), channel_id=1, source_target_pairs={{0,1},{1,2},{2,3},{3,4},{4,5},{5,6},{6,7},{7,0},{8,9},{9,10},{10,1... | collective-permute-start | bytes 786440 | tf_op jit(solution)/shard_map/ppermute | solution.py:358
  50.8 14.7 %collective-permute-start.9 = (bf16[512,256]{1,0:T(8,128)(2,1)}, bf16[512,256]{1,0:T(8,128)(2,1)S(1)}, u32[]{:S(2)}, u32[]{:S(2)}) collective-permute-start(bf16[512,256]{1,0:T(8,128)(2,1)} %get-tuple-element.37.refs_0_), channel_id=1, source_target_pairs={{1,0},{2,1},{3,2},{4,3},{5,4},{6,5},{7,6},{0,7},{9,8},{10,9},{11,1... | collective-permute-start | bytes 786440 | tf_op jit(solution)/shard_map/ppermute | solution.py:360
  56.4 50.6 %copy-start.9 = (bf16[512,256]{1,0:T(8,128)(2,1)}, bf16[512,256]{1,0:T(8,128)(2,1)S(1)}, u32[]{:S(2)}) copy-start(bf16[512,256]{1,0:T(8,128)(2,1)S(1)} %collective-permute-done.2.refs_1_) | copy-start | bytes 786436
  59.9 47.1 %copy-start.11 = (bf16[512,256]{1,0:T(8,128)(2,1)}, bf16[512,256]{1,0:T(8,128)(2,1)S(1)}, u32[]{:S(2)}) copy-start(bf16[512,256]{1,0:T(8,128)(2,1)S(1)} %collective-permute-done.1.refs_7_) | copy-start | bytes 786436
  59.9 11.2 %collective-permute-start.20 = (bf16[512,256]{1,0:T(8,128)(2,1)}, bf16[512,256]{1,0:T(8,128)(2,1)S(1)}, u32[]{:S(2)}, u32[]{:S(2)}) collective-permute-start(bf16[512,256]{1,0:T(8,128)(2,1)} %gate.3.refs_0_), channel_id=1, source_target_pairs={{0,1},{1,2},{2,3},{3,4},{4,5},{5,6},{6,7},{7,0},{8,9},{9,10},{10,1... | collective-permute-start | bytes 786440 | tf_op jit(solution)/shard_map/ppermute | solution.py:358
  59.9 11.2 %collective-permute-start.17 = (bf16[512,256]{1,0:T(8,128)(2,1)}, bf16[512,256]{1,0:T(8,128)(2,1)S(1)}, u32[]{:S(2)}, u32[]{:S(2)}) collective-permute-start(bf16[512,256]{1,0:T(8,128)(2,1)} %gate.3.refs_0_), channel_id=1, source_target_pairs={{1,0},{2,1},{3,2},{4,3},{5,4},{6,5},{7,6},{0,7},{9,8},{10,9},{11,1... | collective-permute-start | bytes 786440 | tf_op jit(solution)/shard_map/ppermute | solution.py:360
  63.1 12.6 %collective-permute-start.3 = (bf16[512,256]{1,0:T(8,128)(2,1)S(1)}, bf16[512,256]{1,0:T(8,128)(2,1)}, u32[]{:S(2)}, u32[]{:S(2)}) collective-permute-start(bf16[512,256]{1,0:T(8,128)(2,1)S(1)} %collective-permute-done.2.refs_1_), channel_id=1, source_target_pairs={{1,0},{2,1},{3,2},{4,3},{5,4},{6,5},{7,6},{0,7},{9,8},{10,9},{11,1... | collective-permute-start | bytes 786440 | tf_op jit(solution)/shard_map/ppermute | solution.py:360
  65.5 45.9 %copy-start.7 = (bf16[512,256]{1,0:T(8,128)(2,1)}, bf16[512,256]{1,0:T(8,128)(2,1)S(1)}, u32[]{:S(2)}) copy-start(bf16[512,256]{1,0:T(8,128)(2,1)S(1)} %collective-permute-done.13.refs_7_) | copy-start | bytes 786436
  65.5 11.2 %collective-permute-start.5 = (bf16[512,256]{1,0:T(8,128)(2,1)S(1)}, bf16[512,256]{1,0:T(8,128)(2,1)S(1)}, u32[]{:S(2)}, u32[]{:S(2)}) collective-permute-start(bf16[512,256]{1,0:T(8,128)(2,1)S(1)} %collective-permute-done.1.refs_7_), channel_id=1, source_target_pairs={{0,1},{1,2},{2,3},{3,4},{4,5},{5,6},{6,7},{7,0},{8,9},{9,10},{10,1... | collective-permute-start | bytes 786440 | tf_op jit(solution)/shard_map/ppermute | solution.py:358
  65.5 45.9 %copy-start.8 = (bf16[512,256]{1,0:T(8,128)(2,1)}, bf16[512,256]{1,0:T(8,128)(2,1)S(1)}, u32[]{:S(2)}) copy-start(bf16[512,256]{1,0:T(8,128)(2,1)S(1)} %collective-permute-done.9.refs_1_) | copy-start | bytes 786436
  65.5 15.8 %collective-permute-start.10 = (bf16[512,256]{1,0:T(8,128)(2,1)S(1)}, bf16[512,256]{1,0:T(8,128)(2,1)S(1)}, u32[]{:S(2)}, u32[]{:S(2)}) collective-permute-start(bf16[512,256]{1,0:T(8,128)(2,1)S(1)} %collective-permute-done.9.refs_1_), channel_id=1, source_target_pairs={{1,0},{2,1},{3,2},{4,3},{5,4},{6,5},{7,6},{0,7},{9,8},{10,9},{11,1... | collective-permute-start | bytes 786440 | tf_op jit(solution)/shard_map/ppermute | solution.py:360
  71.1 40.3 %copy-start.12 = (bf16[512,256]{1,0:T(8,128)(2,1)}, bf16[512,256]{1,0:T(8,128)(2,1)S(1)}, u32[]{:S(2)}) copy-start(bf16[512,256]{1,0:T(8,128)(2,1)S(1)} %collective-permute-done.20.refs_8_) | copy-start | bytes 786436
  71.1 13.9 %collective-permute-start.21 = (bf16[512,256]{1,0:T(8,128)(2,1)S(1)}, bf16[512,256]{1,0:T(8,128)(2,1)S(1)}, u32[]{:S(2)}, u32[]{:S(2)}) collective-permute-start(bf16[512,256]{1,0:T(8,128)(2,1)S(1)} %collective-permute-done.20.refs_8_), channel_id=1, source_target_pairs={{0,1},{1,2},{2,3},{3,4},{4,5},{5,6},{6,7},{7,0},{8,9},{9,10},{10,1... | collective-permute-start | bytes 786440 | tf_op jit(solution)/shard_map/ppermute | solution.py:358
  71.1 40.3 %copy-start.13 = (bf16[512,256]{1,0:T(8,128)(2,1)}, bf16[512,256]{1,0:T(8,128)(2,1)S(1)}, u32[]{:S(2)}) copy-start(bf16[512,256]{1,0:T(8,128)(2,1)S(1)} %collective-permute-done.17.refs_1_) | copy-start | bytes 786436
  71.1 15.8 %collective-permute-start.18 = (bf16[512,256]{1,0:T(8,128)(2,1)S(1)}, bf16[512,256]{1,0:T(8,128)(2,1)}, u32[]{:S(2)}, u32[]{:S(2)}) collective-permute-start(bf16[512,256]{1,0:T(8,128)(2,1)S(1)} %collective-permute-done.17.refs_1_), channel_id=1, source_target_pairs={{1,0},{2,1},{3,2},{4,3},{5,4},{6,5},{7,6},{0,7},{9,8},{10,9},{11,1... | collective-permute-start | bytes 786440 | tf_op jit(solution)/shard_map/ppermute | solution.py:360
  75.7 15.0 %collective-permute-start.14 = (bf16[512,256]{1,0:T(8,128)(2,1)S(1)}, bf16[512,256]{1,0:T(8,128)(2,1)S(1)}, u32[]{:S(2)}, u32[]{:S(2)}) collective-permute-start(bf16[512,256]{1,0:T(8,128)(2,1)S(1)} %collective-permute-done.13.refs_7_), channel_id=1, source_target_pairs={{0,1},{1,2},{2,3},{3,4},{4,5},{5,6},{6,7},{7,0},{8,9},{9,10},{10,1... | collective-permute-start | bytes 786440 | tf_op jit(solution)/shard_map/ppermute | solution.py:358
  76.7 14.0 %copy-start.16 = (bf16[512,256]{1,0:T(8,128)(2,1)}, bf16[512,256]{1,0:T(8,128)(2,1)S(1)}, u32[]{:S(2)}) copy-start(bf16[512,256]{1,0:T(8,128)(2,1)S(1)} %collective-permute-done.5.refs_6_) | copy-start | bytes 786436
  76.7 17.0 %collective-permute-start.6 = (bf16[512,256]{1,0:T(8,128)(2,1)S(1)}, bf16[512,256]{1,0:T(8,128)(2,1)}, u32[]{:S(2)}, u32[]{:S(2)}) collective-permute-start(bf16[512,256]{1,0:T(8,128)(2,1)S(1)} %collective-permute-done.5.refs_6_), channel_id=1, source_target_pairs={{0,1},{1,2},{2,3},{3,4},{4,5},{5,6},{6,7},{7,0},{8,9},{9,10},{10,1... | collective-permute-start | bytes 786440 | tf_op jit(solution)/shard_map/ppermute | solution.py:358
  81.3 30.1 %copy-start.10 = (bf16[512,256]{1,0:T(8,128)(2,1)}, bf16[512,256]{1,0:T(8,128)(2,1)S(1)}, u32[]{:S(2)}) copy-start(bf16[512,256]{1,0:T(8,128)(2,1)S(1)} %collective-permute-done.10.refs_2_) | copy-start | bytes 786436
  81.3 12.4 %collective-permute-start.11 = (bf16[512,256]{1,0:T(8,128)(2,1)S(1)}, bf16[512,256]{1,0:T(8,128)(2,1)}, u32[]{:S(2)}, u32[]{:S(2)}) collective-permute-start(bf16[512,256]{1,0:T(8,128)(2,1)S(1)} %collective-permute-done.10.refs_2_), channel_id=1, source_target_pairs={{1,0},{2,1},{3,2},{4,3},{5,4},{6,5},{7,6},{0,7},{9,8},{10,9},{11,1... | collective-permute-start | bytes 786440 | tf_op jit(solution)/shard_map/ppermute | solution.py:360
  85.0 26.4 %copy-start.15 = (bf16[512,256]{1,0:T(8,128)(2,1)}, bf16[512,256]{1,0:T(8,128)(2,1)S(1)}, u32[]{:S(2)}) copy-start(bf16[512,256]{1,0:T(8,128)(2,1)S(1)} %collective-permute-done.21.refs_7_) | copy-start | bytes 786436
  85.0 14.2 %collective-permute-start.22 = (bf16[512,256]{1,0:T(8,128)(2,1)S(1)}, bf16[512,256]{1,0:T(8,128)(2,1)S(1)}, u32[]{:S(2)}, u32[]{:S(2)}) collective-permute-start(bf16[512,256]{1,0:T(8,128)(2,1)S(1)} %collective-permute-done.21.refs_7_), channel_id=1, source_target_pairs={{0,1},{1,2},{2,3},{3,4},{4,5},{5,6},{6,7},{7,0},{8,9},{9,10},{10,1... | collective-permute-start | bytes 786440 | tf_op jit(solution)/shard_map/ppermute | solution.py:358
  86.9 13.9 %collective-permute-start.19 = (bf16[512,256]{1,0:T(8,128)(2,1)}, bf16[512,256]{1,0:T(8,128)(2,1)S(1)}, u32[]{:S(2)}, u32[]{:S(2)}) collective-permute-start(bf16[512,256]{1,0:T(8,128)(2,1)} %collective-permute-done.18.refs_2_), channel_id=1, source_target_pairs={{1,0},{2,1},{3,2},{4,3},{5,4},{6,5},{7,6},{0,7},{9,8},{10,9},{11,1... | collective-permute-start | bytes 786440 | tf_op jit(solution)/shard_map/ppermute | solution.py:360
  90.7 20.7 %copy-start.14 = (bf16[512,256]{1,0:T(8,128)(2,1)}, bf16[512,256]{1,0:T(8,128)(2,1)S(1)}, u32[]{:S(2)}) copy-start(bf16[512,256]{1,0:T(8,128)(2,1)S(1)} %collective-permute-done.14.refs_6_) | copy-start | bytes 786436
  90.7 12.5 %collective-permute-start.4 = (bf16[512,256]{1,0:T(8,128)(2,1)}, bf16[512,256]{1,0:T(8,128)(2,1)}, u32[]{:S(2)}, u32[]{:S(2)}) collective-permute-start(bf16[512,256]{1,0:T(8,128)(2,1)} %collective-permute-done.3.refs_2_), channel_id=1, source_target_pairs={{1,0},{2,1},{3,2},{4,3},{5,4},{6,5},{7,6},{0,7},{9,8},{10,9},{11,1... | collective-permute-start | bytes 786440 | tf_op jit(solution)/shard_map/ppermute | solution.py:360
  93.7 13.3 %collective-permute-start.7 = (bf16[512,256]{1,0:T(8,128)(2,1)}, bf16[512,256]{1,0:T(8,128)(2,1)}, u32[]{:S(2)}, u32[]{:S(2)}) collective-permute-start(bf16[512,256]{1,0:T(8,128)(2,1)} %collective-permute-done.6.refs_5_), channel_id=1, source_target_pairs={{0,1},{1,2},{2,3},{3,4},{4,5},{5,6},{6,7},{7,0},{8,9},{9,10},{10,1... | collective-permute-start | bytes 786440 | tf_op jit(solution)/shard_map/ppermute | solution.py:358
  93.7 25.1 %collective-permute-start.15 = (bf16[512,256]{1,0:T(8,128)(2,1)S(1)}, bf16[512,256]{1,0:T(8,128)(2,1)}, u32[]{:S(2)}, u32[]{:S(2)}) collective-permute-start(bf16[512,256]{1,0:T(8,128)(2,1)S(1)} %collective-permute-done.14.refs_6_), channel_id=1, source_target_pairs={{0,1},{1,2},{2,3},{3,4},{4,5},{5,6},{6,7},{7,0},{8,9},{9,10},{10,1... | collective-permute-start | bytes 786440 | tf_op jit(solution)/shard_map/ppermute | solution.py:358
  99.2 12.3 %copy-start.5 = (bf16[512,256]{1,0:T(8,128)(2,1)}, bf16[512,256]{1,0:T(8,128)(2,1)S(1)}, u32[]{:S(2)}) copy-start(bf16[512,256]{1,0:T(8,128)(2,1)S(1)} %collective-permute-done.22.refs_6_) | copy-start | bytes 786436
  99.2 19.6 %collective-permute-start.12 = (bf16[512,256]{1,0:T(8,128)(2,1)}, bf16[512,256]{1,0:T(8,128)(2,1)}, u32[]{:S(2)}, u32[]{:S(2)}) collective-permute-start(bf16[512,256]{1,0:T(8,128)(2,1)} %collective-permute-done.11.refs_3_), channel_id=1, source_target_pairs={{1,0},{2,1},{3,2},{4,3},{5,4},{6,5},{7,6},{0,7},{9,8},{10,9},{11,1... | collective-permute-start | bytes 786440 | tf_op jit(solution)/shard_map/ppermute | solution.py:360
  100.8 10.7 %copy-start.6 = (bf16[512,256]{1,0:T(8,128)(2,1)}, bf16[512,256]{1,0:T(8,128)(2,1)S(1)}, u32[]{:S(2)}) copy-start(bf16[512,256]{1,0:T(8,128)(2,1)S(1)} %collective-permute-done.19.refs_3_) | copy-start | bytes 786436
  100.8 12.0 %collective-permute-start.23 = (bf16[256,256]{1,0:T(8,128)(2,1)S(1)}, bf16[256,256]{1,0:T(8,128)(2,1)S(1)}, u32[]{:S(2)}, u32[]{:S(2)}) collective-permute-start(bf16[256,256]{1,0:T(8,128)(2,1)S(1)} %slice.8), channel_id=1, source_target_pairs={{0,1},{1,2},{2,3},{3,4},{4,5},{5,6},{6,7},{7,0},{8,9},{9,10},{10,1... | collective-permute-start | bytes 393224 | tf_op jit(solution)/shard_map/ppermute | solution.py:358
  103.2 9.6 %collective-permute-start.24 = (bf16[256,256]{1,0:T(8,128)(2,1)S(1)}, bf16[256,256]{1,0:T(8,128)(2,1)}, u32[]{:S(2)}, u32[]{:S(2)}) collective-permute-start(bf16[256,256]{1,0:T(8,128)(2,1)S(1)} %slice.9), channel_id=1, source_target_pairs={{1,0},{2,1},{3,2},{4,3},{5,4},{6,5},{7,6},{0,7},{9,8},{10,9},{11,1... | collective-permute-start | bytes 393224 | tf_op jit(solution)/shard_map/ppermute | solution.py:360
  111.5 13.1 %collective-permute-start.8 = (bf16[512,256]{1,0:T(8,128)(2,1)}, bf16[512,256]{1,0:T(8,128)(2,1)S(1)}, u32[]{:S(2)}, u32[]{:S(2)}) collective-permute-start(bf16[512,256]{1,0:T(8,128)(2,1)} %get-tuple-element.36), channel_id=1, source_target_pairs={{0,8},{1,9},{2,10},{3,11},{4,12},{5,13},{6,14},{7,15},{8,0},{9,1},... | collective-permute-start | bytes 786440 | tf_op jit(solution)/shard_map/ppermute | solution.py:398
  112.9 0.7 copy-start.17
  118.0 6.7 %copy-start = (f32[512,256]{1,0:T(8,128)S(1)}, f32[512,256]{1,0:T(8,128)}, u32[]{:S(2)}) copy-start(f32[512,256]{1,0:T(8,128)} %get-tuple-element.35) | copy-start | bytes 1572868
  118.0 8.9 %copy-start.1 = (f32[512,256]{1,0:T(8,128)S(1)}, f32[512,256]{1,0:T(8,128)}, u32[]{:S(2)}) copy-start(f32[512,256]{1,0:T(8,128)} %get-tuple-element.41) | copy-start | bytes 1572868
  118.0 8.9 %collective-permute-start.25 = (bf16[512,256]{1,0:T(8,128)(2,1)}, bf16[512,256]{1,0:T(8,128)(2,1)S(1)}, u32[]{:S(2)}, u32[]{:S(2)}) collective-permute-start(bf16[512,256]{1,0:T(8,128)(2,1)} %get-tuple-element.42), channel_id=1, source_target_pairs={{0,8},{1,9},{2,10},{3,11},{4,12},{5,13},{6,14},{7,15},{8,0},{9,1},... | collective-permute-start | bytes 786440 | tf_op jit(solution)/shard_map/ppermute | solution.py:398
  123.2 8.6 %copy-start.2 = (f32[512,256]{1,0:T(8,128)S(1)}, f32[512,256]{1,0:T(8,128)}, u32[]{:S(2)}) copy-start(f32[512,256]{1,0:T(8,128)} %get-tuple-element.38) | copy-start | bytes 1572868
  123.2 8.6 %collective-permute-start.16 = (bf16[512,256]{1,0:T(8,128)(2,1)}, bf16[512,256]{1,0:T(8,128)(2,1)S(1)}, u32[]{:S(2)}, u32[]{:S(2)}) collective-permute-start(bf16[512,256]{1,0:T(8,128)(2,1)} %get-tuple-element.39), channel_id=1, source_target_pairs={{0,8},{1,9},{2,10},{3,11},{4,12},{5,13},{6,14},{7,15},{8,0},{9,1},... | collective-permute-start | bytes 786440 | tf_op jit(solution)/shard_map/ppermute | solution.py:398
Sparse Core Ops, SparseCore 0:
  21.9 57.0 all-gather.2

commit v3 on v2

--- a/solution.py
+++ b/solution.py
@@ -12,7 +12,6 @@
 SEGS = 8
 CHUNKS = ((0, 512), (512, 512), (1024, 512))
 ROWS = 48
-TILE = 256
 CTX = 16
 CH = 16
 RING = 8
@@ -21,24 +20,25 @@
 MIB = 1024 * 1024
 
 
-PLAN = [
-    ("hop", 0, 1),
-    ("hop", 1, 1),
-    ("later", 2, 0, 1),
-    ("hop", 0, 2),
-    ("hop", 2, 1),
-    ("hop", 1, 2),
-    ("hop", 0, 3),
-    ("hop", 2, 2),
-    ("hop", 1, 3),
-    ("hop", 0, 4, "up"),
-    ("hop", 2, 3),
-    ("hop", 1, 4, "down"),
-    ("hop", 2, 4),
+PLAN = (
+    ("weights", 1, 0, "u"),
+    ("hop", 0, 1, "ud"),
+    ("hop", 1, 1, "ud"),
+    ("hop", 0, 2, "ud"),
+    ("wait", 2, 1, 0, 1),
+    ("hop", 2, 1, "ud"),
+    ("hop", 1, 2, "ud"),
+    ("hop", 0, 3, "ud"),
+    ("hop", 2, 2, "ud"),
+    ("hop", 1, 3, "ud"),
+    ("hop", 0, 4, "u"),
+    ("hop", 2, 3, "ud"),
+    ("hop", 1, 4, "d"),
+    ("hop", 2, 4, "ud"),
     ("project", 0),
     ("project", 1),
     ("project", 2),
-]
+)
 
 
 def row_ids():
@@ -233,14 +233,14 @@
         out_refs[k][...] = gx[pl.ds(base, chunk), :].astype(BF16)
 
 
-def project_kernel(side_ref, *refs):
+def project_kernel(place_ref, *refs):
     w_ref, own_ref, other_ref = refs[-3:]
     values = [r[...] for r in refs[:-3]]
     if len(values) == 9:
-        far = jnp.where(pl.program_id(0) < pl.num_programs(0) // 2, values[4], values[5])
+        far = jnp.where(pl.program_id(0) == 0, values[4], values[5])
         values = values[:4] + [far] + values[6:]
     rows = jnp.concatenate(values, axis=1)
-    side = side_ref[0]
+    side = place_ref[0]
     own_ref[...] = jnp.dot(rows, w_ref[side], preferred_element_type=F32)
     other_ref[...] = jnp.dot(rows, w_ref[1 - side], preferred_element_type=F32).astype(BF16)
 
@@ -258,7 +258,6 @@
                 for z in range(RING):
                     there = h * RING + (z - a) % RING
                     swap.append((((h * RING + a) * 2 + y) * RING + z, (there * 2 + y) * RING + a))
-    w_block = lax.ppermute(w_out, ("ctx", "ch"), swap)
 
     skip_row = skip[None, :]
     me = jnp.reshape(ctx, (1,)).astype(jnp.int32)
@@ -297,8 +296,8 @@
         cost_estimate=cost,
         name="states",
     )(streams, streams, streams, taps, decay.T, residues.T)
-    w_block, send = lax.optimization_barrier((w_block, send))
-    w_all = lax.all_gather(w_block, "ctx").reshape(2, RING * chans, w_out.shape[1])
+    w_block, modes = lax.optimization_barrier((w_out, modes))
+    w_block = lax.ppermute(w_block, ("ctx", "ch"), swap)
     recv = lax.all_to_all(send, "ctx", 0, 0)
 
     def gate(group, entry):
@@ -339,52 +338,48 @@
     up = [(y * RING + z, y * RING + (z + 1) % RING) for y in range(2) for z in range(RING)]
     down = [(d, s) for s, d in up]
     across = [(i, (i + RING) % CH) for i in range(CH)]
-    side = jnp.reshape(ch // RING, (1,)).astype(jnp.int32)
+    place = jnp.reshape(ch // RING, (1,)).astype(jnp.int32)
 
     *gated, entry = gate((0, 1), None)
     gated += gate((2,), entry)
     count = len(CHUNKS)
-    low = [[g] for g in gated]
-    high = [[g] for g in gated]
-
-    def hop(c, s, *ways):
-        a, b = low[c][-1], high[c][-1]
-        if len(ways) == 0:
-            ways = ("up", "down")
-            if s == RING // 2:
-                half = a.shape[0] // 2
-                a, b = a[:half], b[half:]
-        if "up" in ways:
-            low[c].append(lax.ppermute(a, "ch", up))
-        if "down" in ways:
-            high[c].append(lax.ppermute(b, "ch", down))
-
-    def later(d, c, s):
-        low[c][s], high[c][s], g = lax.optimization_barrier((low[c][s], high[c][s], low[d][0]))
-        low[d][0], high[d][0] = g, g
-
-    def after(c, d):
-        low[c][0], low[d][3], high[d][3] = lax.optimization_barrier((low[c][0], low[d][3], high[d][3]))
-
-    tile = pl.BlockSpec((TILE, chans), lambda g: (g, 0))
+    arrived = {(c, 0, way): g for c, g in enumerate(gated) for way in "ud"}
+
+    def hop(c, s, ways):
+        for way in ways:
+            block = arrived[c, s - 1, way]
+            if s == RING // 2 and len(ways) == 2:
+                half = block.shape[0] // 2
+                block = block[half:] if way == "u" else block[:half]
+            arrived[c, s, way] = lax.ppermute(block, "ch", up if way == "u" else down)
+
+    def wait(c, s, d, t):
+        for way in "ud":
+            if (d, t, way) in arrived and (c, s - 1, way) in arrived:
+                pair = arrived[d, t, way], arrived[c, s - 1, way]
+                arrived[d, t, way], arrived[c, s - 1, way] = lax.optimization_barrier(pair)
+
     own = [None] * count
     theirs = [None] * count
 
+    def weights(c, s, way):
+        nonlocal w_all
+        w, arrived[c, s, way] = lax.optimization_barrier((w_block, arrived[c, s, way]))
+        w_all = lax.all_to_all(jnp.broadcast_to(w, (CTX, *w.shape)), "ctx", 0, 0)
+        w_all = w_all.reshape(2, RING * chans, w.shape[1])
+
     def project(c):
         chunk = CHUNKS[c][1]
-        far = [*low[c][4:], *high[c][4:]]
-        parts = [low[c][0], *high[c][1:4], *far, *low[c][3:0:-1]]
-        count = chunk // TILE
-        far_specs = [tile]
-        if len(far) == 2:
-            far_specs = [
-                pl.BlockSpec((TILE, chans), lambda g: (jnp.minimum(g, count // 2 - 1), 0)),
-                pl.BlockSpec((TILE, chans), lambda g: (jnp.maximum(g - count // 2, 0), 0)),
-            ]
+        rows = chunk // 2
+        get = lambda way, *hops: [arrived[c, s, way] for s in hops if (c, s, way) in arrived]
+        parts = [gated[c], *get("d", 1, 2, 3, 4), *get("u", 4, 3, 2, 1)]
+        far = len(parts) - 7
+        tile = pl.BlockSpec((rows, chans), lambda g: (g, 0))
+        whole = pl.BlockSpec((rows, chans), lambda g: (0, 0))
         mine, other = pl.pallas_call(
             project_kernel,
-            grid=(count,),
-            in_specs=[smem] + [tile] * 4 + far_specs + [tile] * 3 + [pl.BlockSpec(w_all.shape, lambda g: (0, 0, 0))],
+            grid=(2,),
+            in_specs=[smem] + [tile] * 4 + [[tile], [whole] * 2][far - 1] + [tile] * 3 + [pl.BlockSpec(w_all.shape, lambda g: (0,) * w_all.ndim)],
             out_specs=[tile] * 2,
             out_shape=[
                 jax.ShapeDtypeStruct((chunk, chans), F32),
@@ -393,11 +388,21 @@
             compiler_params=params(60),
             cost_estimate=cost,
             name="project",
-        )(side, *parts, w_all)
-        own[c] = mine
-        theirs[c] = lax.ppermute(other, "ch", across)
-
-    steps = {"hop": hop, "later": later, "after": after, "project": project}
+        )(place, *parts, w_all)
+        return mine, other
+
+    def send(c, mine, other):
+        own[c], theirs[c] = mine, lax.ppermute(other, "ch", across)
+
+    def ahead(k, c, s):
+        mine, other = project(k)
+        block = [arrived[c, s - 1, way] for way in "ud"]
+        other, block = lax.optimization_barrier((other, block))
+        arrived[c, s - 1, "u"], arrived[c, s - 1, "d"] = block
+        send(k, mine, other)
+
+    w_all = None
+    steps = {"weights": weights, "hop": hop, "wait": wait, "ahead": ahead, "project": lambda c: send(c, *project(c))}
     for kind, *rest in PLAN:
         steps[kind](*rest)
 

time: 140 us -> 126 us (0.900)
  between operations: 13.6 us -> 0.23 us
  waiting for transfers between devices: 42.8 us -> 31.8 us
  starting transfers between devices: 50.2 us -> 58.3 us
  local copies, waits for them, and re-layouts: 2.12 us -> 4.4 us
    all_to_all x0 -> x1, starting transfers between devices: none -> 9.18 us  [weights(): w_all = lax.all_to_all(jnp.broadcast_to(w, (CTX, *w.shape)), 'ctx', 0, 0)]
    all_to_all x1, waiting for transfers between devices: 7.85 us -> 1.14 us  [local(): recv = lax.all_to_all(send, 'ctx', 0, 0)]
    ppermute x26, waiting for transfers between devices: 34.9 us -> 30.6 us  [the longest x22 24.9 us: hop(): arrived[c, s, way] = lax.ppermute(block, 'ch', up if way == 'u' else down)]
    all_to_all x1, starting transfers between devices: 10 us -> 7.48 us  [local(): recv = lax.all_to_all(send, 'ctx', 0, 0)]
    broadcast_in_dim x0 -> x1, local copies, waits for them, and re-layouts: none -> 1.55 us  [weights(): w_all = lax.all_to_all(jnp.broadcast_to(w, (CTX, *w.shape)), 'ctx', 0, 0)]
    ppermute x26, starting transfers between devices: 40.2 us -> 41.7 us  [the longest x22 32 us: hop(): arrived[c, s, way] = lax.ppermute(block, 'ch', up if way == 'u' else down)]
    unnamed x36 -> x40, local copies, waits for them, and re-layouts: 2.1 us -> 2.83 us
  transfers between devices with their start and end apart: 28 -> 28, of which waited for: 15 -> 11; matrix products, arithmetic and copies ran while one was open for 0% -> 0% of each run, Pallas kernels for 21% -> 19%
where the time goes in v3:
time: 126 us
  starting transfers between devices  58.3 us (46%)
  waiting for transfers between devices  31.8 us (25%)
  Pallas kernels  29.8 us (24%)
  local copies, waits for them, and re-layouts  4.4 us (3%)
    ppermute x22, starting transfers between devices, hop(): arrived[c, s, way] = lax.ppermute(block, 'ch', up if way == 'u' else down)  32 us
    ppermute x22, waiting for transfers between devices, hop(): arrived[c, s, way] = lax.ppermute(block, 'ch', up if way == 'u' else down)  24.9 us
    pallas_call x3, Pallas kernels, project(): pl.pallas_call(project_kernel, grid=(2,), in_specs=[smem] + [tile] * 4 +...  13.3 us
    pallas_call x2, Pallas kernels, gate(): pl.pallas_call(functools.partial(gate_kernel, group, tokens), grid=(tiles...  10.2 us
    all_to_all x1, starting transfers between devices, weights(): w_all = lax.all_to_all(jnp.broadcast_to(w, (CTX, *w.shape)), 'ctx', 0, 0)  9.18 us
    all_to_all x1, starting transfers between devices, local(): recv = lax.all_to_all(send, 'ctx', 0, 0)  7.48 us
    ppermute x1, starting transfers between devices, local(): w_block = lax.ppermute(w_block, ('ctx', 'ch'), swap)  6.69 us
    pallas_call x1, Pallas kernels, local(): pl.pallas_call(states_kernel, grid=(tiles,), in_specs=[pl.BlockSpec((1, t...  6.38 us
  transfers between devices with their start and end apart: 28, of which 11 were waited for; matrix products, arithmetic and copies ran while one was open for 0% of the time, Pallas kernels for 19%

profile of v3, /device:TPU:2, one launch (start us, length us, event | category | flops | bytes accessed | tf_op | source)
XLA Modules:
  0.0 125.7 jit_solution(16136968664586620608)
XLA Ops:
  0.0 6.4 %states.1 = (f32[1536,256]{1,0:T(8,128)}, f32[3,16,8,256]{3,2,1,0:T(8,128)}, f32[3,16,256]{2,1,0:T(8,128)}, bf16[16,48,256]{2,1,0:T(8,128)(2,1)}, f32[2,16,256]{2,1,0:T(8,128)}) custom-call(bf16[3,1536,256]{2,1,0:T(8,128)(2,1)} %refs_1_.3, bf16[3,1536,256]{2,1,0:T(8,128)(2,1)} %refs_1_.3, bf16[3,1536,256]{2,1,0:T(8,128)(2,1)} %refs_1_.3, ...), custom_call_target="tpu_custom_call" | custom-call | flops 4000000000 | bytes 4000000 | tf_op jit(solution)/shard_map/states/pallas_call | solution.py:269
  6.4 7.5 %all-to-all-start = ((bf16[16,48,256]{2,1,0:T(8,128)(2,1)}), bf16[16,48,256]{2,1,0:T(8,128)(2,1)S(1)}, u32[]{:S(2)}, u32[]{:S(2)}) async-start(bf16[16,48,256]{2,1,0:T(8,128)(2,1)} %get-tuple-element.32), calls=%async_computation | async-start | bytes 786432 | tf_op jit(solution)/shard_map/all_to_all | solution.py:301
  13.9 6.7 %collective-permute-start.7 = (bf16[256,256]{1,0:T(8,128)(2,1)S(1)}, bf16[256,256]{1,0:T(8,128)(2,1)S(1)}, u32[]{:S(2)}, u32[]{:S(2)}) collective-permute-start(bf16[256,256]{1,0:T(8,128)(2,1)S(1)} %copy-done.18), channel_id=1, source_target_pairs={{0,0},{1,16},{2,32},{3,48},{4,64},{5,80},{6,96},{7,112},{8,8},{9,2... | collective-permute-start | bytes 393224 | tf_op jit(solution)/shard_map/ppermute | solution.py:300
  20.6 1.1 all-to-all-done.refs_8_
  21.7 0.8 copy-done.4
  22.5 6.4 %gate.2 = (bf16[512,256]{1,0:T(8,128)(2,1)}, bf16[512,256]{1,0:T(8,128)(2,1)}, f32[1,16,256]{2,1,0:T(8,128)}) custom-call(s32[1]{0:T(128)} %bitcast.1.refs_0_, bf16[3,1536,256]{2,1,0:T(8,128)(2,1)} %refs_1_.3, f32[3,3,256]{2,1,0:T(4,128)} %refs_2_.3, f32[2,16,256]{2,1,0:T(8,128)} %get-tuple-element.28.refs_3_, f32[1,256]{1,0:T(1,128)} %bitcast.11, ...), custom_call_target="tpu_custom_call" | custom-call | flops 4000000000 | bytes 4000000 | tf_op jit(solution)/shard_map/gate/pallas_call | solution.py:326
  28.9 0.0 collective-permute-done.7
  28.9 1.5 %broadcast_in_dim.7 = bf16[16,256,256]{2,1,0:T(8,128)(2,1)} broadcast(bf16[256,256]{1,0:T(8,128)(2,1)S(1)} %collective-permute-done.7), dimensions={1,2} | broadcast | bytes 2228224 | tf_op jit(solution)/shard_map/broadcast_in_dim | solution.py:368
  30.4 9.2 %all-to-all-start.1 = ((bf16[16,256,256]{2,1,0:T(8,128)(2,1)}), bf16[16,256,256]{2,1,0:T(8,128)(2,1)S(1)}, u32[]{:S(2)}, u32[]{:S(2)}) async-start(bf16[16,256,256]{2,1,0:T(8,128)(2,1)} %broadcast_in_dim.7), calls=%async_computation.1 | async-start | bytes 4194304 | tf_op jit(solution)/shard_map/all_to_all | solution.py:368
  39.6 2.2 %collective-permute-start.3 = (bf16[512,256]{1,0:T(8,128)(2,1)S(1)}, bf16[512,256]{1,0:T(8,128)(2,1)S(1)}, u32[]{:S(2)}, u32[]{:S(2)}) collective-permute-start(bf16[512,256]{1,0:T(8,128)(2,1)S(1)} %copy-done.9), channel_id=1, source_target_pairs={{0,1},{1,2},{2,3},{3,4},{4,5},{5,6},{6,7},{7,0},{8,9},{9,10},{10,1... | collective-permute-start | bytes 786440 | tf_op jit(solution)/shard_map/ppermute | solution.py:354
  41.8 3.3 %collective-permute-start = (bf16[512,256]{1,0:T(8,128)(2,1)S(1)}, bf16[512,256]{1,0:T(8,128)(2,1)}, u32[]{:S(2)}, u32[]{:S(2)}) collective-permute-start(bf16[512,256]{1,0:T(8,128)(2,1)S(1)} %copy-done.9), channel_id=1, source_target_pairs={{1,0},{2,1},{3,2},{4,3},{5,4},{6,5},{7,6},{0,7},{9,8},{10,9},{11,1... | collective-permute-start | bytes 786440 | tf_op jit(solution)/shard_map/ppermute | solution.py:354
  45.0 1.9 %collective-permute-start.9 = (bf16[512,256]{1,0:T(8,128)(2,1)S(1)}, bf16[512,256]{1,0:T(8,128)(2,1)S(1)}, u32[]{:S(2)}, u32[]{:S(2)}) collective-permute-start(bf16[512,256]{1,0:T(8,128)(2,1)S(1)} %copy-done.7), channel_id=1, source_target_pairs={{1,0},{2,1},{3,2},{4,3},{5,4},{6,5},{7,6},{0,7},{9,8},{10,9},{11,1... | collective-permute-start | bytes 786440 | tf_op jit(solution)/shard_map/ppermute | solution.py:354
  47.0 0.1 collective-permute-start.13
  47.1 3.8 %gate.3.refs_0_ = bf16[512,256]{1,0:T(8,128)(2,1)} custom-call(bf16[3,1536,256]{2,1,0:T(8,128)(2,1)} %refs_1_.3, bf16[3,1536,256]{2,1,0:T(8,128)(2,1)} %refs_1_.3, f32[3,3,256]{2,1,0:T(4,128)} %refs_2_.3, f32[2,16,256]{2,1,0:T(8,128)} %get-tuple-element.28.refs_3_, f32[1,256]{1,0:T(1,128)} %bitcast.12, f32[1536,256]{1,0:T(8,128)} %get-tuple-element.29.refs_5_, ...), custom_call_target="tpu_custom_call" | custom-call | flops 4000000000 | bytes 4000000 | tf_op jit(solution)/shard_map/gate/pallas_call | solution.py:326
  50.8 1.2 collective-permute-done.3.refs_7_
  52.0 0.0 collective-permute-start.21
  52.0 0.0 collective-permute-done.refs_1_
  52.0 3.5 %collective-permute-start.17 = (bf16[512,256]{1,0:T(8,128)(2,1)}, bf16[512,256]{1,0:T(8,128)(2,1)S(1)}, u32[]{:S(2)}, u32[]{:S(2)}) collective-permute-start(bf16[512,256]{1,0:T(8,128)(2,1)} %gate.3.refs_0_), channel_id=1, source_target_pairs={{1,0},{2,1},{3,2},{4,3},{5,4},{6,5},{7,6},{0,7},{9,8},{10,9},{11,1... | collective-permute-start | bytes 786440 | tf_op jit(solution)/shard_map/ppermute | solution.py:354
  55.5 0.0 collective-permute-start.4
  55.5 2.1 %collective-permute-done.13.refs_7_ = bf16[512,256]{1,0:T(8,128)(2,1)S(1)} collective-permute-done((bf16[512,256]{1,0:T(8,128)(2,1)S(1)}, bf16[512,256]{1,0:T(8,128)(2,1)S(1)}, u32[]{:S(2)}, u32[]{:S(2)}) %collective-permute-start.13) | collective-permute-done | bytes 262176 | tf_op jit(solution)/shard_map/ppermute | solution.py:354
  57.6 2.1 %collective-permute-start.1 = (bf16[512,256]{1,0:T(8,128)(2,1)}, bf16[512,256]{1,0:T(8,128)(2,1)}, u32[]{:S(2)}, u32[]{:S(2)}) collective-permute-start(bf16[512,256]{1,0:T(8,128)(2,1)} %collective-permute-done.refs_1_), channel_id=1, source_target_pairs={{1,0},{2,1},{3,2},{4,3},{5,4},{6,5},{7,6},{0,7},{9,8},{10,9},{11,1... | collective-permute-start | bytes 786440 | tf_op jit(solution)/shard_map/ppermute | solution.py:354
  59.7 0.0 collective-permute-done.9.refs_1_
  59.7 1.3 %collective-permute-start.10 = (bf16[512,256]{1,0:T(8,128)(2,1)S(1)}, bf16[512,256]{1,0:T(8,128)(2,1)S(1)}, u32[]{:S(2)}, u32[]{:S(2)}) collective-permute-start(bf16[512,256]{1,0:T(8,128)(2,1)S(1)} %collective-permute-done.9.refs_1_), channel_id=1, source_target_pairs={{1,0},{2,1},{3,2},{4,3},{5,4},{6,5},{7,6},{0,7},{9,8},{10,9},{11,1... | collective-permute-start | bytes 786440 | tf_op jit(solution)/shard_map/ppermute | solution.py:354
  61.0 2.3 %collective-permute-done.21.refs_8_ = bf16[512,256]{1,0:T(8,128)(2,1)S(1)} collective-permute-done((bf16[512,256]{1,0:T(8,128)(2,1)}, bf16[512,256]{1,0:T(8,128)(2,1)S(1)}, u32[]{:S(2)}, u32[]{:S(2)}) %collective-permute-start.21) | collective-permute-done | bytes 262176 | tf_op jit(solution)/shard_map/ppermute | solution.py:354
  63.3 0.0 collective-permute-start.22
  63.3 0.0 collective-permute-done.17.refs_1_
  63.3 3.3 %collective-permute-start.18 = (bf16[512,256]{1,0:T(8,128)(2,1)S(1)}, bf16[512,256]{1,0:T(8,128)(2,1)}, u32[]{:S(2)}, u32[]{:S(2)}) collective-permute-start(bf16[512,256]{1,0:T(8,128)(2,1)S(1)} %collective-permute-done.17.refs_1_), channel_id=1, source_target_pairs={{1,0},{2,1},{3,2},{4,3},{5,4},{6,5},{7,6},{0,7},{9,8},{10,9},{11,1... | collective-permute-start | bytes 786440 | tf_op jit(solution)/shard_map/ppermute | solution.py:354
  66.6 2.3 %collective-permute-done.4.refs_6_ = bf16[512,256]{1,0:T(8,128)(2,1)S(1)} collective-permute-done((bf16[512,256]{1,0:T(8,128)(2,1)S(1)}, bf16[512,256]{1,0:T(8,128)(2,1)S(1)}, u32[]{:S(2)}, u32[]{:S(2)}) %collective-permute-start.4) | collective-permute-done | bytes 262176 | tf_op jit(solution)/shard_map/ppermute | solution.py:354
  68.9 0.0 collective-permute-start.14
  68.9 0.0 collective-permute-done.1.refs_2_
  68.9 0.1 collective-permute-start.5
  69.0 5.2 %collective-permute-done.10.refs_2_ = bf16[512,256]{1,0:T(8,128)(2,1)S(1)} collective-permute-done((bf16[512,256]{1,0:T(8,128)(2,1)S(1)}, bf16[512,256]{1,0:T(8,128)(2,1)S(1)}, u32[]{:S(2)}, u32[]{:S(2)}) %collective-permute-start.10) | collective-permute-done | bytes 262176 | tf_op jit(solution)/shard_map/ppermute | solution.py:354
  74.2 3.7 %collective-permute-start.11 = (bf16[512,256]{1,0:T(8,128)(2,1)S(1)}, bf16[512,256]{1,0:T(8,128)(2,1)}, u32[]{:S(2)}, u32[]{:S(2)}) collective-permute-start(bf16[512,256]{1,0:T(8,128)(2,1)S(1)} %collective-permute-done.10.refs_2_), channel_id=1, source_target_pairs={{1,0},{2,1},{3,2},{4,3},{5,4},{6,5},{7,6},{0,7},{9,8},{10,9},{11,1... | collective-permute-start | bytes 786440 | tf_op jit(solution)/shard_map/ppermute | solution.py:354
  77.9 0.1 collective-permute-start.23
  78.0 1.8 %collective-permute-done.18.refs_2_ = bf16[512,256]{1,0:T(8,128)(2,1)} collective-permute-done((bf16[512,256]{1,0:T(8,128)(2,1)S(1)}, bf16[512,256]{1,0:T(8,128)(2,1)}, u32[]{:S(2)}, u32[]{:S(2)}) %collective-permute-start.18) | collective-permute-done | bytes 262176 | tf_op jit(solution)/shard_map/ppermute | solution.py:354
  79.8 3.8 %collective-permute-start.19 = (bf16[512,256]{1,0:T(8,128)(2,1)}, bf16[512,256]{1,0:T(8,128)(2,1)S(1)}, u32[]{:S(2)}, u32[]{:S(2)}) collective-permute-start(bf16[512,256]{1,0:T(8,128)(2,1)} %collective-permute-done.18.refs_2_), channel_id=1, source_target_pairs={{1,0},{2,1},{3,2},{4,3},{5,4},{6,5},{7,6},{0,7},{9,8},{10,9},{11,1... | collective-permute-start | bytes 786440 | tf_op jit(solution)/shard_map/ppermute | solution.py:354
  83.6 0.0 collective-permute-done.14.refs_6_
  83.6 0.8 collective-permute-start.2
  84.4 1.4 %collective-permute-done.5.refs_5_ = bf16[512,256]{1,0:T(8,128)(2,1)} collective-permute-done((bf16[512,256]{1,0:T(8,128)(2,1)S(1)}, bf16[512,256]{1,0:T(8,128)(2,1)}, u32[]{:S(2)}, u32[]{:S(2)}) %collective-permute-start.5) | collective-permute-done | bytes 262176 | tf_op jit(solution)/shard_map/ppermute | solution.py:354
  85.9 0.1 collective-permute-start.15
  85.9 5.4 %collective-permute-done.23.refs_6_ = bf16[512,256]{1,0:T(8,128)(2,1)S(1)} collective-permute-done((bf16[512,256]{1,0:T(8,128)(2,1)S(1)}, bf16[512,256]{1,0:T(8,128)(2,1)S(1)}, u32[]{:S(2)}, u32[]{:S(2)}) %collective-permute-start.23) | collective-permute-done | bytes 262176 | tf_op jit(solution)/shard_map/ppermute | solution.py:354
  91.4 2.1 %collective-permute-start.12 = (bf16[512,256]{1,0:T(8,128)(2,1)}, bf16[512,256]{1,0:T(8,128)(2,1)}, u32[]{:S(2)}, u32[]{:S(2)}) collective-permute-start(bf16[512,256]{1,0:T(8,128)(2,1)} %collective-permute-done.11.refs_3_), channel_id=1, source_target_pairs={{1,0},{2,1},{3,2},{4,3},{5,4},{6,5},{7,6},{0,7},{9,8},{10,9},{11,1... | collective-permute-start | bytes 786440 | tf_op jit(solution)/shard_map/ppermute | solution.py:354
  93.4 0.0 collective-permute-done.19.refs_3_
  93.5 0.1 collective-permute-start.24
  93.6 3.2 %collective-permute-done.2.refs_3_ = bf16[512,256]{1,0:T(8,128)(2,1)} collective-permute-done((bf16[512,256]{1,0:T(8,128)(2,1)}, bf16[512,256]{1,0:T(8,128)(2,1)}, u32[]{:S(2)}, u32[]{:S(2)}) %collective-permute-start.2) | collective-permute-done | bytes 262176 | tf_op jit(solution)/shard_map/ppermute | solution.py:354
  96.7 3.7 %collective-permute-start.20 = (bf16[256,256]{1,0:T(8,128)(2,1)S(1)}, bf16[256,256]{1,0:T(8,128)(2,1)}, u32[]{:S(2)}, u32[]{:S(2)}) collective-permute-start(bf16[256,256]{1,0:T(8,128)(2,1)S(1)} %slice.8), channel_id=1, source_target_pairs={{1,0},{2,1},{3,2},{4,3},{5,4},{6,5},{7,6},{0,7},{9,8},{10,9},{11,1... | collective-permute-start | bytes 393224 | tf_op jit(solution)/shard_map/ppermute | solution.py:354
  100.4 0.0 collective-permute-done.6.refs_4_
  100.4 1.3 %copy-done = bf16[16,256,256]{2,1,0:T(8,128)(2,1)} copy-done((bf16[16,256,256]{2,1,0:T(8,128)(2,1)}, bf16[16,256,256]{2,1,0:T(8,128)(2,1)S(1)}, u32[]{:S(2)}) %copy-start) | copy-done | bytes 2097176
  101.8 4.4 %project.3 = (f32[512,256]{1,0:T(8,128)}, bf16[512,256]{1,0:T(8,128)(2,1)}) custom-call(s32[1]{0:T(128)} %bitcast.place_ref, bf16[512,256]{1,0:T(8,128)(2,1)} %get-tuple-element.33.refs_0_, bf16[512,256]{1,0:T(8,128)(2,1)} %collective-permute-done.refs_1_, bf16[512,256]{1,0:T(8,128)(2,1)} %collective-permute-done.1.refs_2_, ...), custom_call_target="tpu_custom_call" | custom-call | flops 4000000000 | bytes 4000000 | tf_op jit(solution)/shard_map/project/pallas_call | solution.py:379
  106.3 0.8 collective-permute-start.8
  107.0 0.0 collective-permute-done.15.refs_5_
  107.0 0.0 collective-permute-done.12.refs_4_
  107.0 4.4 %project.4 = (f32[512,256]{1,0:T(8,128)}, bf16[512,256]{1,0:T(8,128)(2,1)}) custom-call(s32[1]{0:T(128)} %bitcast.place_ref, bf16[512,256]{1,0:T(8,128)(2,1)} %get-tuple-element.42.refs_0_, bf16[512,256]{1,0:T(8,128)(2,1)} %copy-done.11, bf16[512,256]{1,0:T(8,128)(2,1)} %copy-done.15, bf16[512,256]{1,0:T(8,128)(2,1)} %collective-permute-done.11.refs_3_, ...), custom_call_target="tpu_custom_call" | custom-call | flops 4000000000 | bytes 4000000 | tf_op jit(solution)/shard_map/project/pallas_call | solution.py:379
  111.5 1.4 %collective-permute-start.16 = (bf16[512,256]{1,0:T(8,128)(2,1)}, bf16[512,256]{1,0:T(8,128)(2,1)S(1)}, u32[]{:S(2)}, u32[]{:S(2)}) collective-permute-start(bf16[512,256]{1,0:T(8,128)(2,1)} %get-tuple-element.44), channel_id=1, source_target_pairs={{0,8},{1,9},{2,10},{3,11},{4,12},{5,13},{6,14},{7,15},{8,0},{9,1},... | collective-permute-start | bytes 786440 | tf_op jit(solution)/shard_map/ppermute | solution.py:395
  112.9 0.0 collective-permute-done.20.refs_4_
  112.9 0.7 copy-done.19
  113.6 4.4 %project.5 = (f32[512,256]{1,0:T(8,128)}, bf16[512,256]{1,0:T(8,128)(2,1)}) custom-call(s32[1]{0:T(128)} %bitcast.place_ref, bf16[512,256]{1,0:T(8,128)(2,1)} %gate.3.refs_0_, bf16[512,256]{1,0:T(8,128)(2,1)} %copy-done.10, bf16[512,256]{1,0:T(8,128)(2,1)} %collective-permute-done.18.refs_2_, bf16[512,256]{1,0:T(8,128)(2,1)} %copy-done.6, ...), custom_call_target="tpu_custom_call" | custom-call | flops 4000000000 | bytes 4000000 | tf_op jit(solution)/shard_map/project/pallas_call | solution.py:379
  118.0 0.8 collective-permute-start.25
  118.8 0.1 add_convert_fusion.2
  118.8 0.0 collective-permute-done.16
  118.9 0.1 add_convert_fusion.1
  118.9 5.7 %collective-permute-done.25 = bf16[512,256]{1,0:T(8,128)(2,1)S(1)} collective-permute-done((bf16[512,256]{1,0:T(8,128)(2,1)}, bf16[512,256]{1,0:T(8,128)(2,1)S(1)}, u32[]{:S(2)}, u32[]{:S(2)}) %collective-permute-start.25) | collective-permute-done | bytes 262176 | tf_op jit(solution)/shard_map/ppermute | solution.py:395
  124.7 0.1 add_convert_fusion
  124.7 0.9 pad_maximum_fusion
  (45 shorter events, 0.1 us)
Async XLA Ops:
  0.0 13.9 %copy-start.18 = (bf16[256,256]{1,0:T(8,128)(2,1)S(1)}, bf16[256,256]{1,0:T(8,128)(2,1)}, u32[]{:S(2)}) copy-start(bf16[256,256]{1,0:T(8,128)(2,1)} %param.11) | copy-start | bytes 393220
  6.4 15.3 %all-to-all-start = ((bf16[16,48,256]{2,1,0:T(8,128)(2,1)}), bf16[16,48,256]{2,1,0:T(8,128)(2,1)S(1)}, u32[]{:S(2)}, u32[]{:S(2)}) async-start(bf16[16,48,256]{2,1,0:T(8,128)(2,1)} %get-tuple-element.32), calls=%async_computation | async-start | bytes 786432 | tf_op jit(solution)/shard_map/all_to_all | solution.py:301
  13.9 15.0 %collective-permute-start.7 = (bf16[256,256]{1,0:T(8,128)(2,1)S(1)}, bf16[256,256]{1,0:T(8,128)(2,1)S(1)}, u32[]{:S(2)}, u32[]{:S(2)}) collective-permute-start(bf16[256,256]{1,0:T(8,128)(2,1)S(1)} %copy-done.18), channel_id=1, source_target_pairs={{0,0},{1,16},{2,32},{3,48},{4,64},{5,80},{6,96},{7,112},{8,8},{9,2... | collective-permute-start | bytes 393224 | tf_op jit(solution)/shard_map/ppermute | solution.py:300
  21.7 0.8 copy-start.4
  30.4 9.2 %copy-start.9 = (bf16[512,256]{1,0:T(8,128)(2,1)S(1)}, bf16[512,256]{1,0:T(8,128)(2,1)}, u32[]{:S(2)}) copy-start(bf16[512,256]{1,0:T(8,128)(2,1)} %get-tuple-element.33.refs_0_) | copy-start | bytes 786436
  30.4 14.6 %copy-start.7 = (bf16[512,256]{1,0:T(8,128)(2,1)S(1)}, bf16[512,256]{1,0:T(8,128)(2,1)}, u32[]{:S(2)}) copy-start(bf16[512,256]{1,0:T(8,128)(2,1)} %get-tuple-element.42.refs_0_) | copy-start | bytes 786436
  30.4 70.0 %all-to-all-start.1 = ((bf16[16,256,256]{2,1,0:T(8,128)(2,1)}), bf16[16,256,256]{2,1,0:T(8,128)(2,1)S(1)}, u32[]{:S(2)}, u32[]{:S(2)}) async-start(bf16[16,256,256]{2,1,0:T(8,128)(2,1)} %broadcast_in_dim.7), calls=%async_computation.1 | async-start | bytes 4194304 | tf_op jit(solution)/shard_map/all_to_all | solution.py:368
  39.6 12.4 %collective-permute-start.3 = (bf16[512,256]{1,0:T(8,128)(2,1)S(1)}, bf16[512,256]{1,0:T(8,128)(2,1)S(1)}, u32[]{:S(2)}, u32[]{:S(2)}) collective-permute-start(bf16[512,256]{1,0:T(8,128)(2,1)S(1)} %copy-done.9), channel_id=1, source_target_pairs={{0,1},{1,2},{2,3},{3,4},{4,5},{5,6},{6,7},{7,0},{8,9},{9,10},{10,1... | collective-permute-start | bytes 786440 | tf_op jit(solution)/shard_map/ppermute | solution.py:354
  41.8 10.3 %collective-permute-start = (bf16[512,256]{1,0:T(8,128)(2,1)S(1)}, bf16[512,256]{1,0:T(8,128)(2,1)}, u32[]{:S(2)}, u32[]{:S(2)}) collective-permute-start(bf16[512,256]{1,0:T(8,128)(2,1)S(1)} %copy-done.9), channel_id=1, source_target_pairs={{1,0},{2,1},{3,2},{4,3},{5,4},{6,5},{7,6},{0,7},{9,8},{10,9},{11,1... | collective-permute-start | bytes 786440 | tf_op jit(solution)/shard_map/ppermute | solution.py:354
  45.0 14.7 %collective-permute-start.9 = (bf16[512,256]{1,0:T(8,128)(2,1)S(1)}, bf16[512,256]{1,0:T(8,128)(2,1)S(1)}, u32[]{:S(2)}, u32[]{:S(2)}) collective-permute-start(bf16[512,256]{1,0:T(8,128)(2,1)S(1)} %copy-done.7), channel_id=1, source_target_pairs={{1,0},{2,1},{3,2},{4,3},{5,4},{6,5},{7,6},{0,7},{9,8},{10,9},{11,1... | collective-permute-start | bytes 786440 | tf_op jit(solution)/shard_map/ppermute | solution.py:354
  47.0 10.7 %collective-permute-start.13 = (bf16[512,256]{1,0:T(8,128)(2,1)S(1)}, bf16[512,256]{1,0:T(8,128)(2,1)S(1)}, u32[]{:S(2)}, u32[]{:S(2)}) collective-permute-start(bf16[512,256]{1,0:T(8,128)(2,1)S(1)} %copy-done.7), channel_id=1, source_target_pairs={{0,1},{1,2},{2,3},{3,4},{4,5},{5,6},{6,7},{7,0},{8,9},{9,10},{10,1... | collective-permute-start | bytes 786440 | tf_op jit(solution)/shard_map/ppermute | solution.py:354
  52.0 31.6 %copy-start.13 = (bf16[512,256]{1,0:T(8,128)(2,1)}, bf16[512,256]{1,0:T(8,128)(2,1)S(1)}, u32[]{:S(2)}) copy-start(bf16[512,256]{1,0:T(8,128)(2,1)S(1)} %collective-permute-done.3.refs_7_) | copy-start | bytes 786436
  52.0 11.2 %collective-permute-start.21 = (bf16[512,256]{1,0:T(8,128)(2,1)}, bf16[512,256]{1,0:T(8,128)(2,1)S(1)}, u32[]{:S(2)}, u32[]{:S(2)}) collective-permute-start(bf16[512,256]{1,0:T(8,128)(2,1)} %gate.3.refs_0_), channel_id=1, source_target_pairs={{0,1},{1,2},{2,3},{3,4},{4,5},{5,6},{6,7},{7,0},{8,9},{9,10},{10,1... | collective-permute-start | bytes 786440 | tf_op jit(solution)/shard_map/ppermute | solution.py:354
  52.0 11.2 %collective-permute-start.17 = (bf16[512,256]{1,0:T(8,128)(2,1)}, bf16[512,256]{1,0:T(8,128)(2,1)S(1)}, u32[]{:S(2)}, u32[]{:S(2)}) collective-permute-start(bf16[512,256]{1,0:T(8,128)(2,1)} %gate.3.refs_0_), channel_id=1, source_target_pairs={{1,0},{2,1},{3,2},{4,3},{5,4},{6,5},{7,6},{0,7},{9,8},{10,9},{11,1... | collective-permute-start | bytes 786440 | tf_op jit(solution)/shard_map/ppermute | solution.py:354
  55.5 13.4 %collective-permute-start.4 = (bf16[512,256]{1,0:T(8,128)(2,1)S(1)}, bf16[512,256]{1,0:T(8,128)(2,1)S(1)}, u32[]{:S(2)}, u32[]{:S(2)}) collective-permute-start(bf16[512,256]{1,0:T(8,128)(2,1)S(1)} %collective-permute-done.3.refs_7_), channel_id=1, source_target_pairs={{0,1},{1,2},{2,3},{3,4},{4,5},{5,6},{6,7},{7,0},{8,9},{9,10},{10,1... | collective-permute-start | bytes 786440 | tf_op jit(solution)/shard_map/ppermute | solution.py:354
  57.6 22.1 %copy-start.12 = (bf16[512,256]{1,0:T(8,128)(2,1)}, bf16[512,256]{1,0:T(8,128)(2,1)S(1)}, u32[]{:S(2)}) copy-start(bf16[512,256]{1,0:T(8,128)(2,1)S(1)} %collective-permute-done.13.refs_7_) | copy-start | bytes 786436
  57.6 11.2 %collective-permute-start.1 = (bf16[512,256]{1,0:T(8,128)(2,1)}, bf16[512,256]{1,0:T(8,128)(2,1)}, u32[]{:S(2)}, u32[]{:S(2)}) collective-permute-start(bf16[512,256]{1,0:T(8,128)(2,1)} %collective-permute-done.refs_1_), channel_id=1, source_target_pairs={{1,0},{2,1},{3,2},{4,3},{5,4},{6,5},{7,6},{0,7},{9,8},{10,9},{11,1... | collective-permute-start | bytes 786440 | tf_op jit(solution)/shard_map/ppermute | solution.py:354
  59.7 18.2 %copy-start.11 = (bf16[512,256]{1,0:T(8,128)(2,1)}, bf16[512,256]{1,0:T(8,128)(2,1)S(1)}, u32[]{:S(2)}) copy-start(bf16[512,256]{1,0:T(8,128)(2,1)S(1)} %collective-permute-done.9.refs_1_) | copy-start | bytes 786436
  59.7 14.5 %collective-permute-start.10 = (bf16[512,256]{1,0:T(8,128)(2,1)S(1)}, bf16[512,256]{1,0:T(8,128)(2,1)S(1)}, u32[]{:S(2)}, u32[]{:S(2)}) collective-permute-start(bf16[512,256]{1,0:T(8,128)(2,1)S(1)} %collective-permute-done.9.refs_1_), channel_id=1, source_target_pairs={{1,0},{2,1},{3,2},{4,3},{5,4},{6,5},{7,6},{0,7},{9,8},{10,9},{11,1... | collective-permute-start | bytes 786440 | tf_op jit(solution)/shard_map/ppermute | solution.py:354
  63.3 43.0 %copy-start.8 = (bf16[512,256]{1,0:T(8,128)(2,1)}, bf16[512,256]{1,0:T(8,128)(2,1)S(1)}, u32[]{:S(2)}) copy-start(bf16[512,256]{1,0:T(8,128)(2,1)S(1)} %collective-permute-done.21.refs_8_) | copy-start | bytes 786436
  63.3 14.6 %collective-permute-start.22 = (bf16[512,256]{1,0:T(8,128)(2,1)S(1)}, bf16[512,256]{1,0:T(8,128)(2,1)S(1)}, u32[]{:S(2)}, u32[]{:S(2)}) collective-permute-start(bf16[512,256]{1,0:T(8,128)(2,1)S(1)} %collective-permute-done.21.refs_8_), channel_id=1, source_target_pairs={{0,1},{1,2},{2,3},{3,4},{4,5},{5,6},{6,7},{7,0},{8,9},{9,10},{10,1... | collective-permute-start | bytes 786440 | tf_op jit(solution)/shard_map/ppermute | solution.py:354
  63.3 14.7 %copy-start.10 = (bf16[512,256]{1,0:T(8,128)(2,1)}, bf16[512,256]{1,0:T(8,128)(2,1)S(1)}, u32[]{:S(2)}) copy-start(bf16[512,256]{1,0:T(8,128)(2,1)S(1)} %collective-permute-done.17.refs_1_) | copy-start | bytes 786436
  63.3 16.5 %collective-permute-start.18 = (bf16[512,256]{1,0:T(8,128)(2,1)S(1)}, bf16[512,256]{1,0:T(8,128)(2,1)}, u32[]{:S(2)}, u32[]{:S(2)}) collective-permute-start(bf16[512,256]{1,0:T(8,128)(2,1)S(1)} %collective-permute-done.17.refs_1_), channel_id=1, source_target_pairs={{1,0},{2,1},{3,2},{4,3},{5,4},{6,5},{7,6},{0,7},{9,8},{10,9},{11,1... | collective-permute-start | bytes 786440 | tf_op jit(solution)/shard_map/ppermute | solution.py:354
  68.9 15.5 %copy-start.16 = (bf16[512,256]{1,0:T(8,128)(2,1)}, bf16[512,256]{1,0:T(8,128)(2,1)S(1)}, u32[]{:S(2)}) copy-start(bf16[512,256]{1,0:T(8,128)(2,1)S(1)} %collective-permute-done.4.refs_6_) | copy-start | bytes 786436
  68.9 14.7 %collective-permute-start.14 = (bf16[512,256]{1,0:T(8,128)(2,1)S(1)}, bf16[512,256]{1,0:T(8,128)(2,1)S(1)}, u32[]{:S(2)}, u32[]{:S(2)}) collective-permute-start(bf16[512,256]{1,0:T(8,128)(2,1)S(1)} %collective-permute-done.13.refs_7_), channel_id=1, source_target_pairs={{0,1},{1,2},{2,3},{3,4},{4,5},{5,6},{6,7},{7,0},{8,9},{9,10},{10,1... | collective-permute-start | bytes 786440 | tf_op jit(solution)/shard_map/ppermute | solution.py:354
  68.9 16.9 %collective-permute-start.5 = (bf16[512,256]{1,0:T(8,128)(2,1)S(1)}, bf16[512,256]{1,0:T(8,128)(2,1)}, u32[]{:S(2)}, u32[]{:S(2)}) collective-permute-start(bf16[512,256]{1,0:T(8,128)(2,1)S(1)} %collective-permute-done.4.refs_6_), channel_id=1, source_target_pairs={{0,1},{1,2},{2,3},{3,4},{4,5},{5,6},{6,7},{7,0},{8,9},{9,10},{10,1... | collective-permute-start | bytes 786440 | tf_op jit(solution)/shard_map/ppermute | solution.py:354
  74.2 17.2 %copy-start.15 = (bf16[512,256]{1,0:T(8,128)(2,1)}, bf16[512,256]{1,0:T(8,128)(2,1)S(1)}, u32[]{:S(2)}) copy-start(bf16[512,256]{1,0:T(8,128)(2,1)S(1)} %collective-permute-done.10.refs_2_) | copy-start | bytes 786436
  74.2 11.7 %collective-permute-start.11 = (bf16[512,256]{1,0:T(8,128)(2,1)S(1)}, bf16[512,256]{1,0:T(8,128)(2,1)}, u32[]{:S(2)}, u32[]{:S(2)}) collective-permute-start(bf16[512,256]{1,0:T(8,128)(2,1)S(1)} %collective-permute-done.10.refs_2_), channel_id=1, source_target_pairs={{1,0},{2,1},{3,2},{4,3},{5,4},{6,5},{7,6},{0,7},{9,8},{10,9},{11,1... | collective-permute-start | bytes 786440 | tf_op jit(solution)/shard_map/ppermute | solution.py:354
  77.9 28.4 %copy-start.14 = (bf16[512,256]{1,0:T(8,128)(2,1)}, bf16[512,256]{1,0:T(8,128)(2,1)S(1)}, u32[]{:S(2)}) copy-start(bf16[512,256]{1,0:T(8,128)(2,1)S(1)} %collective-permute-done.22.refs_7_) | copy-start | bytes 786436
  77.9 13.5 %collective-permute-start.23 = (bf16[512,256]{1,0:T(8,128)(2,1)S(1)}, bf16[512,256]{1,0:T(8,128)(2,1)S(1)}, u32[]{:S(2)}, u32[]{:S(2)}) collective-permute-start(bf16[512,256]{1,0:T(8,128)(2,1)S(1)} %collective-permute-done.22.refs_7_), channel_id=1, source_target_pairs={{0,1},{1,2},{2,3},{3,4},{4,5},{5,6},{6,7},{7,0},{8,9},{9,10},{10,1... | collective-permute-start | bytes 786440 | tf_op jit(solution)/shard_map/ppermute | solution.py:354
  79.8 13.6 %collective-permute-start.19 = (bf16[512,256]{1,0:T(8,128)(2,1)}, bf16[512,256]{1,0:T(8,128)(2,1)S(1)}, u32[]{:S(2)}, u32[]{:S(2)}) collective-permute-start(bf16[512,256]{1,0:T(8,128)(2,1)} %collective-permute-done.18.refs_2_), channel_id=1, source_target_pairs={{1,0},{2,1},{3,2},{4,3},{5,4},{6,5},{7,6},{0,7},{9,8},{10,9},{11,1... | collective-permute-start | bytes 786440 | tf_op jit(solution)/shard_map/ppermute | solution.py:354
  83.6 2.3 %copy-start.17 = (bf16[512,256]{1,0:T(8,128)(2,1)}, bf16[512,256]{1,0:T(8,128)(2,1)S(1)}, u32[]{:S(2)}) copy-start(bf16[512,256]{1,0:T(8,128)(2,1)S(1)} %collective-permute-done.14.refs_6_) | copy-start | bytes 786436
  83.6 13.1 %collective-permute-start.2 = (bf16[512,256]{1,0:T(8,128)(2,1)}, bf16[512,256]{1,0:T(8,128)(2,1)}, u32[]{:S(2)}, u32[]{:S(2)}) collective-permute-start(bf16[512,256]{1,0:T(8,128)(2,1)} %collective-permute-done.1.refs_2_), channel_id=1, source_target_pairs={{1,0},{2,1},{3,2},{4,3},{5,4},{6,5},{7,6},{0,7},{9,8},{10,9},{11,1... | collective-permute-start | bytes 786440 | tf_op jit(solution)/shard_map/ppermute | solution.py:354
  85.8 14.6 %collective-permute-start.6 = (bf16[512,256]{1,0:T(8,128)(2,1)}, bf16[512,256]{1,0:T(8,128)(2,1)}, u32[]{:S(2)}, u32[]{:S(2)}) collective-permute-start(bf16[512,256]{1,0:T(8,128)(2,1)} %collective-permute-done.5.refs_5_), channel_id=1, source_target_pairs={{0,1},{1,2},{2,3},{3,4},{4,5},{5,6},{6,7},{7,0},{8,9},{9,10},{10,1... | collective-permute-start | bytes 786440 | tf_op jit(solution)/shard_map/ppermute | solution.py:354
  85.9 21.2 %collective-permute-start.15 = (bf16[512,256]{1,0:T(8,128)(2,1)}, bf16[512,256]{1,0:T(8,128)(2,1)}, u32[]{:S(2)}, u32[]{:S(2)}) collective-permute-start(bf16[512,256]{1,0:T(8,128)(2,1)} %copy-done.17), channel_id=1, source_target_pairs={{0,1},{1,2},{2,3},{3,4},{4,5},{5,6},{6,7},{7,0},{8,9},{9,10},{10,1... | collective-permute-start | bytes 786440 | tf_op jit(solution)/shard_map/ppermute | solution.py:354
  91.4 14.9 %copy-start.5 = (bf16[512,256]{1,0:T(8,128)(2,1)}, bf16[512,256]{1,0:T(8,128)(2,1)S(1)}, u32[]{:S(2)}) copy-start(bf16[512,256]{1,0:T(8,128)(2,1)S(1)} %collective-permute-done.23.refs_6_) | copy-start | bytes 786436
  91.4 15.7 %collective-permute-start.12 = (bf16[512,256]{1,0:T(8,128)(2,1)}, bf16[512,256]{1,0:T(8,128)(2,1)}, u32[]{:S(2)}, u32[]{:S(2)}) collective-permute-start(bf16[512,256]{1,0:T(8,128)(2,1)} %collective-permute-done.11.refs_3_), channel_id=1, source_target_pairs={{1,0},{2,1},{3,2},{4,3},{5,4},{6,5},{7,6},{0,7},{9,8},{10,9},{11,1... | collective-permute-start | bytes 786440 | tf_op jit(solution)/shard_map/ppermute | solution.py:354
  93.4 12.8 %copy-start.6 = (bf16[512,256]{1,0:T(8,128)(2,1)}, bf16[512,256]{1,0:T(8,128)(2,1)S(1)}, u32[]{:S(2)}) copy-start(bf16[512,256]{1,0:T(8,128)(2,1)S(1)} %collective-permute-done.19.refs_3_) | copy-start | bytes 786436
  93.5 19.4 %collective-permute-start.24 = (bf16[256,256]{1,0:T(8,128)(2,1)S(1)}, bf16[256,256]{1,0:T(8,128)(2,1)S(1)}, u32[]{:S(2)}, u32[]{:S(2)}) collective-permute-start(bf16[256,256]{1,0:T(8,128)(2,1)S(1)} %slice.9), channel_id=1, source_target_pairs={{0,1},{1,2},{2,3},{3,4},{4,5},{5,6},{6,7},{7,0},{8,9},{9,10},{10,1... | collective-permute-start | bytes 393224 | tf_op jit(solution)/shard_map/ppermute | solution.py:354
  96.7 16.2 %collective-permute-start.20 = (bf16[256,256]{1,0:T(8,128)(2,1)S(1)}, bf16[256,256]{1,0:T(8,128)(2,1)}, u32[]{:S(2)}, u32[]{:S(2)}) collective-permute-start(bf16[256,256]{1,0:T(8,128)(2,1)S(1)} %slice.8), channel_id=1, source_target_pairs={{1,0},{2,1},{3,2},{4,3},{5,4},{6,5},{7,6},{0,7},{9,8},{10,9},{11,1... | collective-permute-start | bytes 393224 | tf_op jit(solution)/shard_map/ppermute | solution.py:354
  100.4 1.3 %copy-start = (bf16[16,256,256]{2,1,0:T(8,128)(2,1)}, bf16[16,256,256]{2,1,0:T(8,128)(2,1)S(1)}, u32[]{:S(2)}) copy-start(bf16[16,256,256]{2,1,0:T(8,128)(2,1)S(1)} %all-to-all-done.1) | copy-start | bytes 6291460
  106.3 12.5 %collective-permute-start.8 = (bf16[512,256]{1,0:T(8,128)(2,1)}, bf16[512,256]{1,0:T(8,128)(2,1)S(1)}, u32[]{:S(2)}, u32[]{:S(2)}) collective-permute-start(bf16[512,256]{1,0:T(8,128)(2,1)} %get-tuple-element.41), channel_id=1, source_target_pairs={{0,8},{1,9},{2,10},{3,11},{4,12},{5,13},{6,14},{7,15},{8,0},{9,1},... | collective-permute-start | bytes 786440 | tf_op jit(solution)/shard_map/ppermute | solution.py:395
  111.4 7.3 %copy-start.1 = (f32[512,256]{1,0:T(8,128)S(1)}, f32[512,256]{1,0:T(8,128)}, u32[]{:S(2)}) copy-start(f32[512,256]{1,0:T(8,128)} %get-tuple-element.40) | copy-start | bytes 1572868
  111.5 7.4 %copy-start.2 = (f32[512,256]{1,0:T(8,128)S(1)}, f32[512,256]{1,0:T(8,128)}, u32[]{:S(2)}) copy-start(f32[512,256]{1,0:T(8,128)} %get-tuple-element.43) | copy-start | bytes 1572868
  111.5 7.4 %collective-permute-start.16 = (bf16[512,256]{1,0:T(8,128)(2,1)}, bf16[512,256]{1,0:T(8,128)(2,1)S(1)}, u32[]{:S(2)}, u32[]{:S(2)}) collective-permute-start(bf16[512,256]{1,0:T(8,128)(2,1)} %get-tuple-element.44), channel_id=1, source_target_pairs={{0,8},{1,9},{2,10},{3,11},{4,12},{5,13},{6,14},{7,15},{8,0},{9,1},... | collective-permute-start | bytes 786440 | tf_op jit(solution)/shard_map/ppermute | solution.py:395
  112.9 0.7 copy-start.19
  118.0 6.7 %copy-start.3 = (f32[512,256]{1,0:T(8,128)S(1)}, f32[512,256]{1,0:T(8,128)}, u32[]{:S(2)}) copy-start(f32[512,256]{1,0:T(8,128)} %get-tuple-element.47) | copy-start | bytes 1572868
  118.0 6.7 %collective-permute-start.25 = (bf16[512,256]{1,0:T(8,128)(2,1)}, bf16[512,256]{1,0:T(8,128)(2,1)S(1)}, u32[]{:S(2)}, u32[]{:S(2)}) collective-permute-start(bf16[512,256]{1,0:T(8,128)(2,1)} %get-tuple-element.48), channel_id=1, source_target_pairs={{0,8},{1,9},{2,10},{3,11},{4,12},{5,13},{6,14},{7,15},{8,0},{9,1},... | collective-permute-start | bytes 786440 | tf_op jit(solution)/shard_map/ppermute | solution.py:395

commit v4 on v3

--- a/solution.py
+++ b/solution.py
@@ -34,8 +34,8 @@
     ("hop", 0, 4, "u"),
     ("hop", 2, 3, "ud"),
     ("hop", 1, 4, "d"),
+    ("ahead", 0, 2, 4),
     ("hop", 2, 4, "ud"),
-    ("project", 0),
     ("project", 1),
     ("project", 2),
 )
@@ -47,6 +47,20 @@
 
 def wide(row):
     return jnp.broadcast_to(row, (SEGS, LANES))
+
+
+def spread(ref, base, source, start, chunk):
+    steps = chunk // SEGS
+    for r in range(SEGS):
+        at, row = base + r * (steps + 8), start + r * steps
+        if row > 0:
+            ref[pl.ds(at, steps + 8), :] = source[0, pl.ds(row - 16, steps + 16), :].astype(F32)[8:]
+        else:
+            ref[pl.ds(at + 8, steps), :] = source[0, pl.ds(0, steps), :].astype(F32)
+
+
+def room(chunk):
+    return chunk + SEGS * 8
 
 
 def states_kernel(
@@ -56,8 +70,6 @@
     tokens = k_ref.shape[1]
     kx[pl.ds(0, 8), :] = jnp.zeros((8, LANES), F32)
     vx[pl.ds(0, 8), :] = jnp.zeros((8, LANES), F32)
-    kx[pl.ds(8, tokens), :] = k_ref[0].astype(F32)
-    vx[pl.ds(8, tokens), :] = v_ref[0].astype(F32)
     decay = decay_ref[...]
     modes_ref[0] = decay
     modes_ref[1] = res_ref[...] * jnp.sqrt(decay)
@@ -68,11 +80,14 @@
     later = (SEGS - 1 - row_ids()).astype(F32)
     state = jnp.zeros((MODES, LANES), F32)
 
+    base = 0
     for c, (offset, chunk) in enumerate(CHUNKS):
         steps = chunk // SEGS
+        spread(kx, base, k_ref, offset, chunk)
+        spread(vx, base, v_ref, offset, chunk)
 
         def at(ref, i):
-            return ref[pl.ds(8 + offset + i, SEGS, stride=steps), :]
+            return ref[pl.ds(base + 8 + i, SEGS, stride=steps + 8), :]
 
         def step(i, carry):
             k1, k2, v1, v2, acc = carry
@@ -87,7 +102,7 @@
         acc = lax.fori_loop(
             0, steps, step,
             (at(kx, -1), at(kx, -2), at(vx, -1), at(vx, -2), zero),
-            unroll=8,
+            unroll=16,
         )[4]
         start_ref[c] = state
         ends = []
@@ -96,6 +111,7 @@
             weight = jnp.exp(-wide(decay[m : m + 1]) * (later * steps))
             ends.append(jnp.sum(acc[m] * weight, axis=0, keepdims=True))
         state = state * jnp.exp(-decay * chunk) + jnp.concatenate(ends, axis=0)
+        base += room(chunk)
 
     tail = q_tail_ref.shape[1] - 2
     upper = state.astype(BF16).astype(F32)
@@ -106,8 +122,8 @@
             kx[pl.ds(8, 2), :],
             vx[pl.ds(8, 2), :],
             q_tail_ref[0].astype(F32)[tail:],
-            kx[pl.ds(6 + tokens, 2), :],
-            vx[pl.ds(6 + tokens, 2), :],
+            kx[pl.ds(base - 2, 2), :],
+            vx[pl.ds(base - 2, 2), :],
             jnp.zeros((ROWS - 2 * MODES - 10, LANES), F32),
         ],
         axis=0,
@@ -158,7 +174,6 @@
         out_refs = refs[8 : 8 + len(group)]
         (qx, gx) = refs[8 + len(group) :]
     decay = modes_ref[0]
-    qx[pl.ds(8, q_ref.shape[1]), :] = q_ref[0].astype(F32)
     extra = None
     if first:
         state, extra, q_halo = incoming_states(me_ref[0], tokens, taps_ref, decay, recv_ref)
@@ -186,10 +201,12 @@
     tq = [wide(taps_ref[0, j : j + 1, :]) for j in range(3)]
     skip = wide(skip_ref[...])
 
+    place = 0
     for k, c in enumerate(group):
         offset, chunk = CHUNKS[c]
         base = offset - CHUNKS[group[0]][0]
         steps = chunk // SEGS
+        spread(qx, place, q_ref, base, chunk)
         keep1 = jnp.exp(-decay * steps)
         keep2 = jnp.exp(-decay * (2 * steps))
         keep4 = jnp.exp(-decay * (4 * steps))
@@ -207,7 +224,7 @@
             acc.append(x)
 
         def at(i):
-            return qx[pl.ds(8 + base + i, SEGS, stride=steps), :]
+            return qx[pl.ds(place + 8 + i, SEGS, stride=steps + 8), :]
 
         def step(i, carry, more=None):
             q1, q2, acc = carry
@@ -220,17 +237,19 @@
             while len(terms) > 1:
                 terms = [sum(terms[i + 1 : i + 2], terms[i]) for i in range(0, len(terms), 2)]
             query = tq[0] * q0 + tq[1] * q1 + tq[2] * q2
-            gx[pl.ds(base + i, SEGS, stride=steps), :] = query * terms[0]
+            gx[pl.ds(place + i, SEGS, stride=steps + 8), :] = query * terms[0]
             return q0, q1, acc
 
         carry = (at(-1), at(-2), tuple(acc))
         begin = 0
         if c == 0:
-            for begin in range(4):
+            for begin in range(8):
                 carry = step(begin, carry, extra[begin] if begin < 2 else None)
-            begin = 4
-        lax.fori_loop(begin, steps, step, carry, unroll=4)
-        out_refs[k][...] = gx[pl.ds(base, chunk), :].astype(BF16)
+            begin = 8
+        lax.fori_loop(begin, steps, step, carry, unroll=8)
+        for r in range(SEGS):
+            out_refs[k][pl.ds(r * steps, steps), :] = gx[pl.ds(place + r * (steps + 8), steps), :].astype(BF16)
+        place += room(chunk)
 
 
 def project_kernel(place_ref, *refs):
@@ -291,7 +310,7 @@
             jax.ShapeDtypeStruct((CTX, ROWS, chans), BF16),
             jax.ShapeDtypeStruct((2, MODES, chans), F32),
         ],
-        scratch_shapes=[pltpu.VMEM((tokens + 8, LANES), F32)] * 2,
+        scratch_shapes=[pltpu.VMEM((sum(room(n) for _, n in CHUNKS), LANES), F32)] * 2,
         compiler_params=params(60),
         cost_estimate=cost,
         name="states",
@@ -329,7 +348,7 @@
             in_specs=in_specs,
             out_specs=out_specs,
             out_shape=out_shape,
-            scratch_shapes=[pltpu.VMEM((size + 8, LANES), F32), pltpu.VMEM((size, LANES), F32)],
+            scratch_shapes=[pltpu.VMEM((sum(room(CHUNKS[c][1]) for c in group), LANES), F32)] * 2,
             compiler_params=params(60),
             cost_estimate=cost,
             name="gate",
@@ -385,7 +404,7 @@
                 jax.ShapeDtypeStruct((chunk, chans), F32),
                 jax.ShapeDtypeStruct((chunk, chans), BF16),
             ],
-            compiler_params=params(60),
+            compiler_params=params(20),
             cost_estimate=cost,
             name="project",
         )(place, *parts, w_all)

time: 126 us -> 120 us (0.952)
  Pallas kernels: 29.8 us -> 22.1 us
  local copies, waits for them, and re-layouts: 4.4 us -> 6.61 us
  starting transfers between devices: 58.3 us -> 56.4 us
  waiting for transfers between devices: 31.8 us -> 33.1 us
    pallas_call x3, Pallas kernels: 13.3 us -> 7.72 us  [project(): pl.pallas_call(project_kernel, grid=(2,), in_specs=[smem] + [tile] * 4 +...]
    ppermute x22, starting transfers between devices: 32 us -> 29.3 us  [hop(): arrived[c, s, way] = lax.ppermute(block, 'ch', up if way == 'u' else down)]
    unnamed x40 -> x32, local copies, waits for them, and re-layouts: 2.83 us -> 5.04 us
  transfers between devices with their start and end apart: 28 -> 28, of which waited for: 11 -> 13; matrix products, arithmetic and copies ran while one was open for 0% -> 0% of each run, Pallas kernels for 19% -> 14%
where the time goes in v4:
time: 120 us
  starting transfers between devices  56.4 us (47%)
  waiting for transfers between devices  33.1 us (28%)
  Pallas kernels  22.1 us (18%)
  local copies, waits for them, and re-layouts  6.61 us (6%)
    ppermute x22, starting transfers between devices, hop(): arrived[c, s, way] = lax.ppermute(block, 'ch', up if way == 'u' else down)  29.3 us
    ppermute x22, waiting for transfers between devices, hop(): arrived[c, s, way] = lax.ppermute(block, 'ch', up if way == 'u' else down)  26.1 us
    all_to_all x1, starting transfers between devices, weights(): w_all = lax.all_to_all(jnp.broadcast_to(w, (CTX, *w.shape)), 'ctx', 0, 0)  9.45 us
    pallas_call x2, Pallas kernels, gate(): pl.pallas_call(functools.partial(gate_kernel, group, tokens), grid=(tiles...  9.2 us
    pallas_call x3, Pallas kernels, project(): pl.pallas_call(project_kernel, grid=(2,), in_specs=[smem] + [tile] * 4 +...  7.72 us
    all_to_all x1, starting transfers between devices, local(): recv = lax.all_to_all(send, 'ctx', 0, 0)  7.48 us
    ppermute x1, starting transfers between devices, local(): w_block = lax.ppermute(w_block, ('ctx', 'ch'), swap)  6.69 us
    ppermute x3, waiting for transfers between devices, send(): own[c], theirs[c] = (mine, lax.ppermute(other, 'ch', across))  5.51 us
  transfers between devices with their start and end apart: 28, of which 13 were waited for; matrix products, arithmetic and copies ran while one was open for 0% of the time, Pallas kernels for 14%

profile of v4, /device:TPU:2, one launch (start us, length us, event | category | flops | bytes accessed | tf_op | source)
XLA Modules:
  0.0 119.6 jit_solution(3912669983842038082)
XLA Ops:
  0.0 5.2 %states.1 = (f32[1536,256]{1,0:T(8,128)}, f32[3,16,8,256]{3,2,1,0:T(8,128)}, f32[3,16,256]{2,1,0:T(8,128)}, bf16[16,48,256]{2,1,0:T(8,128)(2,1)}, f32[2,16,256]{2,1,0:T(8,128)}) custom-call(bf16[3,1536,256]{2,1,0:T(8,128)(2,1)} %refs_1_.3, bf16[3,1536,256]{2,1,0:T(8,128)(2,1)} %refs_1_.3, bf16[3,1536,256]{2,1,0:T(8,128)(2,1)} %refs_1_.3, ...), custom_call_target="tpu_custom_call" | custom-call | flops 4000000000 | bytes 4000000 | tf_op jit(solution)/shard_map/states/pallas_call | solution.py:288
  5.2 7.5 %all-to-all-start = ((bf16[16,48,256]{2,1,0:T(8,128)(2,1)}), bf16[16,48,256]{2,1,0:T(8,128)(2,1)S(1)}, u32[]{:S(2)}, u32[]{:S(2)}) async-start(bf16[16,48,256]{2,1,0:T(8,128)(2,1)} %get-tuple-element.35), calls=%async_computation | async-start | bytes 786432 | tf_op jit(solution)/shard_map/all_to_all | solution.py:320
  12.7 6.7 %collective-permute-start.7 = (bf16[256,256]{1,0:T(8,128)(2,1)S(1)}, bf16[256,256]{1,0:T(8,128)(2,1)S(1)}, u32[]{:S(2)}, u32[]{:S(2)}) collective-permute-start(bf16[256,256]{1,0:T(8,128)(2,1)S(1)} %copy-done.15), channel_id=1, source_target_pairs={{0,0},{1,16},{2,32},{3,48},{4,64},{5,80},{6,96},{7,112},{8,8},{9,2... | collective-permute-start | bytes 393224 | tf_op jit(solution)/shard_map/ppermute | solution.py:319
  19.4 1.1 all-to-all-done.refs_8_
  20.5 0.7 copy-done.14
  21.3 5.7 %gate.2 = (bf16[512,256]{1,0:T(8,128)(2,1)}, bf16[512,256]{1,0:T(8,128)(2,1)}, f32[1,16,256]{2,1,0:T(8,128)}) custom-call(s32[1]{0:T(128)} %bitcast.1.refs_0_, bf16[3,1536,256]{2,1,0:T(8,128)(2,1)} %refs_1_.3, f32[3,3,256]{2,1,0:T(4,128)} %refs_2_.3, f32[2,16,256]{2,1,0:T(8,128)} %get-tuple-element.31.refs_3_, f32[1,256]{1,0:T(1,128)} %bitcast.11, ...), custom_call_target="tpu_custom_call" | custom-call | flops 4000000000 | bytes 4000000 | tf_op jit(solution)/shard_map/gate/pallas_call | solution.py:345
  27.0 0.4 collective-permute-done.7
  27.4 1.5 %broadcast_in_dim.7 = bf16[16,256,256]{2,1,0:T(8,128)(2,1)} broadcast(bf16[256,256]{1,0:T(8,128)(2,1)S(1)} %collective-permute-done.7), dimensions={1,2} | broadcast | bytes 2228224 | tf_op jit(solution)/shard_map/broadcast_in_dim | solution.py:387
  29.0 9.5 %all-to-all-start.1 = ((bf16[16,256,256]{2,1,0:T(8,128)(2,1)}), bf16[16,256,256]{2,1,0:T(8,128)(2,1)S(1)}, u32[]{:S(2)}, u32[]{:S(2)}) async-start(bf16[16,256,256]{2,1,0:T(8,128)(2,1)} %broadcast_in_dim.7), calls=%async_computation.1 | async-start | bytes 4194304 | tf_op jit(solution)/shard_map/all_to_all | solution.py:387
  38.4 2.2 %collective-permute-start.3 = (bf16[512,256]{1,0:T(8,128)(2,1)S(1)}, bf16[512,256]{1,0:T(8,128)(2,1)S(1)}, u32[]{:S(2)}, u32[]{:S(2)}) collective-permute-start(bf16[512,256]{1,0:T(8,128)(2,1)S(1)} %copy-done.6), channel_id=1, source_target_pairs={{0,1},{1,2},{2,3},{3,4},{4,5},{5,6},{6,7},{7,0},{8,9},{9,10},{10,1... | collective-permute-start | bytes 786440 | tf_op jit(solution)/shard_map/ppermute | solution.py:373
  40.6 2.6 %collective-permute-start = (bf16[512,256]{1,0:T(8,128)(2,1)S(1)}, bf16[512,256]{1,0:T(8,128)(2,1)S(1)}, u32[]{:S(2)}, u32[]{:S(2)}) collective-permute-start(bf16[512,256]{1,0:T(8,128)(2,1)S(1)} %copy-done.6), channel_id=1, source_target_pairs={{1,0},{2,1},{3,2},{4,3},{5,4},{6,5},{7,6},{0,7},{9,8},{10,9},{11,1... | collective-permute-start | bytes 786440 | tf_op jit(solution)/shard_map/ppermute | solution.py:373
  43.2 1.9 %collective-permute-start.15 = (bf16[512,256]{1,0:T(8,128)(2,1)S(1)}, bf16[512,256]{1,0:T(8,128)(2,1)S(1)}, u32[]{:S(2)}, u32[]{:S(2)}) collective-permute-start(bf16[512,256]{1,0:T(8,128)(2,1)S(1)} %copy-done), channel_id=1, source_target_pairs={{1,0},{2,1},{3,2},{4,3},{5,4},{6,5},{7,6},{0,7},{9,8},{10,9},{11,1... | collective-permute-start | bytes 786440 | tf_op jit(solution)/shard_map/ppermute | solution.py:373
  45.1 0.1 collective-permute-start.19
  45.2 5.0 %collective-permute-done.3.refs_7_ = bf16[512,256]{1,0:T(8,128)(2,1)S(1)} collective-permute-done((bf16[512,256]{1,0:T(8,128)(2,1)S(1)}, bf16[512,256]{1,0:T(8,128)(2,1)S(1)}, u32[]{:S(2)}, u32[]{:S(2)}) %collective-permute-start.3) | collective-permute-done | bytes 262176 | tf_op jit(solution)/shard_map/ppermute | solution.py:373
  50.2 0.0 collective-permute-start.4
  50.2 0.0 collective-permute-done.refs_1_
  50.2 3.3 %collective-permute-start.1 = (bf16[512,256]{1,0:T(8,128)(2,1)S(1)}, bf16[512,256]{1,0:T(8,128)(2,1)}, u32[]{:S(2)}, u32[]{:S(2)}) collective-permute-start(bf16[512,256]{1,0:T(8,128)(2,1)S(1)} %collective-permute-done.refs_1_), channel_id=1, source_target_pairs={{1,0},{2,1},{3,2},{4,3},{5,4},{6,5},{7,6},{0,7},{9,8},{10,9},{11,1... | collective-permute-start | bytes 786440 | tf_op jit(solution)/shard_map/ppermute | solution.py:373
  53.5 3.5 %gate.3.refs_0_ = bf16[512,256]{1,0:T(8,128)(2,1)} custom-call(bf16[3,1536,256]{2,1,0:T(8,128)(2,1)} %refs_1_.3, bf16[3,1536,256]{2,1,0:T(8,128)(2,1)} %refs_1_.3, f32[3,3,256]{2,1,0:T(4,128)} %refs_2_.3, f32[2,16,256]{2,1,0:T(8,128)} %get-tuple-element.31.refs_3_, f32[1,256]{1,0:T(1,128)} %bitcast.12, f32[1536,256]{1,0:T(8,128)} %get-tuple-element.32.refs_5_, ...), custom_call_target="tpu_custom_call" | custom-call | flops 4000000000 | bytes 4000000 | tf_op jit(solution)/shard_map/gate/pallas_call | solution.py:345
  57.0 0.1 collective-permute-start.8
  57.1 0.0 collective-permute-done.19.refs_7_
  57.1 3.2 %collective-permute-start.11 = (bf16[512,256]{1,0:T(8,128)(2,1)}, bf16[512,256]{1,0:T(8,128)(2,1)S(1)}, u32[]{:S(2)}, u32[]{:S(2)}) collective-permute-start(bf16[512,256]{1,0:T(8,128)(2,1)} %gate.3.refs_0_), channel_id=1, source_target_pairs={{1,0},{2,1},{3,2},{4,3},{5,4},{6,5},{7,6},{0,7},{9,8},{10,9},{11,1... | collective-permute-start | bytes 786440 | tf_op jit(solution)/shard_map/ppermute | solution.py:373
  60.3 1.2 collective-permute-done.4.refs_6_
  61.5 2.1 %collective-permute-start.16 = (bf16[512,256]{1,0:T(8,128)(2,1)S(1)}, bf16[512,256]{1,0:T(8,128)(2,1)}, u32[]{:S(2)}, u32[]{:S(2)}) collective-permute-start(bf16[512,256]{1,0:T(8,128)(2,1)S(1)} %collective-permute-done.15.refs_1_), channel_id=1, source_target_pairs={{1,0},{2,1},{3,2},{4,3},{5,4},{6,5},{7,6},{0,7},{9,8},{10,9},{11,1... | collective-permute-start | bytes 786440 | tf_op jit(solution)/shard_map/ppermute | solution.py:373
  63.6 4.2 %collective-permute-done.8.refs_8_ = bf16[512,256]{1,0:T(8,128)(2,1)S(1)} collective-permute-done((bf16[512,256]{1,0:T(8,128)(2,1)}, bf16[512,256]{1,0:T(8,128)(2,1)S(1)}, u32[]{:S(2)}, u32[]{:S(2)}) %collective-permute-start.8) | collective-permute-done | bytes 262176 | tf_op jit(solution)/shard_map/ppermute | solution.py:373
  67.8 1.3 %collective-permute-start.2 = (bf16[512,256]{1,0:T(8,128)(2,1)}, bf16[512,256]{1,0:T(8,128)(2,1)}, u32[]{:S(2)}, u32[]{:S(2)}) collective-permute-start(bf16[512,256]{1,0:T(8,128)(2,1)} %collective-permute-done.1.refs_2_), channel_id=1, source_target_pairs={{1,0},{2,1},{3,2},{4,3},{5,4},{6,5},{7,6},{0,7},{9,8},{10,9},{11,1... | collective-permute-start | bytes 786440 | tf_op jit(solution)/shard_map/ppermute | solution.py:373
  69.1 0.0 collective-permute-done.11.refs_1_
  69.1 0.7 collective-permute-start.9
  69.8 0.7 copy-done.2
  70.5 2.9 %collective-permute-done.20.refs_6_ = bf16[512,256]{1,0:T(8,128)(2,1)S(1)} collective-permute-done((bf16[512,256]{1,0:T(8,128)(2,1)S(1)}, bf16[512,256]{1,0:T(8,128)(2,1)S(1)}, u32[]{:S(2)}, u32[]{:S(2)}) %collective-permute-start.20) | collective-permute-done | bytes 262176 | tf_op jit(solution)/shard_map/ppermute | solution.py:373
  73.4 1.3 %collective-permute-start.12 = (bf16[512,256]{1,0:T(8,128)(2,1)S(1)}, bf16[512,256]{1,0:T(8,128)(2,1)}, u32[]{:S(2)}, u32[]{:S(2)}) collective-permute-start(bf16[512,256]{1,0:T(8,128)(2,1)S(1)} %collective-permute-done.11.refs_1_), channel_id=1, source_target_pairs={{1,0},{2,1},{3,2},{4,3},{5,4},{6,5},{7,6},{0,7},{9,8},{10,9},{11,1... | collective-permute-start | bytes 786440 | tf_op jit(solution)/shard_map/ppermute | solution.py:373
  74.7 0.7 copy-done.4
  75.4 1.3 %collective-permute-start.17 = (bf16[512,256]{1,0:T(8,128)(2,1)}, bf16[512,256]{1,0:T(8,128)(2,1)}, u32[]{:S(2)}, u32[]{:S(2)}) collective-permute-start(bf16[512,256]{1,0:T(8,128)(2,1)} %collective-permute-done.16.refs_2_), channel_id=1, source_target_pairs={{1,0},{2,1},{3,2},{4,3},{5,4},{6,5},{7,6},{0,7},{9,8},{10,9},{11,1... | collective-permute-start | bytes 786440 | tf_op jit(solution)/shard_map/ppermute | solution.py:373
  76.7 2.4 %collective-permute-done.5.refs_5_ = bf16[512,256]{1,0:T(8,128)(2,1)} collective-permute-done((bf16[512,256]{1,0:T(8,128)(2,1)}, bf16[512,256]{1,0:T(8,128)(2,1)}, u32[]{:S(2)}, u32[]{:S(2)}) %collective-permute-start.5) | collective-permute-done | bytes 262176 | tf_op jit(solution)/shard_map/ppermute | solution.py:373
  79.1 0.0 collective-permute-start.21
  79.1 5.6 %collective-permute-done.9.refs_7_ = bf16[512,256]{1,0:T(8,128)(2,1)} collective-permute-done((bf16[512,256]{1,0:T(8,128)(2,1)S(1)}, bf16[512,256]{1,0:T(8,128)(2,1)}, u32[]{:S(2)}, u32[]{:S(2)}) %collective-permute-start.9) | collective-permute-done | bytes 262176 | tf_op jit(solution)/shard_map/ppermute | solution.py:373
  84.7 0.0 collective-permute-start.10
  84.7 0.0 collective-permute-done.12.refs_2_
  84.7 3.2 %collective-permute-start.13 = (bf16[512,256]{1,0:T(8,128)(2,1)}, bf16[512,256]{1,0:T(8,128)(2,1)S(1)}, u32[]{:S(2)}, u32[]{:S(2)}) collective-permute-start(bf16[512,256]{1,0:T(8,128)(2,1)} %collective-permute-done.12.refs_2_), channel_id=1, source_target_pairs={{1,0},{2,1},{3,2},{4,3},{5,4},{6,5},{7,6},{0,7},{9,8},{10,9},{11,1... | collective-permute-start | bytes 786440 | tf_op jit(solution)/shard_map/ppermute | solution.py:373
  88.0 1.9 %collective-permute-done.17.refs_3_ = bf16[512,256]{1,0:T(8,128)(2,1)} collective-permute-done((bf16[512,256]{1,0:T(8,128)(2,1)}, bf16[512,256]{1,0:T(8,128)(2,1)}, u32[]{:S(2)}, u32[]{:S(2)}) %collective-permute-start.17) | collective-permute-done | bytes 262176 | tf_op jit(solution)/shard_map/ppermute | solution.py:373
  89.9 3.7 %collective-permute-start.18 = (bf16[512,256]{1,0:T(8,128)(2,1)}, bf16[512,256]{1,0:T(8,128)(2,1)}, u32[]{:S(2)}, u32[]{:S(2)}) collective-permute-start(bf16[512,256]{1,0:T(8,128)(2,1)} %collective-permute-done.17.refs_3_), channel_id=1, source_target_pairs={{1,0},{2,1},{3,2},{4,3},{5,4},{6,5},{7,6},{0,7},{9,8},{10,9},{11,1... | collective-permute-start | bytes 786440 | tf_op jit(solution)/shard_map/ppermute | solution.py:373
  93.6 0.0 collective-permute-done.6.refs_4_
  93.6 0.0 all-to-all-done.1
  93.6 0.9 copy-done.7
  94.5 0.9 copy-done.9
  95.5 0.9 copy-done.11
  96.4 2.7 %project.3 = (f32[512,256]{1,0:T(8,128)S(1)}, bf16[512,256]{1,0:T(8,128)(2,1)S(1)}) custom-call(s32[1]{0:T(128)} %bitcast.place_ref, bf16[512,256]{1,0:T(8,128)(2,1)S(1)} %copy-done.7, bf16[512,256]{1,0:T(8,128)(2,1)S(1)} %copy-done.11, bf16[512,256]{1,0:T(8,128)(2,1)} %collective-permute-done.1.refs_2_, bf16[512,256]{1,0:T(8,128)(2,1)} %collective-permute-done.2.refs_3_, ...), custom_call_target="tpu_custom_call" | custom-call | flops 4000000000 | bytes 4000000 | tf_op jit(solution)/shard_map/project/pallas_call | solution.py:398
  99.1 1.1 collective-permute-done.10.refs_6_
  100.2 0.7 collective-permute-start.14
  100.9 1.8 %collective-permute-start.23 = (bf16[256,256]{1,0:T(8,128)(2,1)S(1)}, bf16[256,256]{1,0:T(8,128)(2,1)S(1)}, u32[]{:S(2)}, u32[]{:S(2)}) collective-permute-start(bf16[256,256]{1,0:T(8,128)(2,1)S(1)} %slice.6), channel_id=1, source_target_pairs={{1,0},{2,1},{3,2},{4,3},{5,4},{6,5},{7,6},{0,7},{9,8},{10,9},{11,1... | collective-permute-start | bytes 393224 | tf_op jit(solution)/shard_map/ppermute | solution.py:373
  102.8 0.0 copy-start.5
  102.8 0.4 collective-permute-start.24
  103.2 0.0 collective-permute-done.21.refs_5_
  103.2 0.0 collective-permute-done.18.refs_4_
  103.2 2.6 %project.4 = (f32[512,256]{1,0:T(8,128)S(1)}, bf16[512,256]{1,0:T(8,128)(2,1)S(1)}) custom-call(s32[1]{0:T(128)} %bitcast.place_ref, bf16[512,256]{1,0:T(8,128)(2,1)S(1)} %copy-done, bf16[512,256]{1,0:T(8,128)(2,1)S(1)} %collective-permute-done.15.refs_1_, bf16[512,256]{1,0:T(8,128)(2,1)} %collective-permute-done.16.refs_2_, ...), custom_call_target="tpu_custom_call" | custom-call | flops 4000000000 | bytes 4000000 | tf_op jit(solution)/shard_map/project/pallas_call | solution.py:398
  105.8 1.4 %collective-permute-start.22 = (bf16[512,256]{1,0:T(8,128)(2,1)S(1)}, bf16[512,256]{1,0:T(8,128)(2,1)S(1)}, u32[]{:S(2)}, u32[]{:S(2)}) collective-permute-start(bf16[512,256]{1,0:T(8,128)(2,1)S(1)} %get-tuple-element.50), channel_id=1, source_target_pairs={{0,8},{1,9},{2,10},{3,11},{4,12},{5,13},{6,14},{7,15},{8,0},{9,1},... | collective-permute-start | bytes 786440 | tf_op jit(solution)/shard_map/ppermute | solution.py:414
  107.2 1.8 %collective-permute-done.24.refs_5_ = bf16[256,256]{1,0:T(8,128)(2,1)S(1)} collective-permute-done((bf16[256,256]{1,0:T(8,128)(2,1)S(1)}, bf16[256,256]{1,0:T(8,128)(2,1)S(1)}, u32[]{:S(2)}, u32[]{:S(2)}) %collective-permute-start.24) | collective-permute-done | bytes 131104 | tf_op jit(solution)/shard_map/ppermute | solution.py:373
  109.1 2.5 %project.5 = (f32[512,256]{1,0:T(8,128)S(1)}, bf16[512,256]{1,0:T(8,128)(2,1)S(1)}) custom-call(s32[1]{0:T(128)} %bitcast.place_ref, bf16[512,256]{1,0:T(8,128)(2,1)S(1)} %copy-done.1, bf16[512,256]{1,0:T(8,128)(2,1)S(1)} %copy-done.5, bf16[512,256]{1,0:T(8,128)(2,1)} %collective-permute-done.12.refs_2_, ...), custom_call_target="tpu_custom_call" | custom-call | flops 4000000000 | bytes 4000000 | tf_op jit(solution)/shard_map/project/pallas_call | solution.py:398
  111.5 1.4 %collective-permute-start.25 = (bf16[512,256]{1,0:T(8,128)(2,1)S(1)}, bf16[512,256]{1,0:T(8,128)(2,1)S(1)}, u32[]{:S(2)}, u32[]{:S(2)}) collective-permute-start(bf16[512,256]{1,0:T(8,128)(2,1)S(1)} %get-tuple-element.54), channel_id=1, source_target_pairs={{0,8},{1,9},{2,10},{3,11},{4,12},{5,13},{6,14},{7,15},{8,0},{9,1},... | collective-permute-start | bytes 786440 | tf_op jit(solution)/shard_map/ppermute | solution.py:414
  113.0 0.1 add_convert_fusion.2
  113.0 0.9 collective-permute-done.22
  114.0 0.1 add_convert_fusion.1
  114.0 4.6 %collective-permute-done.25 = bf16[512,256]{1,0:T(8,128)(2,1)S(1)} collective-permute-done((bf16[512,256]{1,0:T(8,128)(2,1)S(1)}, bf16[512,256]{1,0:T(8,128)(2,1)S(1)}, u32[]{:S(2)}, u32[]{:S(2)}) %collective-permute-start.25) | collective-permute-done | bytes 262176 | tf_op jit(solution)/shard_map/ppermute | solution.py:414
  118.6 0.1 add_convert_fusion
  118.7 0.9 pad_maximum_fusion
  (37 shorter events, 0.1 us)
Async XLA Ops:
  0.0 12.7 %copy-start.15 = (bf16[256,256]{1,0:T(8,128)(2,1)S(1)}, bf16[256,256]{1,0:T(8,128)(2,1)}, u32[]{:S(2)}) copy-start(bf16[256,256]{1,0:T(8,128)(2,1)} %param.11) | copy-start | bytes 393220
  5.2 15.3 %all-to-all-start = ((bf16[16,48,256]{2,1,0:T(8,128)(2,1)}), bf16[16,48,256]{2,1,0:T(8,128)(2,1)S(1)}, u32[]{:S(2)}, u32[]{:S(2)}) async-start(bf16[16,48,256]{2,1,0:T(8,128)(2,1)} %get-tuple-element.35), calls=%async_computation | async-start | bytes 786432 | tf_op jit(solution)/shard_map/all_to_all | solution.py:320
  12.7 14.7 %collective-permute-start.7 = (bf16[256,256]{1,0:T(8,128)(2,1)S(1)}, bf16[256,256]{1,0:T(8,128)(2,1)S(1)}, u32[]{:S(2)}, u32[]{:S(2)}) collective-permute-start(bf16[256,256]{1,0:T(8,128)(2,1)S(1)} %copy-done.15), channel_id=1, source_target_pairs={{0,0},{1,16},{2,32},{3,48},{4,64},{5,80},{6,96},{7,112},{8,8},{9,2... | collective-permute-start | bytes 393224 | tf_op jit(solution)/shard_map/ppermute | solution.py:319
  20.5 0.7 copy-start.14
  29.0 9.5 %copy-start.6 = (bf16[512,256]{1,0:T(8,128)(2,1)S(1)}, bf16[512,256]{1,0:T(8,128)(2,1)}, u32[]{:S(2)}) copy-start(bf16[512,256]{1,0:T(8,128)(2,1)} %get-tuple-element.36.refs_0_) | copy-start | bytes 786436
  29.0 14.2 %copy-start = (bf16[512,256]{1,0:T(8,128)(2,1)S(1)}, bf16[512,256]{1,0:T(8,128)(2,1)}, u32[]{:S(2)}) copy-start(bf16[512,256]{1,0:T(8,128)(2,1)} %get-tuple-element.48.refs_0_) | copy-start | bytes 786436
  29.0 64.6 %all-to-all-start.1 = ((bf16[16,256,256]{2,1,0:T(8,128)(2,1)}), bf16[16,256,256]{2,1,0:T(8,128)(2,1)S(1)}, u32[]{:S(2)}, u32[]{:S(2)}) async-start(bf16[16,256,256]{2,1,0:T(8,128)(2,1)} %broadcast_in_dim.7), calls=%async_computation.1 | async-start | bytes 4194304 | tf_op jit(solution)/shard_map/all_to_all | solution.py:387
  38.4 11.7 %collective-permute-start.3 = (bf16[512,256]{1,0:T(8,128)(2,1)S(1)}, bf16[512,256]{1,0:T(8,128)(2,1)S(1)}, u32[]{:S(2)}, u32[]{:S(2)}) collective-permute-start(bf16[512,256]{1,0:T(8,128)(2,1)S(1)} %copy-done.6), channel_id=1, source_target_pairs={{0,1},{1,2},{2,3},{3,4},{4,5},{5,6},{6,7},{7,0},{8,9},{9,10},{10,1... | collective-permute-start | bytes 786440 | tf_op jit(solution)/shard_map/ppermute | solution.py:373
  40.6 9.6 %collective-permute-start = (bf16[512,256]{1,0:T(8,128)(2,1)S(1)}, bf16[512,256]{1,0:T(8,128)(2,1)S(1)}, u32[]{:S(2)}, u32[]{:S(2)}) collective-permute-start(bf16[512,256]{1,0:T(8,128)(2,1)S(1)} %copy-done.6), channel_id=1, source_target_pairs={{1,0},{2,1},{3,2},{4,3},{5,4},{6,5},{7,6},{0,7},{9,8},{10,9},{11,1... | collective-permute-start | bytes 786440 | tf_op jit(solution)/shard_map/ppermute | solution.py:373
  43.2 17.2 %collective-permute-start.15 = (bf16[512,256]{1,0:T(8,128)(2,1)S(1)}, bf16[512,256]{1,0:T(8,128)(2,1)S(1)}, u32[]{:S(2)}, u32[]{:S(2)}) collective-permute-start(bf16[512,256]{1,0:T(8,128)(2,1)S(1)} %copy-done), channel_id=1, source_target_pairs={{1,0},{2,1},{3,2},{4,3},{5,4},{6,5},{7,6},{0,7},{9,8},{10,9},{11,1... | collective-permute-start | bytes 786440 | tf_op jit(solution)/shard_map/ppermute | solution.py:373
  45.1 12.0 %collective-permute-start.19 = (bf16[512,256]{1,0:T(8,128)(2,1)S(1)}, bf16[512,256]{1,0:T(8,128)(2,1)S(1)}, u32[]{:S(2)}, u32[]{:S(2)}) collective-permute-start(bf16[512,256]{1,0:T(8,128)(2,1)S(1)} %copy-done), channel_id=1, source_target_pairs={{0,1},{1,2},{2,3},{3,4},{4,5},{5,6},{6,7},{7,0},{8,9},{9,10},{10,1... | collective-permute-start | bytes 786440 | tf_op jit(solution)/shard_map/ppermute | solution.py:373
  50.2 6.8 %copy-start.8 = (bf16[512,256]{1,0:T(8,128)(2,1)}, bf16[512,256]{1,0:T(8,128)(2,1)S(1)}, u32[]{:S(2)}) copy-start(bf16[512,256]{1,0:T(8,128)(2,1)S(1)} %collective-permute-done.3.refs_7_) | copy-start | bytes 786436
  50.2 11.3 %collective-permute-start.4 = (bf16[512,256]{1,0:T(8,128)(2,1)S(1)}, bf16[512,256]{1,0:T(8,128)(2,1)}, u32[]{:S(2)}, u32[]{:S(2)}) collective-permute-start(bf16[512,256]{1,0:T(8,128)(2,1)S(1)} %collective-permute-done.3.refs_7_), channel_id=1, source_target_pairs={{0,1},{1,2},{2,3},{3,4},{4,5},{5,6},{6,7},{7,0},{8,9},{9,10},{10,1... | collective-permute-start | bytes 786440 | tf_op jit(solution)/shard_map/ppermute | solution.py:373
  50.2 6.8 %copy-start.10 = (bf16[512,256]{1,0:T(8,128)(2,1)}, bf16[512,256]{1,0:T(8,128)(2,1)S(1)}, u32[]{:S(2)}) copy-start(bf16[512,256]{1,0:T(8,128)(2,1)S(1)} %collective-permute-done.refs_1_) | copy-start | bytes 786436
  50.2 13.4 %collective-permute-start.1 = (bf16[512,256]{1,0:T(8,128)(2,1)S(1)}, bf16[512,256]{1,0:T(8,128)(2,1)}, u32[]{:S(2)}, u32[]{:S(2)}) collective-permute-start(bf16[512,256]{1,0:T(8,128)(2,1)S(1)} %collective-permute-done.refs_1_), channel_id=1, source_target_pairs={{1,0},{2,1},{3,2},{4,3},{5,4},{6,5},{7,6},{0,7},{9,8},{10,9},{11,1... | collective-permute-start | bytes 786440 | tf_op jit(solution)/shard_map/ppermute | solution.py:373
  57.0 10.7 %collective-permute-start.8 = (bf16[512,256]{1,0:T(8,128)(2,1)}, bf16[512,256]{1,0:T(8,128)(2,1)S(1)}, u32[]{:S(2)}, u32[]{:S(2)}) collective-permute-start(bf16[512,256]{1,0:T(8,128)(2,1)} %gate.3.refs_0_), channel_id=1, source_target_pairs={{0,1},{1,2},{2,3},{3,4},{4,5},{5,6},{6,7},{7,0},{8,9},{9,10},{10,1... | collective-permute-start | bytes 786440 | tf_op jit(solution)/shard_map/ppermute | solution.py:373
  57.1 12.0 %collective-permute-start.11 = (bf16[512,256]{1,0:T(8,128)(2,1)}, bf16[512,256]{1,0:T(8,128)(2,1)S(1)}, u32[]{:S(2)}, u32[]{:S(2)}) collective-permute-start(bf16[512,256]{1,0:T(8,128)(2,1)} %gate.3.refs_0_), channel_id=1, source_target_pairs={{1,0},{2,1},{3,2},{4,3},{5,4},{6,5},{7,6},{0,7},{9,8},{10,9},{11,1... | collective-permute-start | bytes 786440 | tf_op jit(solution)/shard_map/ppermute | solution.py:373
  60.3 13.0 %collective-permute-start.20 = (bf16[512,256]{1,0:T(8,128)(2,1)S(1)}, bf16[512,256]{1,0:T(8,128)(2,1)S(1)}, u32[]{:S(2)}, u32[]{:S(2)}) collective-permute-start(bf16[512,256]{1,0:T(8,128)(2,1)S(1)} %collective-permute-done.19.refs_7_), channel_id=1, source_target_pairs={{0,1},{1,2},{2,3},{3,4},{4,5},{5,6},{6,7},{7,0},{8,9},{9,10},{10,1... | collective-permute-start | bytes 786440 | tf_op jit(solution)/shard_map/ppermute | solution.py:373
  61.5 13.9 %collective-permute-start.16 = (bf16[512,256]{1,0:T(8,128)(2,1)S(1)}, bf16[512,256]{1,0:T(8,128)(2,1)}, u32[]{:S(2)}, u32[]{:S(2)}) collective-permute-start(bf16[512,256]{1,0:T(8,128)(2,1)S(1)} %collective-permute-done.15.refs_1_), channel_id=1, source_target_pairs={{1,0},{2,1},{3,2},{4,3},{5,4},{6,5},{7,6},{0,7},{9,8},{10,9},{11,1... | collective-permute-start | bytes 786440 | tf_op jit(solution)/shard_map/ppermute | solution.py:373
  63.6 15.5 %collective-permute-start.5 = (bf16[512,256]{1,0:T(8,128)(2,1)}, bf16[512,256]{1,0:T(8,128)(2,1)}, u32[]{:S(2)}, u32[]{:S(2)}) collective-permute-start(bf16[512,256]{1,0:T(8,128)(2,1)} %collective-permute-done.4.refs_6_), channel_id=1, source_target_pairs={{0,1},{1,2},{2,3},{3,4},{4,5},{5,6},{6,7},{7,0},{8,9},{9,10},{10,1... | collective-permute-start | bytes 786440 | tf_op jit(solution)/shard_map/ppermute | solution.py:373
  67.8 11.3 %collective-permute-start.2 = (bf16[512,256]{1,0:T(8,128)(2,1)}, bf16[512,256]{1,0:T(8,128)(2,1)}, u32[]{:S(2)}, u32[]{:S(2)}) collective-permute-start(bf16[512,256]{1,0:T(8,128)(2,1)} %collective-permute-done.1.refs_2_), channel_id=1, source_target_pairs={{1,0},{2,1},{3,2},{4,3},{5,4},{6,5},{7,6},{0,7},{9,8},{10,9},{11,1... | collective-permute-start | bytes 786440 | tf_op jit(solution)/shard_map/ppermute | solution.py:373
  69.1 15.6 %collective-permute-start.9 = (bf16[512,256]{1,0:T(8,128)(2,1)S(1)}, bf16[512,256]{1,0:T(8,128)(2,1)}, u32[]{:S(2)}, u32[]{:S(2)}) collective-permute-start(bf16[512,256]{1,0:T(8,128)(2,1)S(1)} %collective-permute-done.8.refs_8_), channel_id=1, source_target_pairs={{0,1},{1,2},{2,3},{3,4},{4,5},{5,6},{6,7},{7,0},{8,9},{9,10},{10,1... | collective-permute-start | bytes 786440 | tf_op jit(solution)/shard_map/ppermute | solution.py:373
  69.8 0.7 copy-start.2
  73.4 2.0 %copy-start.12 = (bf16[512,256]{1,0:T(8,128)(2,1)}, bf16[512,256]{1,0:T(8,128)(2,1)S(1)}, u32[]{:S(2)}) copy-start(bf16[512,256]{1,0:T(8,128)(2,1)S(1)} %collective-permute-done.20.refs_6_) | copy-start | bytes 786436
  73.4 11.3 %collective-permute-start.12 = (bf16[512,256]{1,0:T(8,128)(2,1)S(1)}, bf16[512,256]{1,0:T(8,128)(2,1)}, u32[]{:S(2)}, u32[]{:S(2)}) collective-permute-start(bf16[512,256]{1,0:T(8,128)(2,1)S(1)} %collective-permute-done.11.refs_1_), channel_id=1, source_target_pairs={{1,0},{2,1},{3,2},{4,3},{5,4},{6,5},{7,6},{0,7},{9,8},{10,9},{11,1... | collective-permute-start | bytes 786440 | tf_op jit(solution)/shard_map/ppermute | solution.py:373
  74.7 0.7 copy-start.4
  75.4 14.5 %collective-permute-start.17 = (bf16[512,256]{1,0:T(8,128)(2,1)}, bf16[512,256]{1,0:T(8,128)(2,1)}, u32[]{:S(2)}, u32[]{:S(2)}) collective-permute-start(bf16[512,256]{1,0:T(8,128)(2,1)} %collective-permute-done.16.refs_2_), channel_id=1, source_target_pairs={{1,0},{2,1},{3,2},{4,3},{5,4},{6,5},{7,6},{0,7},{9,8},{10,9},{11,1... | collective-permute-start | bytes 786440 | tf_op jit(solution)/shard_map/ppermute | solution.py:373
  79.1 14.5 %collective-permute-start.6 = (bf16[512,256]{1,0:T(8,128)(2,1)}, bf16[512,256]{1,0:T(8,128)(2,1)}, u32[]{:S(2)}, u32[]{:S(2)}) collective-permute-start(bf16[512,256]{1,0:T(8,128)(2,1)} %collective-permute-done.5.refs_5_), channel_id=1, source_target_pairs={{0,1},{1,2},{2,3},{3,4},{4,5},{5,6},{6,7},{7,0},{8,9},{9,10},{10,1... | collective-permute-start | bytes 786440 | tf_op jit(solution)/shard_map/ppermute | solution.py:373
  79.1 24.1 %collective-permute-start.21 = (bf16[512,256]{1,0:T(8,128)(2,1)}, bf16[512,256]{1,0:T(8,128)(2,1)}, u32[]{:S(2)}, u32[]{:S(2)}) collective-permute-start(bf16[512,256]{1,0:T(8,128)(2,1)} %copy-done.12), channel_id=1, source_target_pairs={{0,1},{1,2},{2,3},{3,4},{4,5},{5,6},{6,7},{7,0},{8,9},{9,10},{10,1... | collective-permute-start | bytes 786440 | tf_op jit(solution)/shard_map/ppermute | solution.py:373
  84.7 15.5 %collective-permute-start.10 = (bf16[512,256]{1,0:T(8,128)(2,1)}, bf16[512,256]{1,0:T(8,128)(2,1)S(1)}, u32[]{:S(2)}, u32[]{:S(2)}) collective-permute-start(bf16[512,256]{1,0:T(8,128)(2,1)} %collective-permute-done.9.refs_7_), channel_id=1, source_target_pairs={{0,1},{1,2},{2,3},{3,4},{4,5},{5,6},{6,7},{7,0},{8,9},{9,10},{10,1... | collective-permute-start | bytes 786440 | tf_op jit(solution)/shard_map/ppermute | solution.py:373
  84.7 15.5 %collective-permute-start.13 = (bf16[512,256]{1,0:T(8,128)(2,1)}, bf16[512,256]{1,0:T(8,128)(2,1)S(1)}, u32[]{:S(2)}, u32[]{:S(2)}) collective-permute-start(bf16[512,256]{1,0:T(8,128)(2,1)} %collective-permute-done.12.refs_2_), channel_id=1, source_target_pairs={{1,0},{2,1},{3,2},{4,3},{5,4},{6,5},{7,6},{0,7},{9,8},{10,9},{11,1... | collective-permute-start | bytes 786440 | tf_op jit(solution)/shard_map/ppermute | solution.py:373
  89.9 13.3 %collective-permute-start.18 = (bf16[512,256]{1,0:T(8,128)(2,1)}, bf16[512,256]{1,0:T(8,128)(2,1)}, u32[]{:S(2)}, u32[]{:S(2)}) collective-permute-start(bf16[512,256]{1,0:T(8,128)(2,1)} %collective-permute-done.17.refs_3_), channel_id=1, source_target_pairs={{1,0},{2,1},{3,2},{4,3},{5,4},{6,5},{7,6},{0,7},{9,8},{10,9},{11,1... | collective-permute-start | bytes 786440 | tf_op jit(solution)/shard_map/ppermute | solution.py:373
  93.6 1.0 copy-start.7
  94.5 0.9 copy-start.9
  95.5 0.9 copy-start.11
  96.4 6.7 %copy-start.13 = (bf16[512,256]{1,0:T(8,128)(2,1)S(1)}, bf16[512,256]{1,0:T(8,128)(2,1)}, u32[]{:S(2)}) copy-start(bf16[512,256]{1,0:T(8,128)(2,1)} %copy-done.12) | copy-start | bytes 786436
  100.2 12.7 %collective-permute-start.14 = (bf16[512,256]{1,0:T(8,128)(2,1)S(1)}, bf16[512,256]{1,0:T(8,128)(2,1)S(1)}, u32[]{:S(2)}, u32[]{:S(2)}) collective-permute-start(bf16[512,256]{1,0:T(8,128)(2,1)S(1)} %get-tuple-element.47), channel_id=1, source_target_pairs={{0,8},{1,9},{2,10},{3,11},{4,12},{5,13},{6,14},{7,15},{8,0},{9,1},... | collective-permute-start | bytes 786440 | tf_op jit(solution)/shard_map/ppermute | solution.py:414
  100.9 6.3 %collective-permute-start.23 = (bf16[256,256]{1,0:T(8,128)(2,1)S(1)}, bf16[256,256]{1,0:T(8,128)(2,1)S(1)}, u32[]{:S(2)}, u32[]{:S(2)}) collective-permute-start(bf16[256,256]{1,0:T(8,128)(2,1)S(1)} %slice.6), channel_id=1, source_target_pairs={{1,0},{2,1},{3,2},{4,3},{5,4},{6,5},{7,6},{0,7},{9,8},{10,9},{11,1... | collective-permute-start | bytes 393224 | tf_op jit(solution)/shard_map/ppermute | solution.py:373
  102.8 6.3 %copy-start.1 = (bf16[512,256]{1,0:T(8,128)(2,1)S(1)}, bf16[512,256]{1,0:T(8,128)(2,1)}, u32[]{:S(2)}) copy-start(bf16[512,256]{1,0:T(8,128)(2,1)} %gate.3.refs_0_) | copy-start | bytes 786436
  102.8 6.3 %copy-start.3 = (bf16[512,256]{1,0:T(8,128)(2,1)S(1)}, bf16[512,256]{1,0:T(8,128)(2,1)}, u32[]{:S(2)}) copy-start(bf16[512,256]{1,0:T(8,128)(2,1)} %copy-done.2) | copy-start | bytes 786436
  102.8 6.3 %copy-start.5 = (bf16[512,256]{1,0:T(8,128)(2,1)S(1)}, bf16[512,256]{1,0:T(8,128)(2,1)}, u32[]{:S(2)}) copy-start(bf16[512,256]{1,0:T(8,128)(2,1)} %copy-done.4) | copy-start | bytes 786436
  102.8 6.3 %collective-permute-start.24 = (bf16[256,256]{1,0:T(8,128)(2,1)S(1)}, bf16[256,256]{1,0:T(8,128)(2,1)S(1)}, u32[]{:S(2)}, u32[]{:S(2)}) collective-permute-start(bf16[256,256]{1,0:T(8,128)(2,1)S(1)} %slice.7), channel_id=1, source_target_pairs={{0,1},{1,2},{2,3},{3,4},{4,5},{5,6},{6,7},{7,0},{8,9},{9,10},{10,1... | collective-permute-start | bytes 393224 | tf_op jit(solution)/shard_map/ppermute | solution.py:373
  105.8 8.2 %collective-permute-start.22 = (bf16[512,256]{1,0:T(8,128)(2,1)S(1)}, bf16[512,256]{1,0:T(8,128)(2,1)S(1)}, u32[]{:S(2)}, u32[]{:S(2)}) collective-permute-start(bf16[512,256]{1,0:T(8,128)(2,1)S(1)} %get-tuple-element.50), channel_id=1, source_target_pairs={{0,8},{1,9},{2,10},{3,11},{4,12},{5,13},{6,14},{7,15},{8,0},{9,1},... | collective-permute-start | bytes 786440 | tf_op jit(solution)/shard_map/ppermute | solution.py:414
  111.5 7.1 %collective-permute-start.25 = (bf16[512,256]{1,0:T(8,128)(2,1)S(1)}, bf16[512,256]{1,0:T(8,128)(2,1)S(1)}, u32[]{:S(2)}, u32[]{:S(2)}) collective-permute-start(bf16[512,256]{1,0:T(8,128)(2,1)S(1)} %get-tuple-element.54), channel_id=1, source_target_pairs={{0,8},{1,9},{2,10},{3,11},{4,12},{5,13},{6,14},{7,15},{8,0},{9,1},... | collective-permute-start | bytes 786440 | tf_op jit(solution)/shard_map/ppermute | solution.py:414

commit v5 on v4

--- a/solution.py
+++ b/solution.py
@@ -25,7 +25,6 @@
     ("hop", 0, 1, "ud"),
     ("hop", 1, 1, "ud"),
     ("hop", 0, 2, "ud"),
-    ("wait", 2, 1, 0, 1),
     ("hop", 2, 1, "ud"),
     ("hop", 1, 2, "ud"),
     ("hop", 0, 3, "ud"),

time: 120 us -> 120 us (level)
  waiting for transfers between devices: 33.1 us -> 30 us
  local copies, waits for them, and re-layouts: 6.61 us -> 9.64 us
    ppermute x22, waiting for transfers between devices: 26.1 us -> 21.9 us  [hop(): arrived[c, s, way] = lax.ppermute(block, 'ch', up if way == 'u' else down)]
    unnamed x32, local copies, waits for them, and re-layouts: 5.04 us -> 8.07 us
  transfers between devices with their start and end apart: 28 -> 28, of which waited for: 13 -> 11; matrix products, arithmetic and copies ran while one was open for 0% -> 0% of each run, Pallas kernels for 14% -> 14%
where the time goes in v5:
time: 120 us
  starting transfers between devices  56.5 us (47%)
  waiting for transfers between devices  30 us (25%)
  Pallas kernels  22.2 us (18%)
  local copies, waits for them, and re-layouts  9.64 us (8%)
    ppermute x22, starting transfers between devices, hop(): arrived[c, s, way] = lax.ppermute(block, 'ch', up if way == 'u' else down)  29.2 us
    ppermute x22, waiting for transfers between devices, hop(): arrived[c, s, way] = lax.ppermute(block, 'ch', up if way == 'u' else down)  21.9 us
    all_to_all x1, starting transfers between devices, weights(): w_all = lax.all_to_all(jnp.broadcast_to(w, (CTX, *w.shape)), 'ctx', 0, 0)  9.45 us
    pallas_call x2, Pallas kernels, gate(): pl.pallas_call(functools.partial(gate_kernel, group, tokens), grid=(tiles...  9.26 us
    unnamed x32, local copies, waits for them, and re-layouts  8.07 us
    pallas_call x3, Pallas kernels, project(): pl.pallas_call(project_kernel, grid=(2,), in_specs=[smem] + [tile] * 4 +...  7.73 us
    all_to_all x1, starting transfers between devices, local(): recv = lax.all_to_all(send, 'ctx', 0, 0)  7.48 us
    ppermute x1, starting transfers between devices, local(): w_block = lax.ppermute(w_block, ('ctx', 'ch'), swap)  6.69 us
  transfers between devices with their start and end apart: 28, of which 11 were waited for; matrix products, arithmetic and copies ran while one was open for 0% of the time, Pallas kernels for 14%

profile of v5, /device:TPU:2, one launch (start us, length us, event | category | flops | bytes accessed | tf_op | source)
XLA Modules:
  0.0 119.5 jit_solution(15595394912913605000)
XLA Ops:
  0.0 5.2 %states.1 = (f32[1536,256]{1,0:T(8,128)}, f32[3,16,8,256]{3,2,1,0:T(8,128)}, f32[3,16,256]{2,1,0:T(8,128)}, bf16[16,48,256]{2,1,0:T(8,128)(2,1)}, f32[2,16,256]{2,1,0:T(8,128)}) custom-call(bf16[3,1536,256]{2,1,0:T(8,128)(2,1)} %refs_1_.3, bf16[3,1536,256]{2,1,0:T(8,128)(2,1)} %refs_1_.3, bf16[3,1536,256]{2,1,0:T(8,128)(2,1)} %refs_1_.3, ...), custom_call_target="tpu_custom_call" | custom-call | flops 4000000000 | bytes 4000000 | tf_op jit(solution)/shard_map/states/pallas_call | solution.py:287
  5.2 7.5 %all-to-all-start = ((bf16[16,48,256]{2,1,0:T(8,128)(2,1)}), bf16[16,48,256]{2,1,0:T(8,128)(2,1)S(1)}, u32[]{:S(2)}, u32[]{:S(2)}) async-start(bf16[16,48,256]{2,1,0:T(8,128)(2,1)} %get-tuple-element.31), calls=%async_computation | async-start | bytes 786432 | tf_op jit(solution)/shard_map/all_to_all | solution.py:319
  12.7 6.7 %collective-permute-start.7 = (bf16[256,256]{1,0:T(8,128)(2,1)S(1)}, bf16[256,256]{1,0:T(8,128)(2,1)S(1)}, u32[]{:S(2)}, u32[]{:S(2)}) collective-permute-start(bf16[256,256]{1,0:T(8,128)(2,1)S(1)} %copy-done.15), channel_id=1, source_target_pairs={{0,0},{1,16},{2,32},{3,48},{4,64},{5,80},{6,96},{7,112},{8,8},{9,2... | collective-permute-start | bytes 393224 | tf_op jit(solution)/shard_map/ppermute | solution.py:318
  19.4 1.1 all-to-all-done.refs_8_
  20.5 0.7 copy-done.14
  21.3 5.7 %gate.2 = (bf16[512,256]{1,0:T(8,128)(2,1)}, bf16[512,256]{1,0:T(8,128)(2,1)}, f32[1,16,256]{2,1,0:T(8,128)}) custom-call(s32[1]{0:T(128)} %bitcast.1.refs_0_, bf16[3,1536,256]{2,1,0:T(8,128)(2,1)} %refs_1_.3, f32[3,3,256]{2,1,0:T(4,128)} %refs_2_.3, f32[2,16,256]{2,1,0:T(8,128)} %get-tuple-element.27.refs_3_, f32[1,256]{1,0:T(1,128)} %bitcast.11, ...), custom_call_target="tpu_custom_call" | custom-call | flops 4000000000 | bytes 4000000 | tf_op jit(solution)/shard_map/gate/pallas_call | solution.py:344
  27.0 0.4 collective-permute-done.7
  27.4 1.5 %broadcast_in_dim.7 = bf16[16,256,256]{2,1,0:T(8,128)(2,1)} broadcast(bf16[256,256]{1,0:T(8,128)(2,1)S(1)} %collective-permute-done.7), dimensions={1,2} | broadcast | bytes 2228224 | tf_op jit(solution)/shard_map/broadcast_in_dim | solution.py:386
  29.0 9.5 %all-to-all-start.1 = ((bf16[16,256,256]{2,1,0:T(8,128)(2,1)}), bf16[16,256,256]{2,1,0:T(8,128)(2,1)S(1)}, u32[]{:S(2)}, u32[]{:S(2)}) async-start(bf16[16,256,256]{2,1,0:T(8,128)(2,1)} %broadcast_in_dim.7), calls=%async_computation.1 | async-start | bytes 4194304 | tf_op jit(solution)/shard_map/all_to_all | solution.py:386
  38.4 2.2 %collective-permute-start.3 = (bf16[512,256]{1,0:T(8,128)(2,1)S(1)}, bf16[512,256]{1,0:T(8,128)(2,1)S(1)}, u32[]{:S(2)}, u32[]{:S(2)}) collective-permute-start(bf16[512,256]{1,0:T(8,128)(2,1)S(1)} %copy-done.2), channel_id=1, source_target_pairs={{0,1},{1,2},{2,3},{3,4},{4,5},{5,6},{6,7},{7,0},{8,9},{9,10},{10,1... | collective-permute-start | bytes 786440 | tf_op jit(solution)/shard_map/ppermute | solution.py:372
  40.6 2.6 %collective-permute-start = (bf16[512,256]{1,0:T(8,128)(2,1)S(1)}, bf16[512,256]{1,0:T(8,128)(2,1)S(1)}, u32[]{:S(2)}, u32[]{:S(2)}) collective-permute-start(bf16[512,256]{1,0:T(8,128)(2,1)S(1)} %copy-done.2), channel_id=1, source_target_pairs={{1,0},{2,1},{3,2},{4,3},{5,4},{6,5},{7,6},{0,7},{9,8},{10,9},{11,1... | collective-permute-start | bytes 786440 | tf_op jit(solution)/shard_map/ppermute | solution.py:372
  43.2 3.5 %gate.3.refs_0_ = bf16[512,256]{1,0:T(8,128)(2,1)} custom-call(bf16[3,1536,256]{2,1,0:T(8,128)(2,1)} %refs_1_.3, bf16[3,1536,256]{2,1,0:T(8,128)(2,1)} %refs_1_.3, f32[3,3,256]{2,1,0:T(4,128)} %refs_2_.3, f32[2,16,256]{2,1,0:T(8,128)} %get-tuple-element.27.refs_3_, f32[1,256]{1,0:T(1,128)} %bitcast.12, f32[1536,256]{1,0:T(8,128)} %get-tuple-element.28.refs_5_, ...), custom_call_target="tpu_custom_call" | custom-call | flops 4000000000 | bytes 4000000 | tf_op jit(solution)/shard_map/gate/pallas_call | solution.py:344
  46.7 0.0 collective-permute-start.8
  46.7 3.2 %collective-permute-start.11 = (bf16[512,256]{1,0:T(8,128)(2,1)}, bf16[512,256]{1,0:T(8,128)(2,1)S(1)}, u32[]{:S(2)}, u32[]{:S(2)}) collective-permute-start(bf16[512,256]{1,0:T(8,128)(2,1)} %gate.3.refs_0_), channel_id=1, source_target_pairs={{1,0},{2,1},{3,2},{4,3},{5,4},{6,5},{7,6},{0,7},{9,8},{10,9},{11,1... | collective-permute-start | bytes 786440 | tf_op jit(solution)/shard_map/ppermute | solution.py:372
  49.9 0.7 collective-permute-start.15
  50.7 1.3 %collective-permute-start.4 = (bf16[512,256]{1,0:T(8,128)(2,1)S(1)}, bf16[512,256]{1,0:T(8,128)(2,1)S(1)}, u32[]{:S(2)}, u32[]{:S(2)}) collective-permute-start(bf16[512,256]{1,0:T(8,128)(2,1)S(1)} %collective-permute-done.3.refs_7_), channel_id=1, source_target_pairs={{0,1},{1,2},{2,3},{3,4},{4,5},{5,6},{6,7},{7,0},{8,9},{9,10},{10,1... | collective-permute-start | bytes 786440 | tf_op jit(solution)/shard_map/ppermute | solution.py:372
  52.0 0.7 copy-done.8
  52.7 0.0 collective-permute-done.refs_1_
  52.7 0.0 collective-permute-start.19
  52.7 4.6 %collective-permute-done.8.refs_8_ = bf16[512,256]{1,0:T(8,128)(2,1)S(1)} collective-permute-done((bf16[512,256]{1,0:T(8,128)(2,1)}, bf16[512,256]{1,0:T(8,128)(2,1)S(1)}, u32[]{:S(2)}, u32[]{:S(2)}) %collective-permute-start.8) | collective-permute-done | bytes 262176 | tf_op jit(solution)/shard_map/ppermute | solution.py:372
  57.3 0.8 collective-permute-start.1
  58.1 0.7 copy-done.10
  58.8 0.0 collective-permute-done.11.refs_1_
  58.8 1.3 %collective-permute-start.9 = (bf16[512,256]{1,0:T(8,128)(2,1)S(1)}, bf16[512,256]{1,0:T(8,128)(2,1)}, u32[]{:S(2)}, u32[]{:S(2)}) collective-permute-start(bf16[512,256]{1,0:T(8,128)(2,1)S(1)} %collective-permute-done.8.refs_8_), channel_id=1, source_target_pairs={{0,1},{1,2},{2,3},{3,4},{4,5},{5,6},{6,7},{7,0},{8,9},{9,10},{10,1... | collective-permute-start | bytes 786440 | tf_op jit(solution)/shard_map/ppermute | solution.py:372
  60.0 2.5 %collective-permute-done.15.refs_1_ = bf16[512,256]{1,0:T(8,128)(2,1)S(1)} collective-permute-done((bf16[512,256]{1,0:T(8,128)(2,1)S(1)}, bf16[512,256]{1,0:T(8,128)(2,1)S(1)}, u32[]{:S(2)}, u32[]{:S(2)}) %collective-permute-start.15) | collective-permute-done | bytes 262176 | tf_op jit(solution)/shard_map/ppermute | solution.py:372
  62.5 3.7 %collective-permute-start.16 = (bf16[512,256]{1,0:T(8,128)(2,1)S(1)}, bf16[512,256]{1,0:T(8,128)(2,1)}, u32[]{:S(2)}, u32[]{:S(2)}) collective-permute-start(bf16[512,256]{1,0:T(8,128)(2,1)S(1)} %collective-permute-done.15.refs_1_), channel_id=1, source_target_pairs={{1,0},{2,1},{3,2},{4,3},{5,4},{6,5},{7,6},{0,7},{9,8},{10,9},{11,1... | collective-permute-start | bytes 786440 | tf_op jit(solution)/shard_map/ppermute | solution.py:372
  66.2 0.7 copy-done.4
  66.9 0.0 collective-permute-done.4.refs_6_
  66.9 0.0 collective-permute-start.5
  66.9 0.7 copy-done.12
  67.6 0.9 collective-permute-done.19.refs_7_
  68.5 2.3 %collective-permute-start.12 = (bf16[512,256]{1,0:T(8,128)(2,1)S(1)}, bf16[512,256]{1,0:T(8,128)(2,1)}, u32[]{:S(2)}, u32[]{:S(2)}) collective-permute-start(bf16[512,256]{1,0:T(8,128)(2,1)S(1)} %collective-permute-done.11.refs_1_), channel_id=1, source_target_pairs={{1,0},{2,1},{3,2},{4,3},{5,4},{6,5},{7,6},{0,7},{9,8},{10,9},{11,1... | collective-permute-start | bytes 786440 | tf_op jit(solution)/shard_map/ppermute | solution.py:372
  70.9 0.0 collective-permute-start.20
  70.9 0.7 copy-done.6
  71.6 2.7 %collective-permute-done.9.refs_7_ = bf16[512,256]{1,0:T(8,128)(2,1)} collective-permute-done((bf16[512,256]{1,0:T(8,128)(2,1)S(1)}, bf16[512,256]{1,0:T(8,128)(2,1)}, u32[]{:S(2)}, u32[]{:S(2)}) %collective-permute-start.9) | collective-permute-done | bytes 262176 | tf_op jit(solution)/shard_map/ppermute | solution.py:372
  74.3 0.8 collective-permute-start.2
  75.0 2.5 %collective-permute-start.17 = (bf16[512,256]{1,0:T(8,128)(2,1)}, bf16[512,256]{1,0:T(8,128)(2,1)}, u32[]{:S(2)}, u32[]{:S(2)}) collective-permute-start(bf16[512,256]{1,0:T(8,128)(2,1)} %collective-permute-done.16.refs_2_), channel_id=1, source_target_pairs={{1,0},{2,1},{3,2},{4,3},{5,4},{6,5},{7,6},{0,7},{9,8},{10,9},{11,1... | collective-permute-start | bytes 786440 | tf_op jit(solution)/shard_map/ppermute | solution.py:372
  77.5 2.3 %collective-permute-done.5.refs_5_ = bf16[512,256]{1,0:T(8,128)(2,1)} collective-permute-done((bf16[512,256]{1,0:T(8,128)(2,1)S(1)}, bf16[512,256]{1,0:T(8,128)(2,1)}, u32[]{:S(2)}, u32[]{:S(2)}) %collective-permute-start.5) | collective-permute-done | bytes 262176 | tf_op jit(solution)/shard_map/ppermute | solution.py:372
  79.9 0.0 collective-permute-start.6
  79.9 0.0 collective-permute-done.12.refs_2_
  79.9 5.6 %collective-permute-done.20.refs_6_ = bf16[512,256]{1,0:T(8,128)(2,1)} collective-permute-done((bf16[512,256]{1,0:T(8,128)(2,1)S(1)}, bf16[512,256]{1,0:T(8,128)(2,1)}, u32[]{:S(2)}, u32[]{:S(2)}) %collective-permute-start.20) | collective-permute-done | bytes 262176 | tf_op jit(solution)/shard_map/ppermute | solution.py:372
  85.5 0.8 collective-permute-start.13
  86.3 1.3 %collective-permute-start.21 = (bf16[512,256]{1,0:T(8,128)(2,1)}, bf16[512,256]{1,0:T(8,128)(2,1)}, u32[]{:S(2)}, u32[]{:S(2)}) collective-permute-start(bf16[512,256]{1,0:T(8,128)(2,1)} %collective-permute-done.20.refs_6_), channel_id=1, source_target_pairs={{0,1},{1,2},{2,3},{3,4},{4,5},{5,6},{6,7},{7,0},{8,9},{9,10},{10,1... | collective-permute-start | bytes 786440 | tf_op jit(solution)/shard_map/ppermute | solution.py:372
  87.5 3.2 %collective-permute-done.17.refs_3_ = bf16[512,256]{1,0:T(8,128)(2,1)} collective-permute-done((bf16[512,256]{1,0:T(8,128)(2,1)}, bf16[512,256]{1,0:T(8,128)(2,1)}, u32[]{:S(2)}, u32[]{:S(2)}) %collective-permute-start.17) | collective-permute-done | bytes 262176 | tf_op jit(solution)/shard_map/ppermute | solution.py:372
  90.7 3.7 %collective-permute-start.18 = (bf16[512,256]{1,0:T(8,128)(2,1)}, bf16[512,256]{1,0:T(8,128)(2,1)}, u32[]{:S(2)}, u32[]{:S(2)}) collective-permute-start(bf16[512,256]{1,0:T(8,128)(2,1)} %collective-permute-done.17.refs_3_), channel_id=1, source_target_pairs={{1,0},{2,1},{3,2},{4,3},{5,4},{6,5},{7,6},{0,7},{9,8},{10,9},{11,1... | collective-permute-start | bytes 786440 | tf_op jit(solution)/shard_map/ppermute | solution.py:372
  94.4 0.9 copy-done.3
  95.3 0.9 copy-done.9
  96.3 0.9 copy-done.11
  97.2 0.9 copy-done.13
  98.2 2.6 %project.3 = (f32[512,256]{1,0:T(8,128)S(1)}, bf16[512,256]{1,0:T(8,128)(2,1)S(1)}) custom-call(s32[1]{0:T(128)} %bitcast.place_ref, bf16[512,256]{1,0:T(8,128)(2,1)S(1)} %copy-done.3, bf16[512,256]{1,0:T(8,128)(2,1)S(1)} %copy-done.11, bf16[512,256]{1,0:T(8,128)(2,1)} %collective-permute-done.1.refs_2_, bf16[512,256]{1,0:T(8,128)(2,1)} %collective-permute-done.2.refs_3_, ...), custom_call_target="tpu_custom_call" | custom-call | flops 4000000000 | bytes 4000000 | tf_op jit(solution)/shard_map/project/pallas_call | solution.py:397
  100.9 0.8 collective-permute-start.14
  101.6 0.1 collective-permute-start.23
  101.8 2.1 %collective-permute-start.24 = (bf16[256,256]{1,0:T(8,128)(2,1)S(1)}, bf16[256,256]{1,0:T(8,128)(2,1)S(1)}, u32[]{:S(2)}, u32[]{:S(2)}) collective-permute-start(bf16[256,256]{1,0:T(8,128)(2,1)S(1)} %slice.7), channel_id=1, source_target_pairs={{0,1},{1,2},{2,3},{3,4},{4,5},{5,6},{6,7},{7,0},{8,9},{9,10},{10,1... | collective-permute-start | bytes 393224 | tf_op jit(solution)/shard_map/ppermute | solution.py:372
  103.9 2.7 %project.4 = (f32[512,256]{1,0:T(8,128)S(1)}, bf16[512,256]{1,0:T(8,128)(2,1)S(1)}) custom-call(s32[1]{0:T(128)} %bitcast.place_ref, bf16[512,256]{1,0:T(8,128)(2,1)S(1)} %copy-done.1, bf16[512,256]{1,0:T(8,128)(2,1)S(1)} %copy-done.5, bf16[512,256]{1,0:T(8,128)(2,1)} %collective-permute-done.16.refs_2_, bf16[512,256]{1,0:T(8,128)(2,1)} %collective-permute-done.17.refs_3_, ...), custom_call_target="tpu_custom_call" | custom-call | flops 4000000000 | bytes 4000000 | tf_op jit(solution)/shard_map/project/pallas_call | solution.py:397
  106.5 1.4 %collective-permute-start.22 = (bf16[512,256]{1,0:T(8,128)(2,1)S(1)}, bf16[512,256]{1,0:T(8,128)(2,1)S(1)}, u32[]{:S(2)}, u32[]{:S(2)}) collective-permute-start(bf16[512,256]{1,0:T(8,128)(2,1)S(1)} %get-tuple-element.42), channel_id=1, source_target_pairs={{0,8},{1,9},{2,10},{3,11},{4,12},{5,13},{6,14},{7,15},{8,0},{9,1},... | collective-permute-start | bytes 786440 | tf_op jit(solution)/shard_map/ppermute | solution.py:413
  108.0 0.0 collective-permute-done.24.refs_5_
  108.0 2.4 %project.5 = (f32[512,256]{1,0:T(8,128)S(1)}, bf16[512,256]{1,0:T(8,128)(2,1)S(1)}) custom-call(s32[1]{0:T(128)} %bitcast.place_ref, bf16[512,256]{1,0:T(8,128)(2,1)S(1)} %copy-done, bf16[512,256]{1,0:T(8,128)(2,1)S(1)} %collective-permute-done.11.refs_1_, bf16[512,256]{1,0:T(8,128)(2,1)} %collective-permute-done.12.refs_2_, ...), custom_call_target="tpu_custom_call" | custom-call | flops 4000000000 | bytes 4000000 | tf_op jit(solution)/shard_map/project/pallas_call | solution.py:397
  110.5 1.4 %collective-permute-start.25 = (bf16[512,256]{1,0:T(8,128)(2,1)S(1)}, bf16[512,256]{1,0:T(8,128)(2,1)S(1)}, u32[]{:S(2)}, u32[]{:S(2)}) collective-permute-start(bf16[512,256]{1,0:T(8,128)(2,1)S(1)} %get-tuple-element.46), channel_id=1, source_target_pairs={{0,8},{1,9},{2,10},{3,11},{4,12},{5,13},{6,14},{7,15},{8,0},{9,1},... | collective-permute-start | bytes 786440 | tf_op jit(solution)/shard_map/ppermute | solution.py:413
  111.9 0.1 add_convert_fusion.2
  112.0 3.8 %collective-permute-done.22 = bf16[512,256]{1,0:T(8,128)(2,1)S(1)} collective-permute-done((bf16[512,256]{1,0:T(8,128)(2,1)S(1)}, bf16[512,256]{1,0:T(8,128)(2,1)S(1)}, u32[]{:S(2)}, u32[]{:S(2)}) %collective-permute-start.22) | collective-permute-done | bytes 262176 | tf_op jit(solution)/shard_map/ppermute | solution.py:413
  115.7 0.1 add_convert_fusion.1
  115.8 2.7 %collective-permute-done.25 = bf16[512,256]{1,0:T(8,128)(2,1)S(1)} collective-permute-done((bf16[512,256]{1,0:T(8,128)(2,1)S(1)}, bf16[512,256]{1,0:T(8,128)(2,1)S(1)}, u32[]{:S(2)}, u32[]{:S(2)}) %collective-permute-start.25) | collective-permute-done | bytes 262176 | tf_op jit(solution)/shard_map/ppermute | solution.py:413
  118.6 0.1 add_convert_fusion
  118.6 0.9 pad_maximum_fusion
  (37 shorter events, 0.1 us)
Async XLA Ops:
  0.0 12.7 %copy-start.15 = (bf16[256,256]{1,0:T(8,128)(2,1)S(1)}, bf16[256,256]{1,0:T(8,128)(2,1)}, u32[]{:S(2)}) copy-start(bf16[256,256]{1,0:T(8,128)(2,1)} %param.11) | copy-start | bytes 393220
  5.2 15.3 %all-to-all-start = ((bf16[16,48,256]{2,1,0:T(8,128)(2,1)}), bf16[16,48,256]{2,1,0:T(8,128)(2,1)S(1)}, u32[]{:S(2)}, u32[]{:S(2)}) async-start(bf16[16,48,256]{2,1,0:T(8,128)(2,1)} %get-tuple-element.31), calls=%async_computation | async-start | bytes 786432 | tf_op jit(solution)/shard_map/all_to_all | solution.py:319
  12.7 14.7 %collective-permute-start.7 = (bf16[256,256]{1,0:T(8,128)(2,1)S(1)}, bf16[256,256]{1,0:T(8,128)(2,1)S(1)}, u32[]{:S(2)}, u32[]{:S(2)}) collective-permute-start(bf16[256,256]{1,0:T(8,128)(2,1)S(1)} %copy-done.15), channel_id=1, source_target_pairs={{0,0},{1,16},{2,32},{3,48},{4,64},{5,80},{6,96},{7,112},{8,8},{9,2... | collective-permute-start | bytes 393224 | tf_op jit(solution)/shard_map/ppermute | solution.py:318
  20.5 0.7 copy-start.14
  29.0 9.5 %copy-start.2 = (bf16[512,256]{1,0:T(8,128)(2,1)S(1)}, bf16[512,256]{1,0:T(8,128)(2,1)}, u32[]{:S(2)}) copy-start(bf16[512,256]{1,0:T(8,128)(2,1)} %get-tuple-element.32.refs_0_) | copy-start | bytes 786436
  29.0 65.4 %all-to-all-start.1 = ((bf16[16,256,256]{2,1,0:T(8,128)(2,1)}), bf16[16,256,256]{2,1,0:T(8,128)(2,1)S(1)}, u32[]{:S(2)}, u32[]{:S(2)}) async-start(bf16[16,256,256]{2,1,0:T(8,128)(2,1)} %broadcast_in_dim.7), calls=%async_computation.1 | async-start | bytes 4194304 | tf_op jit(solution)/shard_map/all_to_all | solution.py:386
  38.4 12.2 %collective-permute-start.3 = (bf16[512,256]{1,0:T(8,128)(2,1)S(1)}, bf16[512,256]{1,0:T(8,128)(2,1)S(1)}, u32[]{:S(2)}, u32[]{:S(2)}) collective-permute-start(bf16[512,256]{1,0:T(8,128)(2,1)S(1)} %copy-done.2), channel_id=1, source_target_pairs={{0,1},{1,2},{2,3},{3,4},{4,5},{5,6},{6,7},{7,0},{8,9},{9,10},{10,1... | collective-permute-start | bytes 786440 | tf_op jit(solution)/shard_map/ppermute | solution.py:372
  40.6 12.1 %collective-permute-start = (bf16[512,256]{1,0:T(8,128)(2,1)S(1)}, bf16[512,256]{1,0:T(8,128)(2,1)S(1)}, u32[]{:S(2)}, u32[]{:S(2)}) collective-permute-start(bf16[512,256]{1,0:T(8,128)(2,1)S(1)} %copy-done.2), channel_id=1, source_target_pairs={{1,0},{2,1},{3,2},{4,3},{5,4},{6,5},{7,6},{0,7},{9,8},{10,9},{11,1... | collective-permute-start | bytes 786440 | tf_op jit(solution)/shard_map/ppermute | solution.py:372
  43.2 6.8 %copy-start.1 = (bf16[512,256]{1,0:T(8,128)(2,1)S(1)}, bf16[512,256]{1,0:T(8,128)(2,1)}, u32[]{:S(2)}) copy-start(bf16[512,256]{1,0:T(8,128)(2,1)} %get-tuple-element.40.refs_0_) | copy-start | bytes 786436
  46.7 10.6 %collective-permute-start.8 = (bf16[512,256]{1,0:T(8,128)(2,1)}, bf16[512,256]{1,0:T(8,128)(2,1)S(1)}, u32[]{:S(2)}, u32[]{:S(2)}) collective-permute-start(bf16[512,256]{1,0:T(8,128)(2,1)} %gate.3.refs_0_), channel_id=1, source_target_pairs={{0,1},{1,2},{2,3},{3,4},{4,5},{5,6},{6,7},{7,0},{8,9},{9,10},{10,1... | collective-permute-start | bytes 786440 | tf_op jit(solution)/shard_map/ppermute | solution.py:372
  46.7 12.1 %collective-permute-start.11 = (bf16[512,256]{1,0:T(8,128)(2,1)}, bf16[512,256]{1,0:T(8,128)(2,1)S(1)}, u32[]{:S(2)}, u32[]{:S(2)}) collective-permute-start(bf16[512,256]{1,0:T(8,128)(2,1)} %gate.3.refs_0_), channel_id=1, source_target_pairs={{1,0},{2,1},{3,2},{4,3},{5,4},{6,5},{7,6},{0,7},{9,8},{10,9},{11,1... | collective-permute-start | bytes 786440 | tf_op jit(solution)/shard_map/ppermute | solution.py:372
  49.9 12.6 %collective-permute-start.15 = (bf16[512,256]{1,0:T(8,128)(2,1)S(1)}, bf16[512,256]{1,0:T(8,128)(2,1)S(1)}, u32[]{:S(2)}, u32[]{:S(2)}) collective-permute-start(bf16[512,256]{1,0:T(8,128)(2,1)S(1)} %copy-done.1), channel_id=1, source_target_pairs={{1,0},{2,1},{3,2},{4,3},{5,4},{6,5},{7,6},{0,7},{9,8},{10,9},{11,1... | collective-permute-start | bytes 786440 | tf_op jit(solution)/shard_map/ppermute | solution.py:372
  50.7 16.2 %collective-permute-start.4 = (bf16[512,256]{1,0:T(8,128)(2,1)S(1)}, bf16[512,256]{1,0:T(8,128)(2,1)S(1)}, u32[]{:S(2)}, u32[]{:S(2)}) collective-permute-start(bf16[512,256]{1,0:T(8,128)(2,1)S(1)} %collective-permute-done.3.refs_7_), channel_id=1, source_target_pairs={{0,1},{1,2},{2,3},{3,4},{4,5},{5,6},{6,7},{7,0},{8,9},{9,10},{10,1... | collective-permute-start | bytes 786440 | tf_op jit(solution)/shard_map/ppermute | solution.py:372
  52.0 0.7 copy-start.8
  52.7 15.9 %collective-permute-start.19 = (bf16[512,256]{1,0:T(8,128)(2,1)S(1)}, bf16[512,256]{1,0:T(8,128)(2,1)S(1)}, u32[]{:S(2)}, u32[]{:S(2)}) collective-permute-start(bf16[512,256]{1,0:T(8,128)(2,1)S(1)} %copy-done.1), channel_id=1, source_target_pairs={{0,1},{1,2},{2,3},{3,4},{4,5},{5,6},{6,7},{7,0},{8,9},{9,10},{10,1... | collective-permute-start | bytes 786440 | tf_op jit(solution)/shard_map/ppermute | solution.py:372
  57.3 13.6 %collective-permute-start.1 = (bf16[512,256]{1,0:T(8,128)(2,1)S(1)}, bf16[512,256]{1,0:T(8,128)(2,1)}, u32[]{:S(2)}, u32[]{:S(2)}) collective-permute-start(bf16[512,256]{1,0:T(8,128)(2,1)S(1)} %collective-permute-done.refs_1_), channel_id=1, source_target_pairs={{1,0},{2,1},{3,2},{4,3},{5,4},{6,5},{7,6},{0,7},{9,8},{10,9},{11,1... | collective-permute-start | bytes 786440 | tf_op jit(solution)/shard_map/ppermute | solution.py:372
  58.1 0.7 copy-start.10
  58.8 15.5 %collective-permute-start.9 = (bf16[512,256]{1,0:T(8,128)(2,1)S(1)}, bf16[512,256]{1,0:T(8,128)(2,1)}, u32[]{:S(2)}, u32[]{:S(2)}) collective-permute-start(bf16[512,256]{1,0:T(8,128)(2,1)S(1)} %collective-permute-done.8.refs_8_), channel_id=1, source_target_pairs={{0,1},{1,2},{2,3},{3,4},{4,5},{5,6},{6,7},{7,0},{8,9},{9,10},{10,1... | collective-permute-start | bytes 786440 | tf_op jit(solution)/shard_map/ppermute | solution.py:372
  62.5 12.5 %collective-permute-start.16 = (bf16[512,256]{1,0:T(8,128)(2,1)S(1)}, bf16[512,256]{1,0:T(8,128)(2,1)}, u32[]{:S(2)}, u32[]{:S(2)}) collective-permute-start(bf16[512,256]{1,0:T(8,128)(2,1)S(1)} %collective-permute-done.15.refs_1_), channel_id=1, source_target_pairs={{1,0},{2,1},{3,2},{4,3},{5,4},{6,5},{7,6},{0,7},{9,8},{10,9},{11,1... | collective-permute-start | bytes 786440 | tf_op jit(solution)/shard_map/ppermute | solution.py:372
  66.2 0.7 copy-start.4
  66.9 13.0 %collective-permute-start.5 = (bf16[512,256]{1,0:T(8,128)(2,1)S(1)}, bf16[512,256]{1,0:T(8,128)(2,1)}, u32[]{:S(2)}, u32[]{:S(2)}) collective-permute-start(bf16[512,256]{1,0:T(8,128)(2,1)S(1)} %collective-permute-done.4.refs_6_), channel_id=1, source_target_pairs={{0,1},{1,2},{2,3},{3,4},{4,5},{5,6},{6,7},{7,0},{8,9},{9,10},{10,1... | collective-permute-start | bytes 786440 | tf_op jit(solution)/shard_map/ppermute | solution.py:372
  66.9 0.7 copy-start.12
  68.5 11.3 %collective-permute-start.12 = (bf16[512,256]{1,0:T(8,128)(2,1)S(1)}, bf16[512,256]{1,0:T(8,128)(2,1)}, u32[]{:S(2)}, u32[]{:S(2)}) collective-permute-start(bf16[512,256]{1,0:T(8,128)(2,1)S(1)} %collective-permute-done.11.refs_1_), channel_id=1, source_target_pairs={{1,0},{2,1},{3,2},{4,3},{5,4},{6,5},{7,6},{0,7},{9,8},{10,9},{11,1... | collective-permute-start | bytes 786440 | tf_op jit(solution)/shard_map/ppermute | solution.py:372
  70.9 14.6 %collective-permute-start.20 = (bf16[512,256]{1,0:T(8,128)(2,1)S(1)}, bf16[512,256]{1,0:T(8,128)(2,1)}, u32[]{:S(2)}, u32[]{:S(2)}) collective-permute-start(bf16[512,256]{1,0:T(8,128)(2,1)S(1)} %collective-permute-done.19.refs_7_), channel_id=1, source_target_pairs={{0,1},{1,2},{2,3},{3,4},{4,5},{5,6},{6,7},{7,0},{8,9},{9,10},{10,1... | collective-permute-start | bytes 786440 | tf_op jit(solution)/shard_map/ppermute | solution.py:372
  70.9 0.7 copy-start.6
  74.3 12.0 %collective-permute-start.2 = (bf16[512,256]{1,0:T(8,128)(2,1)}, bf16[512,256]{1,0:T(8,128)(2,1)}, u32[]{:S(2)}, u32[]{:S(2)}) collective-permute-start(bf16[512,256]{1,0:T(8,128)(2,1)} %collective-permute-done.1.refs_2_), channel_id=1, source_target_pairs={{1,0},{2,1},{3,2},{4,3},{5,4},{6,5},{7,6},{0,7},{9,8},{10,9},{11,1... | collective-permute-start | bytes 786440 | tf_op jit(solution)/shard_map/ppermute | solution.py:372
  75.0 15.7 %collective-permute-start.17 = (bf16[512,256]{1,0:T(8,128)(2,1)}, bf16[512,256]{1,0:T(8,128)(2,1)}, u32[]{:S(2)}, u32[]{:S(2)}) collective-permute-start(bf16[512,256]{1,0:T(8,128)(2,1)} %collective-permute-done.16.refs_2_), channel_id=1, source_target_pairs={{1,0},{2,1},{3,2},{4,3},{5,4},{6,5},{7,6},{0,7},{9,8},{10,9},{11,1... | collective-permute-start | bytes 786440 | tf_op jit(solution)/shard_map/ppermute | solution.py:372
  79.9 14.5 %collective-permute-start.6 = (bf16[512,256]{1,0:T(8,128)(2,1)}, bf16[512,256]{1,0:T(8,128)(2,1)}, u32[]{:S(2)}, u32[]{:S(2)}) collective-permute-start(bf16[512,256]{1,0:T(8,128)(2,1)} %collective-permute-done.5.refs_5_), channel_id=1, source_target_pairs={{0,1},{1,2},{2,3},{3,4},{4,5},{5,6},{6,7},{7,0},{8,9},{9,10},{10,1... | collective-permute-start | bytes 786440 | tf_op jit(solution)/shard_map/ppermute | solution.py:372
  79.9 21.0 %collective-permute-start.10 = (bf16[512,256]{1,0:T(8,128)(2,1)}, bf16[512,256]{1,0:T(8,128)(2,1)S(1)}, u32[]{:S(2)}, u32[]{:S(2)}) collective-permute-start(bf16[512,256]{1,0:T(8,128)(2,1)} %collective-permute-done.9.refs_7_), channel_id=1, source_target_pairs={{0,1},{1,2},{2,3},{3,4},{4,5},{5,6},{6,7},{7,0},{8,9},{9,10},{10,1... | collective-permute-start | bytes 786440 | tf_op jit(solution)/shard_map/ppermute | solution.py:372
  85.5 15.4 %collective-permute-start.13 = (bf16[512,256]{1,0:T(8,128)(2,1)}, bf16[512,256]{1,0:T(8,128)(2,1)S(1)}, u32[]{:S(2)}, u32[]{:S(2)}) collective-permute-start(bf16[512,256]{1,0:T(8,128)(2,1)} %collective-permute-done.12.refs_2_), channel_id=1, source_target_pairs={{1,0},{2,1},{3,2},{4,3},{5,4},{6,5},{7,6},{0,7},{9,8},{10,9},{11,1... | collective-permute-start | bytes 786440 | tf_op jit(solution)/shard_map/ppermute | solution.py:372
  86.3 17.6 %collective-permute-start.21 = (bf16[512,256]{1,0:T(8,128)(2,1)}, bf16[512,256]{1,0:T(8,128)(2,1)}, u32[]{:S(2)}, u32[]{:S(2)}) collective-permute-start(bf16[512,256]{1,0:T(8,128)(2,1)} %collective-permute-done.20.refs_6_), channel_id=1, source_target_pairs={{0,1},{1,2},{2,3},{3,4},{4,5},{5,6},{6,7},{7,0},{8,9},{9,10},{10,1... | collective-permute-start | bytes 786440 | tf_op jit(solution)/shard_map/ppermute | solution.py:372
  90.7 13.2 %collective-permute-start.18 = (bf16[512,256]{1,0:T(8,128)(2,1)}, bf16[512,256]{1,0:T(8,128)(2,1)}, u32[]{:S(2)}, u32[]{:S(2)}) collective-permute-start(bf16[512,256]{1,0:T(8,128)(2,1)} %collective-permute-done.17.refs_3_), channel_id=1, source_target_pairs={{1,0},{2,1},{3,2},{4,3},{5,4},{6,5},{7,6},{0,7},{9,8},{10,9},{11,1... | collective-permute-start | bytes 786440 | tf_op jit(solution)/shard_map/ppermute | solution.py:372
  94.4 1.0 copy-start.3
  95.3 0.9 copy-start.9
  96.3 0.9 copy-start.11
  97.2 0.9 copy-start.13
  98.2 5.7 %copy-start.5 = (bf16[512,256]{1,0:T(8,128)(2,1)S(1)}, bf16[512,256]{1,0:T(8,128)(2,1)}, u32[]{:S(2)}) copy-start(bf16[512,256]{1,0:T(8,128)(2,1)} %copy-done.4) | copy-start | bytes 786436
  98.2 5.7 %copy-start.7 = (bf16[512,256]{1,0:T(8,128)(2,1)S(1)}, bf16[512,256]{1,0:T(8,128)(2,1)}, u32[]{:S(2)}) copy-start(bf16[512,256]{1,0:T(8,128)(2,1)} %copy-done.6) | copy-start | bytes 786436
  100.9 11.0 %collective-permute-start.14 = (bf16[512,256]{1,0:T(8,128)(2,1)S(1)}, bf16[512,256]{1,0:T(8,128)(2,1)S(1)}, u32[]{:S(2)}, u32[]{:S(2)}) collective-permute-start(bf16[512,256]{1,0:T(8,128)(2,1)S(1)} %get-tuple-element.39), channel_id=1, source_target_pairs={{0,8},{1,9},{2,10},{3,11},{4,12},{5,13},{6,14},{7,15},{8,0},{9,1},... | collective-permute-start | bytes 786440 | tf_op jit(solution)/shard_map/ppermute | solution.py:413
  101.6 6.3 %collective-permute-start.23 = (bf16[256,256]{1,0:T(8,128)(2,1)S(1)}, bf16[256,256]{1,0:T(8,128)(2,1)S(1)}, u32[]{:S(2)}, u32[]{:S(2)}) collective-permute-start(bf16[256,256]{1,0:T(8,128)(2,1)S(1)} %slice.6), channel_id=1, source_target_pairs={{1,0},{2,1},{3,2},{4,3},{5,4},{6,5},{7,6},{0,7},{9,8},{10,9},{11,1... | collective-permute-start | bytes 393224 | tf_op jit(solution)/shard_map/ppermute | solution.py:372
  101.8 6.3 %copy-start = (bf16[512,256]{1,0:T(8,128)(2,1)S(1)}, bf16[512,256]{1,0:T(8,128)(2,1)}, u32[]{:S(2)}) copy-start(bf16[512,256]{1,0:T(8,128)(2,1)} %gate.3.refs_0_) | copy-start | bytes 786436
  101.8 6.3 %collective-permute-start.24 = (bf16[256,256]{1,0:T(8,128)(2,1)S(1)}, bf16[256,256]{1,0:T(8,128)(2,1)S(1)}, u32[]{:S(2)}, u32[]{:S(2)}) collective-permute-start(bf16[256,256]{1,0:T(8,128)(2,1)S(1)} %slice.7), channel_id=1, source_target_pairs={{0,1},{1,2},{2,3},{3,4},{4,5},{5,6},{6,7},{7,0},{8,9},{9,10},{10,1... | collective-permute-start | bytes 393224 | tf_op jit(solution)/shard_map/ppermute | solution.py:372
  106.5 9.2 %collective-permute-start.22 = (bf16[512,256]{1,0:T(8,128)(2,1)S(1)}, bf16[512,256]{1,0:T(8,128)(2,1)S(1)}, u32[]{:S(2)}, u32[]{:S(2)}) collective-permute-start(bf16[512,256]{1,0:T(8,128)(2,1)S(1)} %get-tuple-element.42), channel_id=1, source_target_pairs={{0,8},{1,9},{2,10},{3,11},{4,12},{5,13},{6,14},{7,15},{8,0},{9,1},... | collective-permute-start | bytes 786440 | tf_op jit(solution)/shard_map/ppermute | solution.py:413
  110.5 8.1 %collective-permute-start.25 = (bf16[512,256]{1,0:T(8,128)(2,1)S(1)}, bf16[512,256]{1,0:T(8,128)(2,1)S(1)}, u32[]{:S(2)}, u32[]{:S(2)}) collective-permute-start(bf16[512,256]{1,0:T(8,128)(2,1)S(1)} %get-tuple-element.46), channel_id=1, source_target_pairs={{0,8},{1,9},{2,10},{3,11},{4,12},{5,13},{6,14},{7,15},{8,0},{9,1},... | collective-permute-start | bytes 786440 | tf_op jit(solution)/shard_map/ppermute | solution.py:413

commit v6 on v5

--- a/solution.py
+++ b/solution.py
@@ -252,15 +252,27 @@
 
 
 def project_kernel(place_ref, *refs):
-    w_ref, own_ref, other_ref = refs[-3:]
-    values = [r[...] for r in refs[:-3]]
-    if len(values) == 9:
-        far = jnp.where(pl.program_id(0) == 0, values[4], values[5])
-        values = values[:4] + [far] + values[6:]
-    rows = jnp.concatenate(values, axis=1)
+    *blocks, w_ref, own_ref, other_ref, rows_ref, sems = refs
+    chunk, width = own_ref.shape
+    half = chunk // 2
+    column = lambda j: pl.ds(j * width, width)
+    if len(blocks) == 9:
+        wholes = [(j, blocks[j if j < 4 else j + 1]) for j in range(RING) if j != 4]
+        copies = [(blocks[4 + i], rows_ref.at[pl.ds(i * half, half), column(4)]) for i in range(2)]
+    else:
+        wholes, copies = list(enumerate(blocks)), []
+    copies += [(block, rows_ref.at[:, column(j)]) for j, block in wholes]
+    copies = [pltpu.make_async_copy(a, b, sems.at[i]) for i, (a, b) in enumerate(copies)]
+    for copy in copies:
+        copy.start()
+    for copy in copies:
+        copy.wait()
     side = place_ref[0]
-    own_ref[...] = jnp.dot(rows, w_ref[side], preferred_element_type=F32)
-    other_ref[...] = jnp.dot(rows, w_ref[1 - side], preferred_element_type=F32).astype(BF16)
+    for i in range(2):
+        at = pl.ds(i * half, half)
+        rows = rows_ref[at, :]
+        own_ref[at, :] = jnp.dot(rows, w_ref[side], preferred_element_type=F32)
+        other_ref[at, :] = jnp.dot(rows, w_ref[1 - side], preferred_element_type=F32).astype(BF16)
 
 
 def local(streams, taps, residues, decay, skip, w_out):
@@ -388,22 +400,22 @@
 
     def project(c):
         chunk = CHUNKS[c][1]
-        rows = chunk // 2
         get = lambda way, *hops: [arrived[c, s, way] for s in hops if (c, s, way) in arrived]
         parts = [gated[c], *get("d", 1, 2, 3, 4), *get("u", 4, 3, 2, 1)]
-        far = len(parts) - 7
-        tile = pl.BlockSpec((rows, chans), lambda g: (g, 0))
-        whole = pl.BlockSpec((rows, chans), lambda g: (0, 0))
+        vmem = pl.BlockSpec(memory_space=pltpu.VMEM)
         mine, other = pl.pallas_call(
             project_kernel,
-            grid=(2,),
-            in_specs=[smem] + [tile] * 4 + [[tile], [whole] * 2][far - 1] + [tile] * 3 + [pl.BlockSpec(w_all.shape, lambda g: (0,) * w_all.ndim)],
-            out_specs=[tile] * 2,
+            in_specs=[smem] + [pl.BlockSpec(memory_space=pltpu.HBM)] * len(parts) + [vmem],
+            out_specs=[vmem] * 2,
             out_shape=[
                 jax.ShapeDtypeStruct((chunk, chans), F32),
                 jax.ShapeDtypeStruct((chunk, chans), BF16),
             ],
-            compiler_params=params(20),
+            scratch_shapes=[
+                pltpu.VMEM((chunk, RING * chans), BF16),
+                pltpu.SemaphoreType.DMA((len(parts),)),
+            ],
+            compiler_params=params(10),
             cost_estimate=cost,
             name="project",
         )(place, *parts, w_all)

time: 120 us -> 120 us (level)
  no operation moved by 1% of the time
where the time goes in v6:
time: 120 us
  starting transfers between devices  56.5 us (47%)
  waiting for transfers between devices  29.9 us (25%)
  Pallas kernels  22.2 us (18%)
  local copies, waits for them, and re-layouts  9.64 us (8%)
    ppermute x22, starting transfers between devices, hop(): arrived[c, s, way] = lax.ppermute(block, 'ch', up if way == 'u' else down)  29.2 us
    ppermute x22, waiting for transfers between devices, hop(): arrived[c, s, way] = lax.ppermute(block, 'ch', up if way == 'u' else down)  21.9 us
    all_to_all x1, starting transfers between devices, weights(): w_all = lax.all_to_all(jnp.broadcast_to(w, (CTX, *w.shape)), 'ctx', 0, 0)  9.45 us
    pallas_call x2, Pallas kernels, gate(): pl.pallas_call(functools.partial(gate_kernel, group, tokens), grid=(tiles...  9.26 us
    unnamed x32, local copies, waits for them, and re-layouts  8.07 us
    pallas_call x3, Pallas kernels, project(): pl.pallas_call(project_kernel, in_specs=[smem] + [pl.BlockSpec(memory_spa...  7.79 us
    all_to_all x1, starting transfers between devices, local(): recv = lax.all_to_all(send, 'ctx', 0, 0)  7.48 us
    ppermute x1, starting transfers between devices, local(): w_block = lax.ppermute(w_block, ('ctx', 'ch'), swap)  6.69 us
  transfers between devices with their start and end apart: 28, of which 11 were waited for; matrix products, arithmetic and copies ran while one was open for 0% of the time, Pallas kernels for 14%

profile of v6, /device:TPU:2, one launch (start us, length us, event | category | flops | bytes accessed | tf_op | source)
XLA Modules:
  0.0 119.6 jit_solution(16876488179053020062)
XLA Ops:
  0.0 5.2 %states.1 = (f32[1536,256]{1,0:T(8,128)}, f32[3,16,8,256]{3,2,1,0:T(8,128)}, f32[3,16,256]{2,1,0:T(8,128)}, bf16[16,48,256]{2,1,0:T(8,128)(2,1)}, f32[2,16,256]{2,1,0:T(8,128)}) custom-call(bf16[3,1536,256]{2,1,0:T(8,128)(2,1)} %refs_1_.3, bf16[3,1536,256]{2,1,0:T(8,128)(2,1)} %refs_1_.3, bf16[3,1536,256]{2,1,0:T(8,128)(2,1)} %refs_1_.3, ...), custom_call_target="tpu_custom_call" | custom-call | flops 4000000000 | bytes 4000000 | tf_op jit(solution)/shard_map/states/pallas_call | solution.py:299
  5.2 7.5 %all-to-all-start = ((bf16[16,48,256]{2,1,0:T(8,128)(2,1)}), bf16[16,48,256]{2,1,0:T(8,128)(2,1)S(1)}, u32[]{:S(2)}, u32[]{:S(2)}) async-start(bf16[16,48,256]{2,1,0:T(8,128)(2,1)} %get-tuple-element.31), calls=%async_computation | async-start | bytes 786432 | tf_op jit(solution)/shard_map/all_to_all | solution.py:331
  12.7 6.7 %collective-permute-start.7 = (bf16[256,256]{1,0:T(8,128)(2,1)S(1)}, bf16[256,256]{1,0:T(8,128)(2,1)S(1)}, u32[]{:S(2)}, u32[]{:S(2)}) collective-permute-start(bf16[256,256]{1,0:T(8,128)(2,1)S(1)} %copy-done.15), channel_id=1, source_target_pairs={{0,0},{1,16},{2,32},{3,48},{4,64},{5,80},{6,96},{7,112},{8,8},{9,2... | collective-permute-start | bytes 393224 | tf_op jit(solution)/shard_map/ppermute | solution.py:330
  19.4 1.1 all-to-all-done.refs_8_
  20.5 0.7 copy-done.14
  21.3 5.7 %gate.2 = (bf16[512,256]{1,0:T(8,128)(2,1)}, bf16[512,256]{1,0:T(8,128)(2,1)}, f32[1,16,256]{2,1,0:T(8,128)}) custom-call(s32[1]{0:T(128)} %bitcast.1.refs_0_, bf16[3,1536,256]{2,1,0:T(8,128)(2,1)} %refs_1_.3, f32[3,3,256]{2,1,0:T(4,128)} %refs_2_.3, f32[2,16,256]{2,1,0:T(8,128)} %get-tuple-element.27.refs_3_, f32[1,256]{1,0:T(1,128)} %bitcast.11, ...), custom_call_target="tpu_custom_call" | custom-call | flops 4000000000 | bytes 4000000 | tf_op jit(solution)/shard_map/gate/pallas_call | solution.py:356
  27.0 0.4 collective-permute-done.7
  27.4 1.5 %broadcast_in_dim.7 = bf16[16,256,256]{2,1,0:T(8,128)(2,1)} broadcast(bf16[256,256]{1,0:T(8,128)(2,1)S(1)} %collective-permute-done.7), dimensions={1,2} | broadcast | bytes 2228224 | tf_op jit(solution)/shard_map/broadcast_in_dim | solution.py:398
  29.0 9.5 %all-to-all-start.1 = ((bf16[16,256,256]{2,1,0:T(8,128)(2,1)}), bf16[16,256,256]{2,1,0:T(8,128)(2,1)S(1)}, u32[]{:S(2)}, u32[]{:S(2)}) async-start(bf16[16,256,256]{2,1,0:T(8,128)(2,1)} %broadcast_in_dim.7), calls=%async_computation.1 | async-start | bytes 4194304 | tf_op jit(solution)/shard_map/all_to_all | solution.py:398
  38.4 2.2 %collective-permute-start.3 = (bf16[512,256]{1,0:T(8,128)(2,1)S(1)}, bf16[512,256]{1,0:T(8,128)(2,1)S(1)}, u32[]{:S(2)}, u32[]{:S(2)}) collective-permute-start(bf16[512,256]{1,0:T(8,128)(2,1)S(1)} %copy-done.2), channel_id=1, source_target_pairs={{0,1},{1,2},{2,3},{3,4},{4,5},{5,6},{6,7},{7,0},{8,9},{9,10},{10,1... | collective-permute-start | bytes 786440 | tf_op jit(solution)/shard_map/ppermute | solution.py:384
  40.6 2.6 %collective-permute-start = (bf16[512,256]{1,0:T(8,128)(2,1)S(1)}, bf16[512,256]{1,0:T(8,128)(2,1)S(1)}, u32[]{:S(2)}, u32[]{:S(2)}) collective-permute-start(bf16[512,256]{1,0:T(8,128)(2,1)S(1)} %copy-done.2), channel_id=1, source_target_pairs={{1,0},{2,1},{3,2},{4,3},{5,4},{6,5},{7,6},{0,7},{9,8},{10,9},{11,1... | collective-permute-start | bytes 786440 | tf_op jit(solution)/shard_map/ppermute | solution.py:384
  43.2 3.5 %gate.3.refs_0_ = bf16[512,256]{1,0:T(8,128)(2,1)} custom-call(bf16[3,1536,256]{2,1,0:T(8,128)(2,1)} %refs_1_.3, bf16[3,1536,256]{2,1,0:T(8,128)(2,1)} %refs_1_.3, f32[3,3,256]{2,1,0:T(4,128)} %refs_2_.3, f32[2,16,256]{2,1,0:T(8,128)} %get-tuple-element.27.refs_3_, f32[1,256]{1,0:T(1,128)} %bitcast.12, f32[1536,256]{1,0:T(8,128)} %get-tuple-element.28.refs_5_, ...), custom_call_target="tpu_custom_call" | custom-call | flops 4000000000 | bytes 4000000 | tf_op jit(solution)/shard_map/gate/pallas_call | solution.py:356
  46.7 0.0 collective-permute-start.8
  46.7 3.2 %collective-permute-start.11 = (bf16[512,256]{1,0:T(8,128)(2,1)}, bf16[512,256]{1,0:T(8,128)(2,1)S(1)}, u32[]{:S(2)}, u32[]{:S(2)}) collective-permute-start(bf16[512,256]{1,0:T(8,128)(2,1)} %gate.3.refs_0_), channel_id=1, source_target_pairs={{1,0},{2,1},{3,2},{4,3},{5,4},{6,5},{7,6},{0,7},{9,8},{10,9},{11,1... | collective-permute-start | bytes 786440 | tf_op jit(solution)/shard_map/ppermute | solution.py:384
  49.9 0.7 collective-permute-start.15
  50.7 1.3 %collective-permute-start.4 = (bf16[512,256]{1,0:T(8,128)(2,1)S(1)}, bf16[512,256]{1,0:T(8,128)(2,1)S(1)}, u32[]{:S(2)}, u32[]{:S(2)}) collective-permute-start(bf16[512,256]{1,0:T(8,128)(2,1)S(1)} %collective-permute-done.3.refs_7_), channel_id=1, source_target_pairs={{0,1},{1,2},{2,3},{3,4},{4,5},{5,6},{6,7},{7,0},{8,9},{9,10},{10,1... | collective-permute-start | bytes 786440 | tf_op jit(solution)/shard_map/ppermute | solution.py:384
  52.0 0.7 copy-done.8
  52.7 0.0 collective-permute-start.19
  52.7 4.6 %collective-permute-done.8.refs_8_ = bf16[512,256]{1,0:T(8,128)(2,1)S(1)} collective-permute-done((bf16[512,256]{1,0:T(8,128)(2,1)}, bf16[512,256]{1,0:T(8,128)(2,1)S(1)}, u32[]{:S(2)}, u32[]{:S(2)}) %collective-permute-start.8) | collective-permute-done | bytes 262176 | tf_op jit(solution)/shard_map/ppermute | solution.py:384
  57.3 0.8 collective-permute-start.1
  58.1 0.7 copy-done.10
  58.8 0.0 collective-permute-done.11.refs_1_
  58.8 1.3 %collective-permute-start.9 = (bf16[512,256]{1,0:T(8,128)(2,1)S(1)}, bf16[512,256]{1,0:T(8,128)(2,1)}, u32[]{:S(2)}, u32[]{:S(2)}) collective-permute-start(bf16[512,256]{1,0:T(8,128)(2,1)S(1)} %collective-permute-done.8.refs_8_), channel_id=1, source_target_pairs={{0,1},{1,2},{2,3},{3,4},{4,5},{5,6},{6,7},{7,0},{8,9},{9,10},{10,1... | collective-permute-start | bytes 786440 | tf_op jit(solution)/shard_map/ppermute | solution.py:384
  60.0 2.5 %collective-permute-done.15.refs_1_ = bf16[512,256]{1,0:T(8,128)(2,1)S(1)} collective-permute-done((bf16[512,256]{1,0:T(8,128)(2,1)S(1)}, bf16[512,256]{1,0:T(8,128)(2,1)S(1)}, u32[]{:S(2)}, u32[]{:S(2)}) %collective-permute-start.15) | collective-permute-done | bytes 262176 | tf_op jit(solution)/shard_map/ppermute | solution.py:384
  62.5 3.7 %collective-permute-start.16 = (bf16[512,256]{1,0:T(8,128)(2,1)S(1)}, bf16[512,256]{1,0:T(8,128)(2,1)}, u32[]{:S(2)}, u32[]{:S(2)}) collective-permute-start(bf16[512,256]{1,0:T(8,128)(2,1)S(1)} %collective-permute-done.15.refs_1_), channel_id=1, source_target_pairs={{1,0},{2,1},{3,2},{4,3},{5,4},{6,5},{7,6},{0,7},{9,8},{10,9},{11,1... | collective-permute-start | bytes 786440 | tf_op jit(solution)/shard_map/ppermute | solution.py:384
  66.2 0.7 copy-done.4
  66.9 0.0 collective-permute-done.4.refs_6_
  66.9 0.0 collective-permute-start.5
  66.9 0.7 copy-done.12
  67.6 0.9 collective-permute-done.19.refs_7_
  68.5 2.3 %collective-permute-start.12 = (bf16[512,256]{1,0:T(8,128)(2,1)S(1)}, bf16[512,256]{1,0:T(8,128)(2,1)}, u32[]{:S(2)}, u32[]{:S(2)}) collective-permute-start(bf16[512,256]{1,0:T(8,128)(2,1)S(1)} %collective-permute-done.11.refs_1_), channel_id=1, source_target_pairs={{1,0},{2,1},{3,2},{4,3},{5,4},{6,5},{7,6},{0,7},{9,8},{10,9},{11,1... | collective-permute-start | bytes 786440 | tf_op jit(solution)/shard_map/ppermute | solution.py:384
  70.9 0.0 collective-permute-start.20
  70.9 0.7 copy-done.6
  71.6 2.7 %collective-permute-done.9.refs_7_ = bf16[512,256]{1,0:T(8,128)(2,1)} collective-permute-done((bf16[512,256]{1,0:T(8,128)(2,1)S(1)}, bf16[512,256]{1,0:T(8,128)(2,1)}, u32[]{:S(2)}, u32[]{:S(2)}) %collective-permute-start.9) | collective-permute-done | bytes 262176 | tf_op jit(solution)/shard_map/ppermute | solution.py:384
  74.3 0.8 collective-permute-start.2
  75.0 2.5 %collective-permute-start.17 = (bf16[512,256]{1,0:T(8,128)(2,1)}, bf16[512,256]{1,0:T(8,128)(2,1)}, u32[]{:S(2)}, u32[]{:S(2)}) collective-permute-start(bf16[512,256]{1,0:T(8,128)(2,1)} %collective-permute-done.16.refs_2_), channel_id=1, source_target_pairs={{1,0},{2,1},{3,2},{4,3},{5,4},{6,5},{7,6},{0,7},{9,8},{10,9},{11,1... | collective-permute-start | bytes 786440 | tf_op jit(solution)/shard_map/ppermute | solution.py:384
  77.5 2.3 %collective-permute-done.5.refs_5_ = bf16[512,256]{1,0:T(8,128)(2,1)} collective-permute-done((bf16[512,256]{1,0:T(8,128)(2,1)S(1)}, bf16[512,256]{1,0:T(8,128)(2,1)}, u32[]{:S(2)}, u32[]{:S(2)}) %collective-permute-start.5) | collective-permute-done | bytes 262176 | tf_op jit(solution)/shard_map/ppermute | solution.py:384
  79.9 0.0 collective-permute-start.6
  79.9 0.0 collective-permute-done.12.refs_2_
  79.9 0.0 collective-permute-start.10
  79.9 5.6 %collective-permute-done.20.refs_6_ = bf16[512,256]{1,0:T(8,128)(2,1)} collective-permute-done((bf16[512,256]{1,0:T(8,128)(2,1)S(1)}, bf16[512,256]{1,0:T(8,128)(2,1)}, u32[]{:S(2)}, u32[]{:S(2)}) %collective-permute-start.20) | collective-permute-done | bytes 262176 | tf_op jit(solution)/shard_map/ppermute | solution.py:384
  85.5 0.8 collective-permute-start.13
  86.3 1.3 %collective-permute-start.21 = (bf16[512,256]{1,0:T(8,128)(2,1)}, bf16[512,256]{1,0:T(8,128)(2,1)}, u32[]{:S(2)}, u32[]{:S(2)}) collective-permute-start(bf16[512,256]{1,0:T(8,128)(2,1)} %collective-permute-done.20.refs_6_), channel_id=1, source_target_pairs={{0,1},{1,2},{2,3},{3,4},{4,5},{5,6},{6,7},{7,0},{8,9},{9,10},{10,1... | collective-permute-start | bytes 786440 | tf_op jit(solution)/shard_map/ppermute | solution.py:384
  87.5 3.2 %collective-permute-done.17.refs_3_ = bf16[512,256]{1,0:T(8,128)(2,1)} collective-permute-done((bf16[512,256]{1,0:T(8,128)(2,1)}, bf16[512,256]{1,0:T(8,128)(2,1)}, u32[]{:S(2)}, u32[]{:S(2)}) %collective-permute-start.17) | collective-permute-done | bytes 262176 | tf_op jit(solution)/shard_map/ppermute | solution.py:384
  90.7 3.7 %collective-permute-start.18 = (bf16[512,256]{1,0:T(8,128)(2,1)}, bf16[512,256]{1,0:T(8,128)(2,1)}, u32[]{:S(2)}, u32[]{:S(2)}) collective-permute-start(bf16[512,256]{1,0:T(8,128)(2,1)} %collective-permute-done.17.refs_3_), channel_id=1, source_target_pairs={{1,0},{2,1},{3,2},{4,3},{5,4},{6,5},{7,6},{0,7},{9,8},{10,9},{11,1... | collective-permute-start | bytes 786440 | tf_op jit(solution)/shard_map/ppermute | solution.py:384
  94.4 0.9 copy-done.3
  95.3 0.9 copy-done.9
  96.3 0.9 copy-done.11
  97.2 0.9 copy-done.13
  98.2 2.6 %project.3 = (f32[512,256]{1,0:T(8,128)S(1)}, bf16[512,256]{1,0:T(8,128)(2,1)S(1)}) custom-call(s32[1]{0:T(128)} %bitcast.place_ref, bf16[512,256]{1,0:T(8,128)(2,1)S(1)} %copy-done.3, bf16[512,256]{1,0:T(8,128)(2,1)S(1)} %copy-done.11, bf16[512,256]{1,0:T(8,128)(2,1)} %collective-permute-done.1.refs_2_, bf16[512,256]{1,0:T(8,128)(2,1)} %collective-permute-done.2.refs_3_, ...), custom_call_target="tpu_custom_call" | custom-call | flops 4000000000 | bytes 4000000 | tf_op jit(solution)/shard_map/project/pallas_call | solution.py:406
  100.9 0.8 collective-permute-start.14
  101.6 0.1 collective-permute-start.23
  101.8 2.1 %collective-permute-start.24 = (bf16[256,256]{1,0:T(8,128)(2,1)S(1)}, bf16[256,256]{1,0:T(8,128)(2,1)S(1)}, u32[]{:S(2)}, u32[]{:S(2)}) collective-permute-start(bf16[256,256]{1,0:T(8,128)(2,1)S(1)} %slice.7), channel_id=1, source_target_pairs={{0,1},{1,2},{2,3},{3,4},{4,5},{5,6},{6,7},{7,0},{8,9},{9,10},{10,1... | collective-permute-start | bytes 393224 | tf_op jit(solution)/shard_map/ppermute | solution.py:384
  103.9 2.7 %project.4 = (f32[512,256]{1,0:T(8,128)S(1)}, bf16[512,256]{1,0:T(8,128)(2,1)S(1)}) custom-call(s32[1]{0:T(128)} %bitcast.place_ref, bf16[512,256]{1,0:T(8,128)(2,1)S(1)} %copy-done.1, bf16[512,256]{1,0:T(8,128)(2,1)S(1)} %copy-done.5, bf16[512,256]{1,0:T(8,128)(2,1)} %collective-permute-done.16.refs_2_, bf16[512,256]{1,0:T(8,128)(2,1)} %collective-permute-done.17.refs_3_, ...), custom_call_target="tpu_custom_call" | custom-call | flops 4000000000 | bytes 4000000 | tf_op jit(solution)/shard_map/project/pallas_call | solution.py:406
  106.5 1.4 %collective-permute-start.22 = (bf16[512,256]{1,0:T(8,128)(2,1)S(1)}, bf16[512,256]{1,0:T(8,128)(2,1)S(1)}, u32[]{:S(2)}, u32[]{:S(2)}) collective-permute-start(bf16[512,256]{1,0:T(8,128)(2,1)S(1)} %get-tuple-element.42), channel_id=1, source_target_pairs={{0,8},{1,9},{2,10},{3,11},{4,12},{5,13},{6,14},{7,15},{8,0},{9,1},... | collective-permute-start | bytes 786440 | tf_op jit(solution)/shard_map/ppermute | solution.py:425
  108.0 0.0 collective-permute-done.24.refs_5_
  108.0 2.5 %project.5 = (f32[512,256]{1,0:T(8,128)S(1)}, bf16[512,256]{1,0:T(8,128)(2,1)S(1)}) custom-call(s32[1]{0:T(128)} %bitcast.place_ref, bf16[512,256]{1,0:T(8,128)(2,1)S(1)} %copy-done, bf16[512,256]{1,0:T(8,128)(2,1)S(1)} %collective-permute-done.11.refs_1_, bf16[512,256]{1,0:T(8,128)(2,1)} %collective-permute-done.12.refs_2_, ...), custom_call_target="tpu_custom_call" | custom-call | flops 4000000000 | bytes 4000000 | tf_op jit(solution)/shard_map/project/pallas_call | solution.py:406
  110.5 1.4 %collective-permute-start.25 = (bf16[512,256]{1,0:T(8,128)(2,1)S(1)}, bf16[512,256]{1,0:T(8,128)(2,1)S(1)}, u32[]{:S(2)}, u32[]{:S(2)}) collective-permute-start(bf16[512,256]{1,0:T(8,128)(2,1)S(1)} %get-tuple-element.46), channel_id=1, source_target_pairs={{0,8},{1,9},{2,10},{3,11},{4,12},{5,13},{6,14},{7,15},{8,0},{9,1},... | collective-permute-start | bytes 786440 | tf_op jit(solution)/shard_map/ppermute | solution.py:425
  112.0 0.1 add_convert_fusion.2
  112.0 3.7 %collective-permute-done.22 = bf16[512,256]{1,0:T(8,128)(2,1)S(1)} collective-permute-done((bf16[512,256]{1,0:T(8,128)(2,1)S(1)}, bf16[512,256]{1,0:T(8,128)(2,1)S(1)}, u32[]{:S(2)}, u32[]{:S(2)}) %collective-permute-start.22) | collective-permute-done | bytes 262176 | tf_op jit(solution)/shard_map/ppermute | solution.py:425
  115.7 0.1 add_convert_fusion.1
  115.8 2.7 %collective-permute-done.25 = bf16[512,256]{1,0:T(8,128)(2,1)S(1)} collective-permute-done((bf16[512,256]{1,0:T(8,128)(2,1)S(1)}, bf16[512,256]{1,0:T(8,128)(2,1)S(1)}, u32[]{:S(2)}, u32[]{:S(2)}) %collective-permute-start.25) | collective-permute-done | bytes 262176 | tf_op jit(solution)/shard_map/ppermute | solution.py:425
  118.6 0.1 add_convert_fusion
  118.6 0.9 pad_maximum_fusion
  (37 shorter events, 0.1 us)
Async XLA Ops:
  0.0 12.7 %copy-start.15 = (bf16[256,256]{1,0:T(8,128)(2,1)S(1)}, bf16[256,256]{1,0:T(8,128)(2,1)}, u32[]{:S(2)}) copy-start(bf16[256,256]{1,0:T(8,128)(2,1)} %param.11) | copy-start | bytes 393220
  5.2 15.3 %all-to-all-start = ((bf16[16,48,256]{2,1,0:T(8,128)(2,1)}), bf16[16,48,256]{2,1,0:T(8,128)(2,1)S(1)}, u32[]{:S(2)}, u32[]{:S(2)}) async-start(bf16[16,48,256]{2,1,0:T(8,128)(2,1)} %get-tuple-element.31), calls=%async_computation | async-start | bytes 786432 | tf_op jit(solution)/shard_map/all_to_all | solution.py:331
  12.7 14.7 %collective-permute-start.7 = (bf16[256,256]{1,0:T(8,128)(2,1)S(1)}, bf16[256,256]{1,0:T(8,128)(2,1)S(1)}, u32[]{:S(2)}, u32[]{:S(2)}) collective-permute-start(bf16[256,256]{1,0:T(8,128)(2,1)S(1)} %copy-done.15), channel_id=1, source_target_pairs={{0,0},{1,16},{2,32},{3,48},{4,64},{5,80},{6,96},{7,112},{8,8},{9,2... | collective-permute-start | bytes 393224 | tf_op jit(solution)/shard_map/ppermute | solution.py:330
  20.5 0.7 copy-start.14
  29.0 9.5 %copy-start.2 = (bf16[512,256]{1,0:T(8,128)(2,1)S(1)}, bf16[512,256]{1,0:T(8,128)(2,1)}, u32[]{:S(2)}) copy-start(bf16[512,256]{1,0:T(8,128)(2,1)} %get-tuple-element.32.refs_0_) | copy-start | bytes 786436
  29.0 65.4 %all-to-all-start.1 = ((bf16[16,256,256]{2,1,0:T(8,128)(2,1)}), bf16[16,256,256]{2,1,0:T(8,128)(2,1)S(1)}, u32[]{:S(2)}, u32[]{:S(2)}) async-start(bf16[16,256,256]{2,1,0:T(8,128)(2,1)} %broadcast_in_dim.7), calls=%async_computation.1 | async-start | bytes 4194304 | tf_op jit(solution)/shard_map/all_to_all | solution.py:398
  38.4 12.2 %collective-permute-start.3 = (bf16[512,256]{1,0:T(8,128)(2,1)S(1)}, bf16[512,256]{1,0:T(8,128)(2,1)S(1)}, u32[]{:S(2)}, u32[]{:S(2)}) collective-permute-start(bf16[512,256]{1,0:T(8,128)(2,1)S(1)} %copy-done.2), channel_id=1, source_target_pairs={{0,1},{1,2},{2,3},{3,4},{4,5},{5,6},{6,7},{7,0},{8,9},{9,10},{10,1... | collective-permute-start | bytes 786440 | tf_op jit(solution)/shard_map/ppermute | solution.py:384
  40.6 12.1 %collective-permute-start = (bf16[512,256]{1,0:T(8,128)(2,1)S(1)}, bf16[512,256]{1,0:T(8,128)(2,1)S(1)}, u32[]{:S(2)}, u32[]{:S(2)}) collective-permute-start(bf16[512,256]{1,0:T(8,128)(2,1)S(1)} %copy-done.2), channel_id=1, source_target_pairs={{1,0},{2,1},{3,2},{4,3},{5,4},{6,5},{7,6},{0,7},{9,8},{10,9},{11,1... | collective-permute-start | bytes 786440 | tf_op jit(solution)/shard_map/ppermute | solution.py:384
  43.2 6.8 %copy-start.1 = (bf16[512,256]{1,0:T(8,128)(2,1)S(1)}, bf16[512,256]{1,0:T(8,128)(2,1)}, u32[]{:S(2)}) copy-start(bf16[512,256]{1,0:T(8,128)(2,1)} %get-tuple-element.40.refs_0_) | copy-start | bytes 786436
  46.7 10.6 %collective-permute-start.8 = (bf16[512,256]{1,0:T(8,128)(2,1)}, bf16[512,256]{1,0:T(8,128)(2,1)S(1)}, u32[]{:S(2)}, u32[]{:S(2)}) collective-permute-start(bf16[512,256]{1,0:T(8,128)(2,1)} %gate.3.refs_0_), channel_id=1, source_target_pairs={{0,1},{1,2},{2,3},{3,4},{4,5},{5,6},{6,7},{7,0},{8,9},{9,10},{10,1... | collective-permute-start | bytes 786440 | tf_op jit(solution)/shard_map/ppermute | solution.py:384
  46.7 12.1 %collective-permute-start.11 = (bf16[512,256]{1,0:T(8,128)(2,1)}, bf16[512,256]{1,0:T(8,128)(2,1)S(1)}, u32[]{:S(2)}, u32[]{:S(2)}) collective-permute-start(bf16[512,256]{1,0:T(8,128)(2,1)} %gate.3.refs_0_), channel_id=1, source_target_pairs={{1,0},{2,1},{3,2},{4,3},{5,4},{6,5},{7,6},{0,7},{9,8},{10,9},{11,1... | collective-permute-start | bytes 786440 | tf_op jit(solution)/shard_map/ppermute | solution.py:384
  49.9 12.6 %collective-permute-start.15 = (bf16[512,256]{1,0:T(8,128)(2,1)S(1)}, bf16[512,256]{1,0:T(8,128)(2,1)S(1)}, u32[]{:S(2)}, u32[]{:S(2)}) collective-permute-start(bf16[512,256]{1,0:T(8,128)(2,1)S(1)} %copy-done.1), channel_id=1, source_target_pairs={{1,0},{2,1},{3,2},{4,3},{5,4},{6,5},{7,6},{0,7},{9,8},{10,9},{11,1... | collective-permute-start | bytes 786440 | tf_op jit(solution)/shard_map/ppermute | solution.py:384
  50.7 16.2 %collective-permute-start.4 = (bf16[512,256]{1,0:T(8,128)(2,1)S(1)}, bf16[512,256]{1,0:T(8,128)(2,1)S(1)}, u32[]{:S(2)}, u32[]{:S(2)}) collective-permute-start(bf16[512,256]{1,0:T(8,128)(2,1)S(1)} %collective-permute-done.3.refs_7_), channel_id=1, source_target_pairs={{0,1},{1,2},{2,3},{3,4},{4,5},{5,6},{6,7},{7,0},{8,9},{9,10},{10,1... | collective-permute-start | bytes 786440 | tf_op jit(solution)/shard_map/ppermute | solution.py:384
  52.0 0.7 copy-start.8
  52.7 15.9 %collective-permute-start.19 = (bf16[512,256]{1,0:T(8,128)(2,1)S(1)}, bf16[512,256]{1,0:T(8,128)(2,1)S(1)}, u32[]{:S(2)}, u32[]{:S(2)}) collective-permute-start(bf16[512,256]{1,0:T(8,128)(2,1)S(1)} %copy-done.1), channel_id=1, source_target_pairs={{0,1},{1,2},{2,3},{3,4},{4,5},{5,6},{6,7},{7,0},{8,9},{9,10},{10,1... | collective-permute-start | bytes 786440 | tf_op jit(solution)/shard_map/ppermute | solution.py:384
  57.3 13.6 %collective-permute-start.1 = (bf16[512,256]{1,0:T(8,128)(2,1)S(1)}, bf16[512,256]{1,0:T(8,128)(2,1)}, u32[]{:S(2)}, u32[]{:S(2)}) collective-permute-start(bf16[512,256]{1,0:T(8,128)(2,1)S(1)} %collective-permute-done.refs_1_), channel_id=1, source_target_pairs={{1,0},{2,1},{3,2},{4,3},{5,4},{6,5},{7,6},{0,7},{9,8},{10,9},{11,1... | collective-permute-start | bytes 786440 | tf_op jit(solution)/shard_map/ppermute | solution.py:384
  58.1 0.7 copy-start.10
  58.8 15.5 %collective-permute-start.9 = (bf16[512,256]{1,0:T(8,128)(2,1)S(1)}, bf16[512,256]{1,0:T(8,128)(2,1)}, u32[]{:S(2)}, u32[]{:S(2)}) collective-permute-start(bf16[512,256]{1,0:T(8,128)(2,1)S(1)} %collective-permute-done.8.refs_8_), channel_id=1, source_target_pairs={{0,1},{1,2},{2,3},{3,4},{4,5},{5,6},{6,7},{7,0},{8,9},{9,10},{10,1... | collective-permute-start | bytes 786440 | tf_op jit(solution)/shard_map/ppermute | solution.py:384
  62.5 12.5 %collective-permute-start.16 = (bf16[512,256]{1,0:T(8,128)(2,1)S(1)}, bf16[512,256]{1,0:T(8,128)(2,1)}, u32[]{:S(2)}, u32[]{:S(2)}) collective-permute-start(bf16[512,256]{1,0:T(8,128)(2,1)S(1)} %collective-permute-done.15.refs_1_), channel_id=1, source_target_pairs={{1,0},{2,1},{3,2},{4,3},{5,4},{6,5},{7,6},{0,7},{9,8},{10,9},{11,1... | collective-permute-start | bytes 786440 | tf_op jit(solution)/shard_map/ppermute | solution.py:384
  66.2 0.7 copy-start.4
  66.9 13.0 %collective-permute-start.5 = (bf16[512,256]{1,0:T(8,128)(2,1)S(1)}, bf16[512,256]{1,0:T(8,128)(2,1)}, u32[]{:S(2)}, u32[]{:S(2)}) collective-permute-start(bf16[512,256]{1,0:T(8,128)(2,1)S(1)} %collective-permute-done.4.refs_6_), channel_id=1, source_target_pairs={{0,1},{1,2},{2,3},{3,4},{4,5},{5,6},{6,7},{7,0},{8,9},{9,10},{10,1... | collective-permute-start | bytes 786440 | tf_op jit(solution)/shard_map/ppermute | solution.py:384
  66.9 0.7 copy-start.12
  68.5 11.3 %collective-permute-start.12 = (bf16[512,256]{1,0:T(8,128)(2,1)S(1)}, bf16[512,256]{1,0:T(8,128)(2,1)}, u32[]{:S(2)}, u32[]{:S(2)}) collective-permute-start(bf16[512,256]{1,0:T(8,128)(2,1)S(1)} %collective-permute-done.11.refs_1_), channel_id=1, source_target_pairs={{1,0},{2,1},{3,2},{4,3},{5,4},{6,5},{7,6},{0,7},{9,8},{10,9},{11,1... | collective-permute-start | bytes 786440 | tf_op jit(solution)/shard_map/ppermute | solution.py:384
  70.9 14.6 %collective-permute-start.20 = (bf16[512,256]{1,0:T(8,128)(2,1)S(1)}, bf16[512,256]{1,0:T(8,128)(2,1)}, u32[]{:S(2)}, u32[]{:S(2)}) collective-permute-start(bf16[512,256]{1,0:T(8,128)(2,1)S(1)} %collective-permute-done.19.refs_7_), channel_id=1, source_target_pairs={{0,1},{1,2},{2,3},{3,4},{4,5},{5,6},{6,7},{7,0},{8,9},{9,10},{10,1... | collective-permute-start | bytes 786440 | tf_op jit(solution)/shard_map/ppermute | solution.py:384
  70.9 0.7 copy-start.6
  74.3 12.0 %collective-permute-start.2 = (bf16[512,256]{1,0:T(8,128)(2,1)}, bf16[512,256]{1,0:T(8,128)(2,1)}, u32[]{:S(2)}, u32[]{:S(2)}) collective-permute-start(bf16[512,256]{1,0:T(8,128)(2,1)} %collective-permute-done.1.refs_2_), channel_id=1, source_target_pairs={{1,0},{2,1},{3,2},{4,3},{5,4},{6,5},{7,6},{0,7},{9,8},{10,9},{11,1... | collective-permute-start | bytes 786440 | tf_op jit(solution)/shard_map/ppermute | solution.py:384
  75.0 15.7 %collective-permute-start.17 = (bf16[512,256]{1,0:T(8,128)(2,1)}, bf16[512,256]{1,0:T(8,128)(2,1)}, u32[]{:S(2)}, u32[]{:S(2)}) collective-permute-start(bf16[512,256]{1,0:T(8,128)(2,1)} %collective-permute-done.16.refs_2_), channel_id=1, source_target_pairs={{1,0},{2,1},{3,2},{4,3},{5,4},{6,5},{7,6},{0,7},{9,8},{10,9},{11,1... | collective-permute-start | bytes 786440 | tf_op jit(solution)/shard_map/ppermute | solution.py:384
  79.9 14.5 %collective-permute-start.6 = (bf16[512,256]{1,0:T(8,128)(2,1)}, bf16[512,256]{1,0:T(8,128)(2,1)}, u32[]{:S(2)}, u32[]{:S(2)}) collective-permute-start(bf16[512,256]{1,0:T(8,128)(2,1)} %collective-permute-done.5.refs_5_), channel_id=1, source_target_pairs={{0,1},{1,2},{2,3},{3,4},{4,5},{5,6},{6,7},{7,0},{8,9},{9,10},{10,1... | collective-permute-start | bytes 786440 | tf_op jit(solution)/shard_map/ppermute | solution.py:384
  79.9 21.0 %collective-permute-start.10 = (bf16[512,256]{1,0:T(8,128)(2,1)}, bf16[512,256]{1,0:T(8,128)(2,1)S(1)}, u32[]{:S(2)}, u32[]{:S(2)}) collective-permute-start(bf16[512,256]{1,0:T(8,128)(2,1)} %collective-permute-done.9.refs_7_), channel_id=1, source_target_pairs={{0,1},{1,2},{2,3},{3,4},{4,5},{5,6},{6,7},{7,0},{8,9},{9,10},{10,1... | collective-permute-start | bytes 786440 | tf_op jit(solution)/shard_map/ppermute | solution.py:384
  85.5 15.4 %collective-permute-start.13 = (bf16[512,256]{1,0:T(8,128)(2,1)}, bf16[512,256]{1,0:T(8,128)(2,1)S(1)}, u32[]{:S(2)}, u32[]{:S(2)}) collective-permute-start(bf16[512,256]{1,0:T(8,128)(2,1)} %collective-permute-done.12.refs_2_), channel_id=1, source_target_pairs={{1,0},{2,1},{3,2},{4,3},{5,4},{6,5},{7,6},{0,7},{9,8},{10,9},{11,1... | collective-permute-start | bytes 786440 | tf_op jit(solution)/shard_map/ppermute | solution.py:384
  86.3 17.6 %collective-permute-start.21 = (bf16[512,256]{1,0:T(8,128)(2,1)}, bf16[512,256]{1,0:T(8,128)(2,1)}, u32[]{:S(2)}, u32[]{:S(2)}) collective-permute-start(bf16[512,256]{1,0:T(8,128)(2,1)} %collective-permute-done.20.refs_6_), channel_id=1, source_target_pairs={{0,1},{1,2},{2,3},{3,4},{4,5},{5,6},{6,7},{7,0},{8,9},{9,10},{10,1... | collective-permute-start | bytes 786440 | tf_op jit(solution)/shard_map/ppermute | solution.py:384
  90.7 13.2 %collective-permute-start.18 = (bf16[512,256]{1,0:T(8,128)(2,1)}, bf16[512,256]{1,0:T(8,128)(2,1)}, u32[]{:S(2)}, u32[]{:S(2)}) collective-permute-start(bf16[512,256]{1,0:T(8,128)(2,1)} %collective-permute-done.17.refs_3_), channel_id=1, source_target_pairs={{1,0},{2,1},{3,2},{4,3},{5,4},{6,5},{7,6},{0,7},{9,8},{10,9},{11,1... | collective-permute-start | bytes 786440 | tf_op jit(solution)/shard_map/ppermute | solution.py:384
  94.4 1.0 copy-start.3
  95.3 0.9 copy-start.9
  96.3 0.9 copy-start.11
  97.2 0.9 copy-start.13
  98.2 5.7 %copy-start.5 = (bf16[512,256]{1,0:T(8,128)(2,1)S(1)}, bf16[512,256]{1,0:T(8,128)(2,1)}, u32[]{:S(2)}) copy-start(bf16[512,256]{1,0:T(8,128)(2,1)} %copy-done.4) | copy-start | bytes 786436
  98.2 5.7 %copy-start.7 = (bf16[512,256]{1,0:T(8,128)(2,1)S(1)}, bf16[512,256]{1,0:T(8,128)(2,1)}, u32[]{:S(2)}) copy-start(bf16[512,256]{1,0:T(8,128)(2,1)} %copy-done.6) | copy-start | bytes 786436
  100.9 11.1 %collective-permute-start.14 = (bf16[512,256]{1,0:T(8,128)(2,1)S(1)}, bf16[512,256]{1,0:T(8,128)(2,1)S(1)}, u32[]{:S(2)}, u32[]{:S(2)}) collective-permute-start(bf16[512,256]{1,0:T(8,128)(2,1)S(1)} %get-tuple-element.39), channel_id=1, source_target_pairs={{0,8},{1,9},{2,10},{3,11},{4,12},{5,13},{6,14},{7,15},{8,0},{9,1},... | collective-permute-start | bytes 786440 | tf_op jit(solution)/shard_map/ppermute | solution.py:425
  101.6 6.3 %collective-permute-start.23 = (bf16[256,256]{1,0:T(8,128)(2,1)S(1)}, bf16[256,256]{1,0:T(8,128)(2,1)S(1)}, u32[]{:S(2)}, u32[]{:S(2)}) collective-permute-start(bf16[256,256]{1,0:T(8,128)(2,1)S(1)} %slice.6), channel_id=1, source_target_pairs={{1,0},{2,1},{3,2},{4,3},{5,4},{6,5},{7,6},{0,7},{9,8},{10,9},{11,1... | collective-permute-start | bytes 393224 | tf_op jit(solution)/shard_map/ppermute | solution.py:384
  101.8 6.3 %copy-start = (bf16[512,256]{1,0:T(8,128)(2,1)S(1)}, bf16[512,256]{1,0:T(8,128)(2,1)}, u32[]{:S(2)}) copy-start(bf16[512,256]{1,0:T(8,128)(2,1)} %gate.3.refs_0_) | copy-start | bytes 786436
  101.8 6.3 %collective-permute-start.24 = (bf16[256,256]{1,0:T(8,128)(2,1)S(1)}, bf16[256,256]{1,0:T(8,128)(2,1)S(1)}, u32[]{:S(2)}, u32[]{:S(2)}) collective-permute-start(bf16[256,256]{1,0:T(8,128)(2,1)S(1)} %slice.7), channel_id=1, source_target_pairs={{0,1},{1,2},{2,3},{3,4},{4,5},{5,6},{6,7},{7,0},{8,9},{9,10},{10,1... | collective-permute-start | bytes 393224 | tf_op jit(solution)/shard_map/ppermute | solution.py:384
  106.5 9.2 %collective-permute-start.22 = (bf16[512,256]{1,0:T(8,128)(2,1)S(1)}, bf16[512,256]{1,0:T(8,128)(2,1)S(1)}, u32[]{:S(2)}, u32[]{:S(2)}) collective-permute-start(bf16[512,256]{1,0:T(8,128)(2,1)S(1)} %get-tuple-element.42), channel_id=1, source_target_pairs={{0,8},{1,9},{2,10},{3,11},{4,12},{5,13},{6,14},{7,15},{8,0},{9,1},... | collective-permute-start | bytes 786440 | tf_op jit(solution)/shard_map/ppermute | solution.py:425
  110.5 8.0 %collective-permute-start.25 = (bf16[512,256]{1,0:T(8,128)(2,1)S(1)}, bf16[512,256]{1,0:T(8,128)(2,1)S(1)}, u32[]{:S(2)}, u32[]{:S(2)}) collective-permute-start(bf16[512,256]{1,0:T(8,128)(2,1)S(1)} %get-tuple-element.46), channel_id=1, source_target_pairs={{0,8},{1,9},{2,10},{3,11},{4,12},{5,13},{6,14},{7,15},{8,0},{9,1},... | collective-permute-start | bytes 786440 | tf_op jit(solution)/shard_map/ppermute | solution.py:425
